TPU v7x, 128 devices: a whole 4x4x4 slice. The times are simulated.
128 devices in a mesh: train: 8 (over y, x_hi), replica: 4 (over x_lo, core), ep: 4 (over z).
Axes of the slice: x: 4 (x_hi: 2, x_lo: 2; x = x_hi * 2 + x_lo), y: 4, z: 4, core: 2. Of those that a mesh axis runs over, the one named last changes fastest.
Arguments:
- master: float32 [8, 2048, 7168], P('ep', 'replica', 'train'), may hold values from -6 to 6
- gradient: bfloat16 [8, 2048, 7168], P('ep', 'replica', 'train'), may hold values from -1000 to 1000
- second: float32 [8, 2048, 7168], P('ep', 'replica', 'train'), may hold values from 0.1 to 2
- placement: int32 [4, 8], replicated, may hold values from 0 to 3, as said below
Outputs:
- master_new: float32 [8, 2048, 7168], P('ep', 'replica', 'train')
- second_new: float32 [8, 2048, 7168], P('ep', 'replica', 'train')
- quantized: bfloat16 [4, 4, 2, 2048, 7168], P('replica', 'ep', None, None, 'train')
- scales: float32 [4, 4, 2, 16, 56], P('replica', 'ep', None, None, 'train')
Inputs may be any that keep to these rules, and one draw needn't show every extreme that they name: `placement`: in each row every ep index is named by exactly 2 experts.
All inputs are finite; a program needn't handle non-finite values. Where the computation divides by a largest or mean magnitude, that divisor is 1e-20 or more.
Results may differ from a plain program's by a relative error of at most 0.006.
Values may be sent and summed in bfloat16 or wider, within the bound.
No kernel may reach another device: no remote copies, remote signals or barrier semaphores. Data moves between devices by JAX's collectives and lax.ppermute only.
A program may use at most 192 MiB of HBM per device.

v0:
```python
import jax
import jax.numpy as jnp
from jax import lax
from jax.sharding import PartitionSpec as P

BLOCK = 128


decay_rate = 0.95
step_size = 0.3


def block_quantize(values):
    full_shape = values.shape
    blocks = values.astype(jnp.float32).reshape(
        full_shape[:-2] + (full_shape[-2] // BLOCK, BLOCK, full_shape[-1] // BLOCK, BLOCK)
    )
    largest = jnp.max(jnp.abs(blocks), axis=(-3, -1)) + 1e-06
    scaled = (blocks / largest[..., :, None, :, None]).astype(jnp.bfloat16).reshape(full_shape)
    return (scaled, largest)


def slot_table(placement, holders, per_device):
    matches = (placement[:, None, :] == jnp.arange(holders, dtype=jnp.int32)[None, :, None]).astype(
        jnp.int32
    )
    rank_within = jnp.cumsum(matches, axis=-1) - 1
    expert_ids = jnp.arange(placement.shape[-1], dtype=jnp.int32)
    slot_numbers = jnp.arange(per_device, dtype=jnp.int32)
    selected = matches[..., None, :] * (rank_within[..., None, :] == slot_numbers[:, None]).astype(
        jnp.int32
    )
    return jnp.sum(selected * expert_ids, axis=-1)


def body(master, gradient, second, placement):
    values = gradient.astype(jnp.float32)
    square_sum = lax.psum(jnp.sum(values * values), ("train", "replica", "ep"))
    n_train = lax.axis_size("train")
    n_replica = lax.axis_size("replica")
    n_holders = lax.axis_size("ep")
    root_mean = jnp.sqrt(square_sum / (values.size * n_train * n_replica * n_holders) + 1e-06)
    clipped = values / root_mean
    second_new = decay_rate * second + (1.0 - decay_rate) * clipped * clipped
    master_new = master - step_size * clipped / (jnp.sqrt(second_new) + 1e-08)
    weights = master_new.astype(jnp.bfloat16)
    per_device, row_count, col_count = weights.shape
    slot_experts = slot_table(placement, n_holders, per_device)
    replica_index = lax.axis_index("replica")
    holder_index = lax.axis_index("ep")
    own_slots = slot_experts[replica_index, holder_index]
    initial = jnp.zeros((per_device, n_replica * row_count, col_count), jnp.bfloat16)
    pieces = lax.all_gather(weights[None], ("replica", "ep"), axis=0, tiled=True)

    def place_piece(piece_index, current):
        source_replica = piece_index // n_holders
        source_holder = piece_index % n_holders
        arriving = lax.dynamic_index_in_dim(pieces, piece_index, 0, False)
        for slot_index in range(per_device):
            expert_id = own_slots[slot_index]
            chosen = lax.dynamic_index_in_dim(arriving, expert_id % per_device, 0, False)
            corner = (jnp.int32(slot_index), source_replica * row_count, jnp.int32(0))
            existing = lax.dynamic_slice(current, corner, (1, row_count, col_count))[0]
            updated = jnp.where(expert_id // per_device == source_holder, chosen, existing)
            current = lax.dynamic_update_slice(current, updated[None], corner)
        return current

    gathered = lax.fori_loop(0, pieces.shape[0], place_piece, initial)
    scaled, largest = block_quantize(gathered)
    return (master_new, second_new, scaled[None, None], largest[None, None])


def solution(mesh):
    return jax.shard_map(
        body,
        mesh=mesh,
        in_specs=(
            P("ep", "replica", "train"),
            P("ep", "replica", "train"),
            P("ep", "replica", "train"),
            P(),
        ),
        out_specs=(
            P("ep", "replica", "train"),
            P("ep", "replica", "train"),
            P("replica", "ep", None, None, "train"),
            P("replica", "ep", None, None, "train"),
        ),
        check_vma=False,
    )
```

profile of v0, /device:TPU:1, one launch (start us, length us, event | category | flops | bytes accessed | tf_op | source)
XLA Modules:
  0.0 425.3 jit_solution(2495636496769112037)
XLA Ops:
  7.2 3.0 fusion.4
  10.3 68.7 %psum.7 = f32[]{:T(128)} all-reduce(f32[]{:T(128)} %fusion.4), channel_id=1, replica_groups=mesh['train'=8,'replica'=4,'ep'=4] {'train','replica','ep'}, use_global_device_ids=true, to_apply=%region_1.0 | all-reduce | flops 1 | bytes 8 | tf_op jit(solution)/shard_map/psum | solution.py:38
  79.6 9.5 %fusion.8 = (bf16[2,512,896]{2,1,0:T(8,128)(2,1)}, f32[2,512,896]{2,1,0:T(8,128)}, f32[2,512,896]{2,1,0:T(8,128)}) fusion(f32[2,512,896]{2,1,0:T(8,128)} %param.6, f32[]{:T(128)S(6)} %sqrt.6, bf16[2,512,896]{2,1,0:T(8,128)(2,1)} %param.7, f32[2,512,896]{2,1,0:T(8,128)} %param.8), kind=kLoop, calls=%fused_computation.22 | loop fusion | flops 10092544 | bytes 18350084 | tf_op jit(solution)/shard_map/convert_element_type | solution.py:46
  89.2 0.7 reduce_window_sum.11
  96.0 149.5 %all-gather.3.cloned.1.call-done = bf16[32,512,896]{2,1,0:T(8,128)(2,1)} async-done(((bf16[2,512,896]{2,1,0:T(8,128)(2,1)}), bf16[32,512,896]{2,1,0:T(8,128)(2,1)}) %all-gather.3.cloned.1.call-update) | async-done | bytes 29360144 | tf_op jit(solution)/shard_map/all_gather | solution.py:53
  245.5 3.6 broadcast_in_dim.8
  249.1 83.0 %while.17 = (s32[]{:T(128)}, bf16[2,2048,896]{2,1,0:T(8,128)(2,1)}, s32[]{:T(128)}, bf16[16,2,512,896]{3,2,1,0:T(8,128)(2,1)}, s32[]{:T(128)}, /*index=5*/s32[]{...) while((s32[]{:T(128)}, bf16[2,2048,896]{2,1,0:T(8,128)(2,1)}, ...), condition=%wide.region_5.6_spmd, body=%wide.region_4.5_spmd.sunk | while | flops 917525 | bytes 5506418 | solution.py:68
  249.1 2.6 fusion.13
  251.7 2.6 fusion.14
  254.3 2.6 fusion.13
  256.9 2.6 fusion.14
  259.4 2.6 fusion.13
  262.0 2.6 fusion.14
  264.6 2.6 fusion.13
  267.2 2.6 fusion.14
  269.8 2.6 fusion.13
  272.4 2.6 fusion.14
  275.0 2.6 fusion.13
  277.6 2.6 fusion.14
  280.2 2.6 fusion.13
  282.8 2.6 fusion.14
  285.4 2.6 fusion.13
  288.0 2.6 fusion.14
  290.6 2.6 fusion.13
  293.2 2.6 fusion.14
  295.8 2.6 fusion.13
  298.3 2.6 fusion.14
  300.9 2.6 fusion.13
  303.5 2.6 fusion.14
  306.1 2.6 fusion.13
  308.7 2.6 fusion.14
  311.3 2.6 fusion.13
  313.9 2.6 fusion.14
  316.5 2.6 fusion.13
  319.1 2.6 fusion.14
  321.7 2.6 fusion.13
  324.3 2.6 fusion.14
  326.9 2.6 fusion.13
  329.5 2.6 fusion.14
  332.1 11.3 %copy.15 = bf16[2,2048,896]{1,2,0:T(8,128)(2,1)} copy(bf16[2,2048,896]{2,1,0:T(8,128)(2,1)} %get-tuple-element.463) | data formatting | bytes 14680064 | tf_op jit(solution)/shard_map/while | solution.py:68
  343.3 10.4 %convert_abs_fusion = f32[2,2048,896]{1,2,0:T(8,128)} fusion(bf16[2,2048,896]{1,2,0:T(8,128)(2,1)} %copy.15), kind=kLoop, calls=%fused_computation.5 | loop fusion | flops 7340032 | bytes 22020096 | tf_op jit(solution)/shard_map/abs | solution.py:18
  353.8 14.0 %copy.18 = f32[224,8,16,128]{3,2,1,0:T(8,128)} copy(f32[224,8,16,128]{3,1,2,0:T(8,128)} %bitcast.30) | data formatting | bytes 29360128
  367.7 6.0 %reduce_max.9 = f32[2,16,7]{1,2,0:T(8,128)S(1)} reduce(f32[2,16,128,7,128]{2,1,4,3,0:T(8,128)} %bitcast.29, f32[]{:T(128)} %constant.354.clone.1), dimensions={2,4}, to_apply=%region_6.7 | reduce | flops 3669792 | bytes 14680964 | tf_op jit(solution)/shard_map/reduce_max | solution.py:18
  373.7 0.6 copy.17
  374.3 6.2 %div.63 = f32[2,16,128,7,128]{2,1,4,3,0:T(8,128)} broadcast(f32[2,16,7]{1,2,0:T(8,128)S(1)} %get-tuple-element.494), dimensions={0,1,3} | broadcast | bytes 14680960 | tf_op jit(solution)/shard_map/div | solution.py:19
  380.5 15.9 %div.64 = f32[2,2048,896]{1,2,0:T(8,128)} reshape(f32[2,16,128,7,128]{2,1,4,3,0:T(8,128)} %div.63) | data formatting | bytes 29360128 | tf_op jit(solution)/shard_map/div | solution.py:19
  396.4 10.8 %fusion.3 = bf16[1,1,2,2048,896]{3,4,2,1,0:T(8,128)(2,1)} fusion(f32[2,2048,896]{1,2,0:T(8,128)} %div.64, bf16[2,2048,896]{1,2,0:T(8,128)(2,1)} %copy.15), kind=kLoop, calls=%fused_computation.7 | loop fusion | flops 11010048 | bytes 29360128 | tf_op jit(solution)/shard_map/convert_element_type | solution.py:19
  407.2 11.3 %copy.16 = bf16[1,1,2,2048,896]{4,3,2,1,0:T(8,128)(2,1)} copy(bf16[1,1,2,2048,896]{3,4,2,1,0:T(8,128)(2,1)} %fusion.3) | data formatting | bytes 14680064
  (10 shorter events, 1.0 us)
Async XLA Ops:
  7.2 238.3 %all-gather.3.cloned.1.call-start = ((), (), s32[]{:S(2)}) async-start(), calls=%async_computation | async-start | bytes 31195136 | tf_op jit(solution)/shard_map/all_gather | solution.py:53
  79.6 9.5 %copy-start = (s32[4,8]{1,0:T(4,128)S(1)}, s32[4,8]{1,0:T(4,128)}, u32[]{:S(2)}) copy-start(s32[4,8]{1,0:T(4,128)} %param.9) | copy-start | bytes 388
Sparse Core Ops, SparseCore 0:
  89.2 156.1 all-gather.2
where the time goes:
time: 428 us; the launch traced here: 425 us
  waiting for transfers between devices  150 us (35%)
  other arithmetic  124 us (29%)
  blocking collectives  68.7 us (16%)
  local copies, waits for them, and re-layouts  63.5 us (15%)
  between operations  19.9 us (5%)
    all_gather x1, waiting for transfers between devices, body(): lax.all_gather(weights[None], ('replica', 'ep'), axis=0, tiled=True)  150 us
    dynamic_update_slice x32, other arithmetic, place_piece(): current = lax.dynamic_update_slice(current, updated[None], corner)  83 us
    psum x1, blocking collectives, body(): square_sum = lax.psum(jnp.sum(values * values), ('train', 'replica', 'ep'))  68.7 us
    unnamed x5, local copies, waits for them, and re-layouts  25.9 us
    div x2, local copies, waits for them, and re-layouts, block_quantize(): blocks / largest[..., :, None, :, None]  22.1 us
    while x1, local copies, waits for them, and re-layouts, body(): gathered = lax.fori_loop(0, pieces.shape[0], place_piece, initial)  11.3 us
    convert_element_type x1, other arithmetic, block_quantize(): (blocks / largest[..., :, None, :, None]).astype(jnp.bfloat16)  10.8 us
    abs x1, other arithmetic, block_quantize(): largest = jnp.max(jnp.abs(blocks), axis=(-3, -1)) + 1e-06  10.4 us
  transfers between devices with their start and end apart: 1, of which 1 were waited for; matrix products, arithmetic and copies ran while one was open for 0% of the time, Pallas kernels for 0%

commit v1 on v0

v1 whole, which is shorter than its diff:
```python
import functools

import jax
import jax.numpy as jnp
from jax import lax
from jax.experimental import pallas as pl
from jax.experimental.pallas import tpu as pltpu
from jax.sharding import PartitionSpec as P

BLOCK = 128
decay_rate = 0.95
step_size = 0.3

ANY = pl.BlockSpec(memory_space=pl.ANY)
SMEM = pl.BlockSpec(memory_space=pltpu.SMEM)
VMEM = pl.BlockSpec(memory_space=pltpu.VMEM)
HBM = pl.BlockSpec(memory_space=pltpu.HBM)
LIMIT = pltpu.CompilerParams(vmem_limit_bytes=8 << 20)


def held(value):
    return pltpu.with_memory_space_constraint(value, pltpu.VMEM)


def cost(bytes_accessed, flops=0):
    return pl.CostEstimate(flops=flops, bytes_accessed=bytes_accessed, transcendentals=0)


def squares_kernel(gradient_ref, out_ref):
    experts, rows, cols = gradient_ref.shape
    step = 64
    total = jnp.zeros((8, cols), jnp.float32)
    for expert in range(experts):

        def add(i, total):
            values = gradient_ref[expert, pl.ds(pl.multiple_of(i * step, step), step), :].astype(jnp.float32)
            return total + jnp.sum((values * values).reshape(step // 8, 8, cols), axis=0)

        total = lax.fori_loop(0, rows // step, add, total)
    out_ref[...] = sum(total[:, c : c + 128] for c in range(0, cols, 128))


def local_squares(gradient):
    return pl.pallas_call(
        squares_kernel,
        in_specs=[VMEM],
        out_specs=VMEM,
        out_shape=jax.ShapeDtypeStruct((8, 128), jnp.float32),
        cost_estimate=cost(gradient.size * 2, gradient.size * 2),
        compiler_params=LIMIT,
        name="local_squares",
    )(held(gradient))


def all_sum(part):
    n_train, n_replica, n_ep = (lax.axis_size(a) for a in ("train", "replica", "ep"))

    def over(value, axes, orders):
        return value + sum(lax.ppermute(value, axes, order) for order in orders)

    part = over(part, "ep", [[(i, (i + k) % n_ep) for i in range(n_ep)] for k in range(1, n_ep)])
    part = over(
        part, "train", [[(i, (i + 2 * k) % n_train) for i in range(n_train)] for k in range(1, n_train // 2)]
    )
    pairs = [(t, r) for t in range(n_train) for r in range(n_replica)]
    flips = [(0, 2)] + ([(1, 0), (1, 2)] if n_train > 1 else [])
    part = over(
        part,
        ("train", "replica"),
        [[(t * n_replica + r, (t ^ ft) * n_replica + (r ^ fr)) for t, r in pairs] for ft, fr in flips],
    )
    return over(part, "replica", [[(r, r ^ 1) for r in range(n_replica)]])


def update_kernel(count, chunk, total_ref, master_ref, gradient_ref, second_ref, master_out, second_out, weights_out):
    square_sum = jnp.sum(total_ref[...], axis=(0, 1), keepdims=True)
    scale = 1.0 / jnp.sqrt(square_sum / count + 1e-06)
    step = 32
    for expert in range(master_ref.shape[0]):

        @pl.loop(0, BLOCK // step)
        def _(i):
            here = pl.ds(pl.multiple_of(i * step, step), step)
            rows = pl.ds(pl.multiple_of(chunk * BLOCK + i * step, step), step)
            clipped = gradient_ref[expert, rows, :].astype(jnp.float32) * scale
            second_new = decay_rate * second_ref[expert, rows, :] + (1.0 - decay_rate) * clipped * clipped
            master_new = master_ref[expert, rows, :] - step_size * clipped / (jnp.sqrt(second_new) + 1e-08)
            second_out[expert, here, :] = second_new
            master_out[expert, here, :] = master_new
            weights_out[expert, here, :] = master_new.astype(jnp.bfloat16)


def update_rows(count, total, master, gradient, second, chunk):
    experts, rows, cols = master.shape
    shape = (experts, BLOCK, cols)
    size = experts * BLOCK * cols
    return pl.pallas_call(
        functools.partial(update_kernel, count, chunk),
        in_specs=[VMEM] * 4,
        out_specs=[VMEM] * 3,
        out_shape=[pltpu.VMEM(shape, jnp.float32), pltpu.VMEM(shape, jnp.float32), pltpu.VMEM(shape, jnp.bfloat16)],
        cost_estimate=cost(size * 20, size * 20),
        compiler_params=LIMIT,
        name="update_rows",
    )(total, held(master), held(gradient), held(second))


def store_kernel(chunk, *refs):
    pieces, outs, sems = refs[:2], refs[-3:-1], refs[-1]
    copies = [
        pltpu.make_async_copy(
            piece.at[expert], out.at[expert, pl.ds(chunk * BLOCK, BLOCK), :], sems.at[number, expert]
        )
        for number, (piece, out) in enumerate(zip(pieces, outs))
        for expert in range(piece.shape[0])
    ]
    for copy in copies:
        copy.start()
    for copy in copies:
        copy.wait()


def store_rows(pieces, chunk, shape, earlier):
    return pl.pallas_call(
        functools.partial(store_kernel, chunk),
        in_specs=[VMEM] * 2 + [ANY] * len(earlier),
        out_specs=[HBM] * 2,
        out_shape=[jax.ShapeDtypeStruct(shape, jnp.float32)] * 2,
        input_output_aliases={2: 0, 3: 1} if earlier else {},
        scratch_shapes=[pltpu.SemaphoreType.DMA((2, shape[0]))],
        cost_estimate=cost(2 * pieces[0].size * 4),
        compiler_params=LIMIT,
        name="store_rows",
    )(*(held(p) for p in pieces), *earlier)


def slot_table(placement, holders, per_device):
    matches = (placement[:, None, :] == jnp.arange(holders, dtype=jnp.int32)[None, :, None]).astype(jnp.int32)
    rank_within = jnp.cumsum(matches, axis=-1) - 1
    expert_ids = jnp.arange(placement.shape[-1], dtype=jnp.int32)
    slot_numbers = jnp.arange(per_device, dtype=jnp.int32)
    selected = matches[..., None, :] * (rank_within[..., None, :] == slot_numbers[:, None]).astype(jnp.int32)
    return jnp.sum(selected * expert_ids, axis=-1)


def pick_kernel(copies, n, table_ref, *refs):
    arrays, outs = refs[:n], refs[n:]
    for entry, first, out, place in copies:
        code = table_ref[entry]
        for steps in range(4):

            @pl.when(code // 2 == steps)
            def _():
                outs[out][place] = arrays[first + steps][code % 2]


def pick(table, arrays, copies, out_sizes):
    rows, cols = arrays[0].shape[1:]
    return pl.pallas_call(
        functools.partial(pick_kernel, copies, len(arrays)),
        in_specs=[SMEM] + [VMEM] * len(arrays),
        out_specs=[VMEM] * len(out_sizes),
        out_shape=[pltpu.VMEM((n, rows, cols), jnp.bfloat16) for n in out_sizes],
        cost_estimate=cost(len(copies) * rows * cols * 4),
        compiler_params=LIMIT,
        name="pick_slots",
    )(table, *(held(a) for a in arrays))


def quantize_kernel(chunk, places, replica_ref, *refs):
    n = len({place[0] for place in places})
    parts, earlier, (out_ref, scales_ref, ready, sems) = refs[:n], refs[n:-4], refs[-4:]
    scales_ref[...] = earlier[1][...] if earlier else jnp.zeros_like(scales_ref)
    rows, cols = parts[0].shape[1:]
    blocks = cols // BLOCK
    copies = []
    for number, (part, index, flip, slot) in enumerate(places):
        block_row = jnp.bitwise_xor(replica_ref[0], flip) * 4 + chunk
        tops = []
        for block in range(blocks):
            values = jnp.abs(parts[part][index, :, block * BLOCK : (block + 1) * BLOCK].astype(jnp.float32))
            tops.append(jnp.max(values.reshape(rows // 8, 8, BLOCK), axis=0).max(axis=0, keepdims=True))
        tops = jnp.concatenate(tops + [jnp.zeros((8 - blocks, BLOCK), jnp.float32)], axis=0)
        largest = jnp.max(tops, axis=1, keepdims=True) + 1e-06
        inverse = 1.0 / largest
        for block in range(blocks):
            at = slice(block * BLOCK, (block + 1) * BLOCK)
            values = parts[part][index, :, at].astype(jnp.float32)
            ready[number, :, at] = (values * inverse[block : block + 1, :]).astype(jnp.bfloat16)
        lane = lax.broadcasted_iota(jnp.int32, (1, blocks), 1)
        line = jnp.zeros((1, blocks), jnp.float32)
        for block in range(blocks):
            line = jnp.where(lane == block, largest[block : block + 1, :], line)
        scales_ref[0, 0, slot, pl.ds(block_row, 1), :] = line
        target = out_ref.at[0, 0, slot, pl.ds(pl.multiple_of(block_row * BLOCK, BLOCK), BLOCK), :]
        copies.append(pltpu.make_async_copy(ready.at[number], target, sems.at[number]))
        copies[-1].start()
    for copy in copies:
        copy.wait()


def quantize(replica, parts, chunk, places, shape, earlier):
    rows, cols = parts[0].shape[1:]
    scales_shape = (1, 1, shape[2], shape[3] // BLOCK, cols // BLOCK)
    n = len(parts)
    return pl.pallas_call(
        functools.partial(quantize_kernel, chunk, places),
        in_specs=[SMEM] + [VMEM] * n + ([ANY, VMEM] if earlier else []),
        out_specs=[HBM, VMEM],
        out_shape=[jax.ShapeDtypeStruct(shape, jnp.bfloat16), jax.ShapeDtypeStruct(scales_shape, jnp.float32)],
        input_output_aliases={1 + n: 0} if earlier else {},
        scratch_shapes=[
            pltpu.VMEM((len(places), rows, cols), jnp.bfloat16),
            pltpu.SemaphoreType.DMA((len(places),)),
        ],
        cost_estimate=cost(8 * rows * cols * 4, 8 * rows * cols * 5),
        compiler_params=LIMIT,
        name="quantize_rows",
    )(replica, *(held(p) for p in parts), *earlier)


def body(master, gradient, second, placement):
    n_train, n_replica, n_ep = (lax.axis_size(a) for a in ("train", "replica", "ep"))
    experts, rows, cols = master.shape
    chunks = rows // BLOCK
    count = float(master.size * n_train * n_replica * n_ep)
    replica, holder = lax.axis_index("replica"), lax.axis_index("ep")

    slots = slot_table(placement, n_ep, experts)[:, holder]
    order = jnp.bitwise_xor(replica, jnp.arange(n_replica, dtype=jnp.int32))
    named = slots[order].reshape(-1)
    table = 2 * ((named // 2 - holder) % n_ep) + named % 2
    replica_ref = replica[None]

    total = all_sum(local_squares(gradient))

    def up(value):
        return lax.ppermute(value, "ep", [(i, (i + 1) % n_ep) for i in range(n_ep)])

    def down(value):
        return lax.ppermute(value, "ep", [(i, (i - 1) % n_ep) for i in range(n_ep)])

    def flip(value, by):
        return lax.ppermute(value, "replica", [(i, i ^ by) for i in range(n_replica)])

    updated = [update_rows(count, total, master, gradient, second, chunk) for chunk in range(chunks)]
    weights = [u[2] for u in updated]

    def gather(piece, forward_up):
        before, after = up(piece), down(piece)
        return [piece, after, up(before) if forward_up else down(after), before]

    shape = (1, 1, experts, n_replica * rows, cols)
    crossed = flip(weights[0], 2)
    parts = {}
    for chunk in range(1, chunks):
        arrays = gather(weights[chunk], chunk % 2 == 1)
        copies = [(2 * j + k, 0, j, k) for j in (2, 3, 1, 0) for k in range(2)]
        picked = pick(table, arrays, copies, [2] * 4)
        parts[chunk] = [picked[0]] + [flip(picked[j], j) for j in (1, 2, 3)]
    arrays = gather(weights[0], False) + gather(crossed, True)
    copies = [(2 * j + k, 4 * g, j, 2 * g + k) for j in (1, 0) for g in range(2) for k in range(2)]
    mine, other = pick(table, arrays, copies, [4, 4])
    parts[0] = [mine, flip(other, 1)]

    result = ()
    for chunk in range(1, chunks):
        places = [(j, k, j, k) for j in range(4) for k in range(2)]
        result = quantize(replica_ref, parts[chunk], chunk, places, shape, tuple(result))
    places = [(j, 2 * g + k, j ^ (2 * g), k) for j in range(2) for g in range(2) for k in range(2)]
    result = quantize(replica_ref, parts[0], 0, places, shape, tuple(result))
    new = ()
    for chunk in range(chunks):
        new = store_rows(updated[chunk][:2], chunk, master.shape, tuple(new))
    return (*new, *result)


def solution(mesh):
    return jax.shard_map(
        body,
        mesh=mesh,
        in_specs=(
            P("ep", "replica", "train"),
            P("ep", "replica", "train"),
            P("ep", "replica", "train"),
            P(),
        ),
        out_specs=(
            P("ep", "replica", "train"),
            P("ep", "replica", "train"),
            P("replica", "ep", None, None, "train"),
            P("replica", "ep", None, None, "train"),
        ),
        check_vma=False,
    )
```

time: 428 us -> 176 us (0.41)
  other arithmetic: 124 us -> 1.01 us
  waiting for transfers between devices: 150 us -> 78 us
  blocking collectives: 68.7 us -> 0 us
  starting transfers between devices: 0.04 us -> 51.7 us
  local copies, waits for them, and re-layouts: 63.5 us -> 19.4 us
  Pallas kernels: 0 us -> 24.1 us
  between operations: 19.9 us -> 0.93 us
    all_gather x1 -> x0, waiting for transfers between devices: 150 us -> none  [body(): lax.all_gather(weights[None], ('replica', 'ep'), axis=0, tiled=True)]
    dynamic_update_slice x32 -> x0, other arithmetic: 83 us -> none  [place_piece(): current = lax.dynamic_update_slice(current, updated[None], corner)]
    ppermute x0 -> x36, waiting for transfers between devices: none -> 78 us  [the longest x8 31.5 us: up(): return lax.ppermute(value, 'ep', [(i, (i + 1) % n_ep) for i in range(n_ep)])]
    psum x1 -> x0, blocking collectives: 68.7 us -> none  [body(): square_sum = lax.psum(jnp.sum(values * values), ('train', 'replica', 'ep'))]
    ppermute x0 -> x36, starting transfers between devices: none -> 51.7 us  [the longest x10 20.9 us: over(): return value + sum((lax.ppermute(value, axes, order) for order in orders))]
    pallas_call x0 -> x17, Pallas kernels: none -> 24.1 us  [the longest x4 7.15 us: quantize(): pl.pallas_call(functools.partial(quantize_kernel, chunk, places), in_spec...]
    div x2 -> x0, local copies, waits for them, and re-layouts: 22.1 us -> none  [block_quantize(): blocks / largest[..., :, None, :, None]]
    convert_element_type x2 -> x0, other arithmetic: 20.3 us -> none  [the longest x1 10.8 us: block_quantize(): (blocks / largest[..., :, None, :, None]).astype(jnp.bfloat16)]
  transfers between devices with their start and end apart: 1 -> 36, of which waited for: 1 -> 20; matrix products, arithmetic and copies ran while one was open for 0% -> 1% of each run, Pallas kernels for 0% -> 12%
where the time goes in v1:
time: 176 us; the launch traced here: 175 us
  waiting for transfers between devices  78 us (44%)
  starting transfers between devices  51.7 us (29%)
  Pallas kernels  24.1 us (14%)
  local copies, waits for them, and re-layouts  19.4 us (11%)
    ppermute x8, waiting for transfers between devices, up(): return lax.ppermute(value, 'ep', [(i, (i + 1) % n_ep) for i in range(n_ep)])  31.5 us
    ppermute x11, waiting for transfers between devices, flip(): lax.ppermute(value, 'replica', [(i, i ^ by) for i in range(n_replica)])  29.8 us
    ppermute x10, starting transfers between devices, over(): return value + sum((lax.ppermute(value, axes, order) for order in orders))  20.9 us
    unnamed x43, local copies, waits for them, and re-layouts  18.5 us
    ppermute x7, starting transfers between devices, down(): return lax.ppermute(value, 'ep', [(i, (i - 1) % n_ep) for i in range(n_ep)])  16.2 us
    ppermute x11, starting transfers between devices, flip(): lax.ppermute(value, 'replica', [(i, i ^ by) for i in range(n_replica)])  13.8 us
    ppermute x7, waiting for transfers between devices, down(): return lax.ppermute(value, 'ep', [(i, (i - 1) % n_ep) for i in range(n_ep)])  8.9 us
    ppermute x10, waiting for transfers between devices, over(): return value + sum((lax.ppermute(value, axes, order) for order in orders))  7.71 us
  transfers between devices with their start and end apart: 36, of which 20 were waited for; matrix products, arithmetic and copies ran while one was open for 1% of the time, Pallas kernels for 12%

profile of v1, /device:TPU:1, one launch (start us, length us, event | category | flops | bytes accessed | tf_op | source)
XLA Modules:
  0.0 175.1 jit_solution(9237874965428403258)
XLA Ops:
  0.6 1.5 copy-done.2
  2.4 2.5 %collective-permute-start = (f32[8,128]{1,0:T(8,128)S(1)}, f32[8,128]{1,0:T(8,128)S(1)}, u32[]{:S(2)}, u32[]{:S(2)}) collective-permute-start(f32[8,128]{1,0:T(8,128)S(1)} %local_squares.1), channel_id=1, source_target_pairs={{0,1},{1,2},{2,3},{3,0},{4,5},{5,6},{6,7},{7,4},{8,9},{9,10},{10,1... | collective-permute-start | bytes 12296 | tf_op jit(solution)/shard_map/ppermute | solution.py:59
  4.9 3.3 %collective-permute-start.1 = (f32[8,128]{1,0:T(8,128)S(1)}, f32[8,128]{1,0:T(8,128)S(1)}, u32[]{:S(2)}, u32[]{:S(2)}) collective-permute-start(f32[8,128]{1,0:T(8,128)S(1)} %local_squares.1), channel_id=1, source_target_pairs={{0,2},{1,3},{2,0},{3,1},{4,6},{5,7},{6,4},{7,5},{8,10},{9,11},{10,... | collective-permute-start | bytes 12296 | tf_op jit(solution)/shard_map/ppermute | solution.py:59
  9.3 1.4 collective-permute-done.2
  10.7 1.3 collective-permute-start.3
  12.0 2.6 %collective-permute-start.4 = (f32[8,128]{1,0:T(8,128)S(1)}, f32[8,128]{1,0:T(8,128)S(1)}, u32[]{:S(2)}, u32[]{:S(2)}) collective-permute-start(f32[8,128]{1,0:T(8,128)S(1)} %add_add_fusion.2), channel_id=1, source_target_pairs={{0,64},{16,80},{32,96},{48,112},{64,0},{80,16},{96,32},{112,48},{1... | collective-permute-start | bytes 12296 | tf_op jit(solution)/shard_map/ppermute | solution.py:59
  16.0 1.4 collective-permute-done.5
  18.6 2.5 %collective-permute-start.7 = (f32[8,128]{1,0:T(8,128)S(1)}, f32[8,128]{1,0:T(8,128)S(1)}, u32[]{:S(2)}, u32[]{:S(2)}) collective-permute-start(f32[8,128]{1,0:T(8,128)S(1)} %add_add_fusion.1), channel_id=1, source_target_pairs={{0,16},{4,20},{8,24},{12,28},{16,0},{20,4},{24,8},{28,12},{32,48},... | collective-permute-start | bytes 12296 | tf_op jit(solution)/shard_map/ppermute | solution.py:59
  21.2 1.3 collective-permute-done.7
  22.5 2.2 %collective-permute-done.8 = f32[8,128]{1,0:T(8,128)S(1)} collective-permute-done((f32[8,128]{1,0:T(8,128)S(1)}, f32[8,128]{1,0:T(8,128)S(1)}, u32[]{:S(2)}, u32[]{:S(2)}) %collective-permute-start.8) | collective-permute-done | bytes 4128 | tf_op jit(solution)/shard_map/ppermute | solution.py:59
  24.7 5.5 %collective-permute-start.9 = (f32[8,128]{1,0:T(8,128)S(1)}, f32[8,128]{1,0:T(8,128)S(1)}, u32[]{:S(2)}, u32[]{:S(2)}) collective-permute-start(f32[8,128]{1,0:T(8,128)S(1)} %add_add_fusion), channel_id=1, source_target_pairs={{0,4},{4,0},{8,12},{12,8},{1,5},{5,1},{9,13},{13,9},{2,6},{6,2},{1... | collective-permute-start | bytes 12296 | tf_op jit(solution)/shard_map/ppermute | solution.py:59
  31.0 2.0 %copy-done = f32[2,512,896]{2,1,0:T(8,128)S(1)} copy-done((f32[2,512,896]{2,1,0:T(8,128)S(1)}, f32[2,512,896]{2,1,0:T(8,128)}, u32[]{:S(2)}) %copy-start) | copy-done | bytes 3670040
  33.1 2.0 %copy-done.1 = f32[2,512,896]{2,1,0:T(8,128)S(1)} copy-done((f32[2,512,896]{2,1,0:T(8,128)S(1)}, f32[2,512,896]{2,1,0:T(8,128)}, u32[]{:S(2)}) %copy-start.1) | copy-done | bytes 3670040
  35.1 1.5 copy-done.3
  37.5 2.7 %collective-permute-start.30 = (bf16[2,128,896]{2,1,0:T(8,128)(2,1)S(1)}, bf16[2,128,896]{2,1,0:T(8,128)(2,1)S(1)}, u32[]{:S(2)}, u32[]{:S(2)}) collective-permute-start(bf16[2,128,896]{2,1,0:T(8,128)(2,1)S(1)} %get-tuple-element.75.refs_0_), channel_id=1, source_target_pairs={{0,3},{1,0},{2,1},{3,2},{4,7},{5,4},{6,5},{7,6},{8,11},{9,8},{10,9... | collective-permute-start | bytes 1376264 | tf_op jit(solution)/shard_map/ppermute | solution.py:241
  40.2 1.6 update_rows.5
  46.8 1.6 update_rows.7
  52.1 2.5 %collective-permute-start.18 = (bf16[2,128,896]{2,1,0:T(8,128)(2,1)S(1)}, bf16[2,128,896]{2,1,0:T(8,128)(2,1)}, u32[]{:S(2)}, u32[]{:S(2)}) collective-permute-start(bf16[2,128,896]{2,1,0:T(8,128)(2,1)S(1)} %get-tuple-element.65.refs_0_), channel_id=1, source_target_pairs={{0,3},{1,0},{2,1},{3,2},{4,7},{5,4},{6,5},{7,6},{8,11},{9,8},{10,9... | collective-permute-start | bytes 1376264 | tf_op jit(solution)/shard_map/ppermute | solution.py:241
  55.3 4.1 %collective-permute-done.24.refs_1_ = bf16[2,128,896]{2,1,0:T(8,128)(2,1)} collective-permute-done((bf16[2,128,896]{2,1,0:T(8,128)(2,1)}, bf16[2,128,896]{2,1,0:T(8,128)(2,1)}, u32[]{:S(2)}, u32[]{:S(2)}) %collective-permute-start.24) | collective-permute-done | bytes 458784 | tf_op jit(solution)/shard_map/ppermute | solution.py:241
  59.3 3.4 %collective-permute-start.10 = (bf16[2,128,896]{2,1,0:T(8,128)(2,1)}, bf16[2,128,896]{2,1,0:T(8,128)(2,1)}, u32[]{:S(2)}, u32[]{:S(2)}) collective-permute-start(bf16[2,128,896]{2,1,0:T(8,128)(2,1)} %get-tuple-element.62.refs_0_), channel_id=1, source_target_pairs={{0,3},{1,0},{2,1},{3,2},{4,7},{5,4},{6,5},{7,6},{8,11},{9,8},{10,9... | collective-permute-start | bytes 1376264 | tf_op jit(solution)/shard_map/ppermute | solution.py:241
  62.7 7.5 %collective-permute-done.19.refs_3_ = bf16[2,128,896]{2,1,0:T(8,128)(2,1)} collective-permute-done((bf16[2,128,896]{2,1,0:T(8,128)(2,1)S(1)}, bf16[2,128,896]{2,1,0:T(8,128)(2,1)}, u32[]{:S(2)}, u32[]{:S(2)}) %collective-permute-start.19) | collective-permute-done | bytes 458784 | tf_op jit(solution)/shard_map/ppermute | solution.py:238
  70.5 2.8 %collective-permute-start.25 = (bf16[2,128,896]{2,1,0:T(8,128)(2,1)}, bf16[2,128,896]{2,1,0:T(8,128)(2,1)}, u32[]{:S(2)}, u32[]{:S(2)}) collective-permute-start(bf16[2,128,896]{2,1,0:T(8,128)(2,1)} %collective-permute-done.24.refs_1_), channel_id=1, source_target_pairs={{0,3},{1,0},{2,1},{3,2},{4,7},{5,4},{6,5},{7,6},{8,11},{9,8},{10,9... | collective-permute-start | bytes 1376264 | tf_op jit(solution)/shard_map/ppermute | solution.py:241
  74.2 4.8 %collective-permute-done.10.refs_1_ = bf16[2,128,896]{2,1,0:T(8,128)(2,1)} collective-permute-done((bf16[2,128,896]{2,1,0:T(8,128)(2,1)}, bf16[2,128,896]{2,1,0:T(8,128)(2,1)}, u32[]{:S(2)}, u32[]{:S(2)}) %collective-permute-start.10) | collective-permute-done | bytes 458784 | tf_op jit(solution)/shard_map/ppermute | solution.py:241
  79.0 3.4 %collective-permute-start.14 = (bf16[2,128,896]{2,1,0:T(8,128)(2,1)}, bf16[2,128,896]{2,1,0:T(8,128)(2,1)S(1)}, u32[]{:S(2)}, u32[]{:S(2)}) collective-permute-start(bf16[2,128,896]{2,1,0:T(8,128)(2,1)} %collective-permute-done.13.refs_4_), channel_id=1, source_target_pairs={{0,3},{1,0},{2,1},{3,2},{4,7},{5,4},{6,5},{7,6},{8,11},{9,8},{10,9... | collective-permute-start | bytes 1376264 | tf_op jit(solution)/shard_map/ppermute | solution.py:241
  82.4 7.5 %collective-permute-done.32.refs_2_ = bf16[2,128,896]{2,1,0:T(8,128)(2,1)} collective-permute-done((bf16[2,128,896]{2,1,0:T(8,128)(2,1)}, bf16[2,128,896]{2,1,0:T(8,128)(2,1)}, u32[]{:S(2)}, u32[]{:S(2)}) %collective-permute-start.32) | collective-permute-done | bytes 458784 | tf_op jit(solution)/shard_map/ppermute | solution.py:238
  90.6 9.1 %collective-permute-done.15.refs_7_ = bf16[2,128,896]{2,1,0:T(8,128)(2,1)} collective-permute-done((bf16[2,128,896]{2,1,0:T(8,128)(2,1)}, bf16[2,128,896]{2,1,0:T(8,128)(2,1)}, u32[]{:S(2)}, u32[]{:S(2)}) %collective-permute-start.15) | collective-permute-done | bytes 458784 | tf_op jit(solution)/shard_map/ppermute | solution.py:238
  102.8 1.4 pick_slots.7
  104.2 2.0 %collective-permute-start.33 = (bf16[2,128,896]{2,1,0:T(8,128)(2,1)S(1)}, bf16[2,128,896]{2,1,0:T(8,128)(2,1)S(1)}, u32[]{:S(2)}, u32[]{:S(2)}) collective-permute-start(bf16[2,128,896]{2,1,0:T(8,128)(2,1)S(1)} %get-tuple-element.77), channel_id=1, source_target_pairs={{0,4},{4,0},{8,12},{12,8},{1,5},{5,1},{9,13},{13,9},{2,6},{6,2},{1... | collective-permute-start | bytes 1376264 | tf_op jit(solution)/shard_map/ppermute | solution.py:244
  106.2 3.2 %collective-permute-done.20.refs_2_ = bf16[2,128,896]{2,1,0:T(8,128)(2,1)S(1)} collective-permute-done((bf16[2,128,896]{2,1,0:T(8,128)(2,1)}, bf16[2,128,896]{2,1,0:T(8,128)(2,1)S(1)}, u32[]{:S(2)}, u32[]{:S(2)}) %collective-permute-start.20) | collective-permute-done | bytes 458784 | tf_op jit(solution)/shard_map/ppermute | solution.py:238
  109.4 2.1 %pick_slots.6 = (bf16[2,128,896]{2,1,0:T(8,128)(2,1)S(1)}, bf16[2,128,896]{2,1,0:T(8,128)(2,1)S(1)}, bf16[2,128,896]{2,1,0:T(8,128)(2,1)S(1)}, bf16[2,128,896]{2,1,0:T(8,128)(2,1)S(1)}) custom-call(s32[8]{0:T(128)S(1)} %fusion.1.table_ref, bf16[2,128,896]{2,1,0:T(8,128)(2,1)} %get-tuple-element.70.refs_0_, ...), custom_call_target="tpu_custom_call" | custom-call | bytes 3670016 | tf_op jit(solution)/shard_map/pick_slots/pallas_call | solution.py:159
  111.6 3.6 %collective-permute-start.35 = (bf16[2,128,896]{2,1,0:T(8,128)(2,1)S(1)}, bf16[2,128,896]{2,1,0:T(8,128)(2,1)S(1)}, u32[]{:S(2)}, u32[]{:S(2)}) collective-permute-start(bf16[2,128,896]{2,1,0:T(8,128)(2,1)S(1)} %get-tuple-element.79), channel_id=1, source_target_pairs={{0,12},{4,8},{8,4},{12,0},{1,13},{5,9},{9,5},{13,1},{2,14},{6,10},... | collective-permute-start | bytes 1376264 | tf_op jit(solution)/shard_map/ppermute | solution.py:244
  115.2 4.1 %collective-permute-done.16.refs_6_ = bf16[2,128,896]{2,1,0:T(8,128)(2,1)S(1)} collective-permute-done((bf16[2,128,896]{2,1,0:T(8,128)(2,1)}, bf16[2,128,896]{2,1,0:T(8,128)(2,1)S(1)}, u32[]{:S(2)}, u32[]{:S(2)}) %collective-permute-start.16) | collective-permute-done | bytes 458784 | tf_op jit(solution)/shard_map/ppermute | solution.py:238
  119.3 2.0 %pick_slots.4 = (bf16[4,128,896]{2,1,0:T(8,128)(2,1)S(1)}, bf16[4,128,896]{2,1,0:T(8,128)(2,1)S(1)}) custom-call(s32[8]{0:T(128)S(1)} %fusion.1.table_ref, bf16[2,128,896]{2,1,0:T(8,128)(2,1)} %get-tuple-element.62.refs_0_, bf16[2,128,896]{2,1,0:T(8,128)(2,1)} %collective-permute-done.10.refs_1_, bf16[2,128,896]{2,1,0:T(8,128)(2,1)S(1)} %collective-permute-done.11.refs_2_, ...), custom_call_target="tpu_custom_call" | custom-call | bytes 3670016 | tf_op jit(solution)/shard_map/pick_slots/pallas_call | solution.py:159
  121.2 1.3 collective-permute-start.17
  122.5 2.0 %collective-permute-start.29 = (bf16[2,128,896]{2,1,0:T(8,128)(2,1)S(1)}, bf16[2,128,896]{2,1,0:T(8,128)(2,1)S(1)}, u32[]{:S(2)}, u32[]{:S(2)}) collective-permute-start(bf16[2,128,896]{2,1,0:T(8,128)(2,1)S(1)} %get-tuple-element.74), channel_id=1, source_target_pairs={{0,12},{4,8},{8,4},{12,0},{1,13},{5,9},{9,5},{13,1},{2,14},{6,10},... | collective-permute-start | bytes 1376264 | tf_op jit(solution)/shard_map/ppermute | solution.py:244
  124.4 1.5 pick_slots.5
  126.0 8.0 %collective-permute-done.35.refs_3_ = bf16[2,128,896]{2,1,0:T(8,128)(2,1)S(1)} collective-permute-done((bf16[2,128,896]{2,1,0:T(8,128)(2,1)S(1)}, bf16[2,128,896]{2,1,0:T(8,128)(2,1)S(1)}, u32[]{:S(2)}, u32[]{:S(2)}) %collective-permute-start.35) | collective-permute-done | bytes 458784 | tf_op jit(solution)/shard_map/ppermute | solution.py:244
  134.0 5.2 %collective-permute-done.28.refs_2_ = bf16[2,128,896]{2,1,0:T(8,128)(2,1)S(1)} collective-permute-done((bf16[2,128,896]{2,1,0:T(8,128)(2,1)S(1)}, bf16[2,128,896]{2,1,0:T(8,128)(2,1)S(1)}, u32[]{:S(2)}, u32[]{:S(2)}) %collective-permute-start.28) | collective-permute-done | bytes 458784 | tf_op jit(solution)/shard_map/ppermute | solution.py:244
  139.2 4.9 %collective-permute-start.23 = (bf16[2,128,896]{2,1,0:T(8,128)(2,1)S(1)}, bf16[2,128,896]{2,1,0:T(8,128)(2,1)S(1)}, u32[]{:S(2)}, u32[]{:S(2)}) collective-permute-start(bf16[2,128,896]{2,1,0:T(8,128)(2,1)S(1)} %get-tuple-element.69), channel_id=1, source_target_pairs={{0,12},{4,8},{8,4},{12,0},{1,13},{5,9},{9,5},{13,1},{2,14},{6,10},... | collective-permute-start | bytes 1376264 | tf_op jit(solution)/shard_map/ppermute | solution.py:244
  144.1 1.3 store_rows.4
  145.4 1.3 store_rows.5
  150.6 1.8 %quantize_rows.4 = (bf16[1,1,2,2048,896]{4,3,2,1,0:T(8,128)(2,1)}, f32[1,1,2,16,7]{4,3,2,1,0:T(8,128)S(1)}) custom-call(s32[1]{0:T(128)} %bitcast.replica_ref, bf16[2,128,896]{2,1,0:T(8,128)(2,1)S(1)} %get-tuple-element.76.refs_0_, bf16[2,128,896]{2,1,0:T(8,128)(2,1)S(1)} %collective-permute-done.33.refs_1_, ...), custom_call_target="tpu_custom_call" | custom-call | flops 4587520 | bytes 3670016 | tf_op jit(solution)/shard_map/quantize_rows/pallas_call | solution.py:206
  152.4 1.3 collective-permute-done.29.refs_3_
  153.6 1.8 %quantize_rows.5 = (bf16[1,1,2,2048,896]{4,3,2,1,0:T(8,128)(2,1)}, f32[1,1,2,16,7]{4,3,2,1,0:T(8,128)S(1)}) custom-call(s32[1]{0:T(128)} %bitcast.replica_ref, bf16[2,128,896]{2,1,0:T(8,128)(2,1)S(1)} %get-tuple-element.71.refs_0_, bf16[2,128,896]{2,1,0:T(8,128)(2,1)S(1)} %collective-permute-done.27.refs_1_, ...), custom_call_target="tpu_custom_call", output_to_operand_aliasing={{0}: (5, {})} | custom-call | flops 4587520 | bytes 3670016 | tf_op jit(solution)/shard_map/quantize_rows/pallas_call | solution.py:206
  155.5 3.4 %collective-permute-done.22.refs_2_ = bf16[2,128,896]{2,1,0:T(8,128)(2,1)S(1)} collective-permute-done((bf16[2,128,896]{2,1,0:T(8,128)(2,1)S(1)}, bf16[2,128,896]{2,1,0:T(8,128)(2,1)S(1)}, u32[]{:S(2)}, u32[]{:S(2)}) %collective-permute-start.22) | collective-permute-done | bytes 458784 | tf_op jit(solution)/shard_map/ppermute | solution.py:244
  158.8 12.0 %collective-permute-done.23.refs_3_ = bf16[2,128,896]{2,1,0:T(8,128)(2,1)S(1)} collective-permute-done((bf16[2,128,896]{2,1,0:T(8,128)(2,1)S(1)}, bf16[2,128,896]{2,1,0:T(8,128)(2,1)S(1)}, u32[]{:S(2)}, u32[]{:S(2)}) %collective-permute-start.23) | collective-permute-done | bytes 458784 | tf_op jit(solution)/shard_map/ppermute | solution.py:244
  170.8 1.8 %quantize_rows.6 = (bf16[1,1,2,2048,896]{4,3,2,1,0:T(8,128)(2,1)}, f32[1,1,2,16,7]{4,3,2,1,0:T(8,128)S(1)}) custom-call(s32[1]{0:T(128)} %bitcast.replica_ref, bf16[2,128,896]{2,1,0:T(8,128)(2,1)S(1)} %get-tuple-element.66.refs_0_, bf16[2,128,896]{2,1,0:T(8,128)(2,1)S(1)} %collective-permute-done.21.refs_1_, ...), custom_call_target="tpu_custom_call", output_to_operand_aliasing={{0}: (5, {})} | custom-call | flops 4587520 | bytes 3670016 | tf_op jit(solution)/shard_map/quantize_rows/pallas_call | solution.py:206
  172.6 1.8 %quantize_rows.7 = (bf16[1,1,2,2048,896]{4,3,2,1,0:T(8,128)(2,1)}, f32[1,1,2,16,7]{4,3,2,1,0:T(8,128)S(1)}) custom-call(s32[1]{0:T(128)} %bitcast.replica_ref, bf16[4,128,896]{2,1,0:T(8,128)(2,1)S(1)} %get-tuple-element.63.refs_0_, bf16[4,128,896]{2,1,0:T(8,128)(2,1)S(1)} %collective-permute-done.17.refs_1_, ...), custom_call_target="tpu_custom_call", output_to_operand_aliasing={{0}: (3, {})} | custom-call | flops 4587520 | bytes 3670016 | tf_op jit(solution)/shard_map/quantize_rows/pallas_call | solution.py:206
  (100 shorter events, 24.8 us)
Async XLA Ops:
  0.6 1.5 copy-start.2
  2.4 6.6 %collective-permute-start = (f32[8,128]{1,0:T(8,128)S(1)}, f32[8,128]{1,0:T(8,128)S(1)}, u32[]{:S(2)}, u32[]{:S(2)}) collective-permute-start(f32[8,128]{1,0:T(8,128)S(1)} %local_squares.1), channel_id=1, source_target_pairs={{0,1},{1,2},{2,3},{3,0},{4,5},{5,6},{6,7},{7,4},{8,9},{9,10},{10,1... | collective-permute-start | bytes 12296 | tf_op jit(solution)/shard_map/ppermute | solution.py:59
  4.9 4.3 %collective-permute-start.1 = (f32[8,128]{1,0:T(8,128)S(1)}, f32[8,128]{1,0:T(8,128)S(1)}, u32[]{:S(2)}, u32[]{:S(2)}) collective-permute-start(f32[8,128]{1,0:T(8,128)S(1)} %local_squares.1), channel_id=1, source_target_pairs={{0,2},{1,3},{2,0},{3,1},{4,6},{5,7},{6,4},{7,5},{8,10},{9,11},{10,... | collective-permute-start | bytes 12296 | tf_op jit(solution)/shard_map/ppermute | solution.py:59
  8.2 2.5 %collective-permute-start.2 = (f32[8,128]{1,0:T(8,128)S(1)}, f32[8,128]{1,0:T(8,128)S(1)}, u32[]{:S(2)}, u32[]{:S(2)}) collective-permute-start(f32[8,128]{1,0:T(8,128)S(1)} %local_squares.1), channel_id=1, source_target_pairs={{0,3},{1,0},{2,1},{3,2},{4,7},{5,4},{6,5},{7,6},{8,11},{9,8},{10,9... | collective-permute-start | bytes 12296 | tf_op jit(solution)/shard_map/ppermute | solution.py:59
  10.7 5.0 %collective-permute-start.3 = (f32[8,128]{1,0:T(8,128)S(1)}, f32[8,128]{1,0:T(8,128)S(1)}, u32[]{:S(2)}, u32[]{:S(2)}) collective-permute-start(f32[8,128]{1,0:T(8,128)S(1)} %add_add_fusion.2), channel_id=1, source_target_pairs={{0,32},{16,48},{32,64},{48,80},{64,96},{80,112},{96,0},{112,16},{1... | collective-permute-start | bytes 12296 | tf_op jit(solution)/shard_map/ppermute | solution.py:59
  12.0 4.0 %collective-permute-start.4 = (f32[8,128]{1,0:T(8,128)S(1)}, f32[8,128]{1,0:T(8,128)S(1)}, u32[]{:S(2)}, u32[]{:S(2)}) collective-permute-start(f32[8,128]{1,0:T(8,128)S(1)} %add_add_fusion.2), channel_id=1, source_target_pairs={{0,64},{16,80},{32,96},{48,112},{64,0},{80,16},{96,32},{112,48},{1... | collective-permute-start | bytes 12296 | tf_op jit(solution)/shard_map/ppermute | solution.py:59
  14.6 2.8 %collective-permute-start.5 = (f32[8,128]{1,0:T(8,128)S(1)}, f32[8,128]{1,0:T(8,128)S(1)}, u32[]{:S(2)}, u32[]{:S(2)}) collective-permute-start(f32[8,128]{1,0:T(8,128)S(1)} %add_add_fusion.2), channel_id=1, source_target_pairs={{0,96},{16,112},{32,0},{48,16},{64,32},{80,48},{96,64},{112,80},{1... | collective-permute-start | bytes 12296 | tf_op jit(solution)/shard_map/ppermute | solution.py:59
  17.4 3.9 %collective-permute-start.6 = (f32[8,128]{1,0:T(8,128)S(1)}, f32[8,128]{1,0:T(8,128)S(1)}, u32[]{:S(2)}, u32[]{:S(2)}) collective-permute-start(f32[8,128]{1,0:T(8,128)S(1)} %add_add_fusion.1), channel_id=1, source_target_pairs={{0,8},{4,12},{8,0},{12,4},{16,24},{20,28},{24,16},{28,20},{32,40},... | collective-permute-start | bytes 12296 | tf_op jit(solution)/shard_map/ppermute | solution.py:59
  18.6 4.0 %collective-permute-start.7 = (f32[8,128]{1,0:T(8,128)S(1)}, f32[8,128]{1,0:T(8,128)S(1)}, u32[]{:S(2)}, u32[]{:S(2)}) collective-permute-start(f32[8,128]{1,0:T(8,128)S(1)} %add_add_fusion.1), channel_id=1, source_target_pairs={{0,16},{4,20},{8,24},{12,28},{16,0},{20,4},{24,8},{28,12},{32,48},... | collective-permute-start | bytes 12296 | tf_op jit(solution)/shard_map/ppermute | solution.py:59
  21.0 3.7 %collective-permute-start.8 = (f32[8,128]{1,0:T(8,128)S(1)}, f32[8,128]{1,0:T(8,128)S(1)}, u32[]{:S(2)}, u32[]{:S(2)}) collective-permute-start(f32[8,128]{1,0:T(8,128)S(1)} %add_add_fusion.1), channel_id=1, source_target_pairs={{0,24},{4,28},{8,16},{12,20},{16,8},{20,12},{24,0},{28,4},{32,56},... | collective-permute-start | bytes 12296 | tf_op jit(solution)/shard_map/ppermute | solution.py:59
  24.7 6.3 %collective-permute-start.9 = (f32[8,128]{1,0:T(8,128)S(1)}, f32[8,128]{1,0:T(8,128)S(1)}, u32[]{:S(2)}, u32[]{:S(2)}) collective-permute-start(f32[8,128]{1,0:T(8,128)S(1)} %add_add_fusion), channel_id=1, source_target_pairs={{0,4},{4,0},{8,12},{12,8},{1,5},{5,1},{9,13},{13,9},{2,6},{6,2},{1... | collective-permute-start | bytes 12296 | tf_op jit(solution)/shard_map/ppermute | solution.py:59
  31.0 2.0 %copy-start = (f32[2,512,896]{2,1,0:T(8,128)S(1)}, f32[2,512,896]{2,1,0:T(8,128)}, u32[]{:S(2)}) copy-start(f32[2,512,896]{2,1,0:T(8,128)} %master_ref.7) | copy-start | bytes 11010052
  33.1 2.0 %copy-start.1 = (f32[2,512,896]{2,1,0:T(8,128)S(1)}, f32[2,512,896]{2,1,0:T(8,128)}, u32[]{:S(2)}) copy-start(f32[2,512,896]{2,1,0:T(8,128)} %second_ref.7) | copy-start | bytes 11010052
  35.1 1.5 copy-start.3
  37.4 4.3 %copy-start.14 = (bf16[2,128,896]{2,1,0:T(8,128)(2,1)}, bf16[2,128,896]{2,1,0:T(8,128)(2,1)S(1)}, u32[]{:S(2)}) copy-start(bf16[2,128,896]{2,1,0:T(8,128)(2,1)S(1)} %get-tuple-element.75.refs_0_) | copy-start | bytes 1376260
  37.4 13.0 %collective-permute-start.31 = (bf16[2,128,896]{2,1,0:T(8,128)(2,1)S(1)}, bf16[2,128,896]{2,1,0:T(8,128)(2,1)S(1)}, u32[]{:S(2)}, u32[]{:S(2)}) collective-permute-start(bf16[2,128,896]{2,1,0:T(8,128)(2,1)S(1)} %get-tuple-element.75.refs_0_), channel_id=1, source_target_pairs={{0,1},{1,2},{2,3},{3,0},{4,5},{5,6},{6,7},{7,4},{8,9},{9,10},{10,1... | collective-permute-start | bytes 1376264 | tf_op jit(solution)/shard_map/ppermute | solution.py:238
  37.5 13.0 %collective-permute-start.30 = (bf16[2,128,896]{2,1,0:T(8,128)(2,1)S(1)}, bf16[2,128,896]{2,1,0:T(8,128)(2,1)S(1)}, u32[]{:S(2)}, u32[]{:S(2)}) collective-permute-start(bf16[2,128,896]{2,1,0:T(8,128)(2,1)S(1)} %get-tuple-element.75.refs_0_), channel_id=1, source_target_pairs={{0,3},{1,0},{2,1},{3,2},{4,7},{5,4},{6,5},{7,6},{8,11},{9,8},{10,9... | collective-permute-start | bytes 1376264 | tf_op jit(solution)/shard_map/ppermute | solution.py:241
  42.7 16.6 %collective-permute-start.24 = (bf16[2,128,896]{2,1,0:T(8,128)(2,1)}, bf16[2,128,896]{2,1,0:T(8,128)(2,1)}, u32[]{:S(2)}, u32[]{:S(2)}) collective-permute-start(bf16[2,128,896]{2,1,0:T(8,128)(2,1)} %get-tuple-element.70.refs_0_), channel_id=1, source_target_pairs={{0,3},{1,0},{2,1},{3,2},{4,7},{5,4},{6,5},{7,6},{8,11},{9,8},{10,9... | collective-permute-start | bytes 1376264 | tf_op jit(solution)/shard_map/ppermute | solution.py:241
  43.4 19.3 %collective-permute-start.26 = (bf16[2,128,896]{2,1,0:T(8,128)(2,1)}, bf16[2,128,896]{2,1,0:T(8,128)(2,1)}, u32[]{:S(2)}, u32[]{:S(2)}) collective-permute-start(bf16[2,128,896]{2,1,0:T(8,128)(2,1)} %get-tuple-element.70.refs_0_), channel_id=1, source_target_pairs={{0,1},{1,2},{2,3},{3,0},{4,5},{5,6},{6,7},{7,4},{8,9},{9,10},{10,1... | collective-permute-start | bytes 1376264 | tf_op jit(solution)/shard_map/ppermute | solution.py:238
  46.8 7.7 %copy-start.20 = (s32[4,8]{1,0:T(4,128)S(1)}, s32[4,8]{1,0:T(4,128)}, u32[]{:S(2)}) copy-start(s32[4,8]{1,0:T(4,128)} %param.7) | copy-start | bytes 388
  50.2 20.0 %collective-permute-start.19 = (bf16[2,128,896]{2,1,0:T(8,128)(2,1)S(1)}, bf16[2,128,896]{2,1,0:T(8,128)(2,1)}, u32[]{:S(2)}, u32[]{:S(2)}) collective-permute-start(bf16[2,128,896]{2,1,0:T(8,128)(2,1)S(1)} %get-tuple-element.65.refs_0_), channel_id=1, source_target_pairs={{0,1},{1,2},{2,3},{3,0},{4,5},{5,6},{6,7},{7,4},{8,9},{9,10},{10,1... | collective-permute-start | bytes 1376264 | tf_op jit(solution)/shard_map/ppermute | solution.py:238
  50.4 19.8 %collective-permute-start.13 = (bf16[2,128,896]{2,1,0:T(8,128)(2,1)}, bf16[2,128,896]{2,1,0:T(8,128)(2,1)}, u32[]{:S(2)}, u32[]{:S(2)}) collective-permute-start(bf16[2,128,896]{2,1,0:T(8,128)(2,1)} %get-tuple-element.62.refs_0_), channel_id=1, source_target_pairs={{0,8},{4,12},{8,0},{12,4},{1,9},{5,13},{9,1},{13,5},{2,10},{6,14},... | collective-permute-start | bytes 1376264 | tf_op jit(solution)/shard_map/ppermute | solution.py:244
  52.1 18.4 %collective-permute-start.18 = (bf16[2,128,896]{2,1,0:T(8,128)(2,1)S(1)}, bf16[2,128,896]{2,1,0:T(8,128)(2,1)}, u32[]{:S(2)}, u32[]{:S(2)}) collective-permute-start(bf16[2,128,896]{2,1,0:T(8,128)(2,1)S(1)} %get-tuple-element.65.refs_0_), channel_id=1, source_target_pairs={{0,3},{1,0},{2,1},{3,2},{4,7},{5,4},{6,5},{7,6},{8,11},{9,8},{10,9... | collective-permute-start | bytes 1376264 | tf_op jit(solution)/shard_map/ppermute | solution.py:241
  59.3 19.7 %collective-permute-start.10 = (bf16[2,128,896]{2,1,0:T(8,128)(2,1)}, bf16[2,128,896]{2,1,0:T(8,128)(2,1)}, u32[]{:S(2)}, u32[]{:S(2)}) collective-permute-start(bf16[2,128,896]{2,1,0:T(8,128)(2,1)} %get-tuple-element.62.refs_0_), channel_id=1, source_target_pairs={{0,3},{1,0},{2,1},{3,2},{4,7},{5,4},{6,5},{7,6},{8,11},{9,8},{10,9... | collective-permute-start | bytes 1376264 | tf_op jit(solution)/shard_map/ppermute | solution.py:241
  62.7 19.7 %collective-permute-start.12 = (bf16[2,128,896]{2,1,0:T(8,128)(2,1)}, bf16[2,128,896]{2,1,0:T(8,128)(2,1)}, u32[]{:S(2)}, u32[]{:S(2)}) collective-permute-start(bf16[2,128,896]{2,1,0:T(8,128)(2,1)} %get-tuple-element.62.refs_0_), channel_id=1, source_target_pairs={{0,1},{1,2},{2,3},{3,0},{4,5},{5,6},{6,7},{7,4},{8,9},{9,10},{10,1... | collective-permute-start | bytes 1376264 | tf_op jit(solution)/shard_map/ppermute | solution.py:238
  70.2 19.7 %collective-permute-start.32 = (bf16[2,128,896]{2,1,0:T(8,128)(2,1)}, bf16[2,128,896]{2,1,0:T(8,128)(2,1)}, u32[]{:S(2)}, u32[]{:S(2)}) collective-permute-start(bf16[2,128,896]{2,1,0:T(8,128)(2,1)} %copy-done.16), channel_id=1, source_target_pairs={{0,1},{1,2},{2,3},{3,0},{4,5},{5,6},{6,7},{7,4},{8,9},{9,10},{10,1... | collective-permute-start | bytes 1376264 | tf_op jit(solution)/shard_map/ppermute | solution.py:238
  70.2 29.5 %collective-permute-start.15 = (bf16[2,128,896]{2,1,0:T(8,128)(2,1)}, bf16[2,128,896]{2,1,0:T(8,128)(2,1)}, u32[]{:S(2)}, u32[]{:S(2)}) collective-permute-start(bf16[2,128,896]{2,1,0:T(8,128)(2,1)} %collective-permute-done.13.refs_4_), channel_id=1, source_target_pairs={{0,1},{1,2},{2,3},{3,0},{4,5},{5,6},{6,7},{7,4},{8,9},{9,10},{10,1... | collective-permute-start | bytes 1376264 | tf_op jit(solution)/shard_map/ppermute | solution.py:238
  70.5 33.7 %collective-permute-start.25 = (bf16[2,128,896]{2,1,0:T(8,128)(2,1)}, bf16[2,128,896]{2,1,0:T(8,128)(2,1)}, u32[]{:S(2)}, u32[]{:S(2)}) collective-permute-start(bf16[2,128,896]{2,1,0:T(8,128)(2,1)} %collective-permute-done.24.refs_1_), channel_id=1, source_target_pairs={{0,3},{1,0},{2,1},{3,2},{4,7},{5,4},{6,5},{7,6},{8,11},{9,8},{10,9... | collective-permute-start | bytes 1376264 | tf_op jit(solution)/shard_map/ppermute | solution.py:241
  79.0 36.2 %collective-permute-start.14 = (bf16[2,128,896]{2,1,0:T(8,128)(2,1)}, bf16[2,128,896]{2,1,0:T(8,128)(2,1)S(1)}, u32[]{:S(2)}, u32[]{:S(2)}) collective-permute-start(bf16[2,128,896]{2,1,0:T(8,128)(2,1)} %collective-permute-done.13.refs_4_), channel_id=1, source_target_pairs={{0,3},{1,0},{2,1},{3,2},{4,7},{5,4},{6,5},{7,6},{8,11},{9,8},{10,9... | collective-permute-start | bytes 1376264 | tf_op jit(solution)/shard_map/ppermute | solution.py:241
  82.4 27.0 %collective-permute-start.20 = (bf16[2,128,896]{2,1,0:T(8,128)(2,1)}, bf16[2,128,896]{2,1,0:T(8,128)(2,1)S(1)}, u32[]{:S(2)}, u32[]{:S(2)}) collective-permute-start(bf16[2,128,896]{2,1,0:T(8,128)(2,1)} %collective-permute-done.19.refs_3_), channel_id=1, source_target_pairs={{0,1},{1,2},{2,3},{3,0},{4,5},{5,6},{6,7},{7,4},{8,9},{9,10},{10,1... | collective-permute-start | bytes 1376264 | tf_op jit(solution)/shard_map/ppermute | solution.py:238
  89.9 21.7 %collective-permute-start.11 = (bf16[2,128,896]{2,1,0:T(8,128)(2,1)}, bf16[2,128,896]{2,1,0:T(8,128)(2,1)S(1)}, u32[]{:S(2)}, u32[]{:S(2)}) collective-permute-start(bf16[2,128,896]{2,1,0:T(8,128)(2,1)} %collective-permute-done.10.refs_1_), channel_id=1, source_target_pairs={{0,3},{1,0},{2,1},{3,2},{4,7},{5,4},{6,5},{7,6},{8,11},{9,8},{10,9... | collective-permute-start | bytes 1376264 | tf_op jit(solution)/shard_map/ppermute | solution.py:241
  99.7 19.6 %collective-permute-start.16 = (bf16[2,128,896]{2,1,0:T(8,128)(2,1)}, bf16[2,128,896]{2,1,0:T(8,128)(2,1)S(1)}, u32[]{:S(2)}, u32[]{:S(2)}) collective-permute-start(bf16[2,128,896]{2,1,0:T(8,128)(2,1)} %collective-permute-done.15.refs_7_), channel_id=1, source_target_pairs={{0,1},{1,2},{2,3},{3,0},{4,5},{5,6},{6,7},{7,4},{8,9},{9,10},{10,1... | collective-permute-start | bytes 1376264 | tf_op jit(solution)/shard_map/ppermute | solution.py:238
  99.7 1.0 copy-start.15
  104.2 17.0 %collective-permute-start.33 = (bf16[2,128,896]{2,1,0:T(8,128)(2,1)S(1)}, bf16[2,128,896]{2,1,0:T(8,128)(2,1)S(1)}, u32[]{:S(2)}, u32[]{:S(2)}) collective-permute-start(bf16[2,128,896]{2,1,0:T(8,128)(2,1)S(1)} %get-tuple-element.77), channel_id=1, source_target_pairs={{0,4},{4,0},{8,12},{12,8},{1,5},{5,1},{9,13},{13,9},{2,6},{6,2},{1... | collective-permute-start | bytes 1376264 | tf_op jit(solution)/shard_map/ppermute | solution.py:244
  109.4 34.7 %copy-start.11 = (f32[2,128,896]{2,1,0:T(8,128)S(1)}, f32[2,128,896]{2,1,0:T(8,128)}, u32[]{:S(2)}) copy-start(f32[2,128,896]{2,1,0:T(8,128)} %copy-done.10) | copy-start | bytes 2752516
  109.4 34.7 %copy-start.13 = (f32[2,128,896]{2,1,0:T(8,128)S(1)}, f32[2,128,896]{2,1,0:T(8,128)}, u32[]{:S(2)}) copy-start(f32[2,128,896]{2,1,0:T(8,128)} %copy-done.12) | copy-start | bytes 2752516
  109.4 13.1 %collective-permute-start.34 = (bf16[2,128,896]{2,1,0:T(8,128)(2,1)S(1)}, bf16[2,128,896]{2,1,0:T(8,128)(2,1)S(1)}, u32[]{:S(2)}, u32[]{:S(2)}) collective-permute-start(bf16[2,128,896]{2,1,0:T(8,128)(2,1)S(1)} %get-tuple-element.78), channel_id=1, source_target_pairs={{0,8},{4,12},{8,0},{12,4},{1,9},{5,13},{9,1},{13,5},{2,10},{6,14},... | collective-permute-start | bytes 1376264 | tf_op jit(solution)/shard_map/ppermute | solution.py:244
  111.6 22.4 %collective-permute-start.35 = (bf16[2,128,896]{2,1,0:T(8,128)(2,1)S(1)}, bf16[2,128,896]{2,1,0:T(8,128)(2,1)S(1)}, u32[]{:S(2)}, u32[]{:S(2)}) collective-permute-start(bf16[2,128,896]{2,1,0:T(8,128)(2,1)S(1)} %get-tuple-element.79), channel_id=1, source_target_pairs={{0,12},{4,8},{8,4},{12,0},{1,13},{5,9},{9,5},{13,1},{2,14},{6,10},... | collective-permute-start | bytes 1376264 | tf_op jit(solution)/shard_map/ppermute | solution.py:244
  115.2 18.8 %collective-permute-start.27 = (bf16[2,128,896]{2,1,0:T(8,128)(2,1)S(1)}, bf16[2,128,896]{2,1,0:T(8,128)(2,1)S(1)}, u32[]{:S(2)}, u32[]{:S(2)}) collective-permute-start(bf16[2,128,896]{2,1,0:T(8,128)(2,1)S(1)} %get-tuple-element.72), channel_id=1, source_target_pairs={{0,4},{4,0},{8,12},{12,8},{1,5},{5,1},{9,13},{13,9},{2,6},{6,2},{1... | collective-permute-start | bytes 1376264 | tf_op jit(solution)/shard_map/ppermute | solution.py:244
  119.3 19.9 %collective-permute-start.28 = (bf16[2,128,896]{2,1,0:T(8,128)(2,1)S(1)}, bf16[2,128,896]{2,1,0:T(8,128)(2,1)S(1)}, u32[]{:S(2)}, u32[]{:S(2)}) collective-permute-start(bf16[2,128,896]{2,1,0:T(8,128)(2,1)S(1)} %get-tuple-element.73), channel_id=1, source_target_pairs={{0,8},{4,12},{8,0},{12,4},{1,9},{5,13},{9,1},{13,5},{2,10},{6,14},... | collective-permute-start | bytes 1376264 | tf_op jit(solution)/shard_map/ppermute | solution.py:244
  121.2 51.4 %collective-permute-start.17 = (bf16[4,128,896]{2,1,0:T(8,128)(2,1)S(1)}, bf16[4,128,896]{2,1,0:T(8,128)(2,1)S(1)}, u32[]{:S(2)}, u32[]{:S(2)}) collective-permute-start(bf16[4,128,896]{2,1,0:T(8,128)(2,1)S(1)} %get-tuple-element.64), channel_id=1, source_target_pairs={{0,4},{4,0},{8,12},{12,8},{1,5},{5,1},{9,13},{13,9},{2,6},{6,2},{1... | collective-permute-start | bytes 2752520 | tf_op jit(solution)/shard_map/ppermute | solution.py:244
  122.5 31.1 %collective-permute-start.29 = (bf16[2,128,896]{2,1,0:T(8,128)(2,1)S(1)}, bf16[2,128,896]{2,1,0:T(8,128)(2,1)S(1)}, u32[]{:S(2)}, u32[]{:S(2)}) collective-permute-start(bf16[2,128,896]{2,1,0:T(8,128)(2,1)S(1)} %get-tuple-element.74), channel_id=1, source_target_pairs={{0,12},{4,8},{8,4},{12,0},{1,13},{5,9},{9,5},{13,1},{2,14},{6,10},... | collective-permute-start | bytes 1376264 | tf_op jit(solution)/shard_map/ppermute | solution.py:244
  134.0 21.5 %collective-permute-start.21 = (bf16[2,128,896]{2,1,0:T(8,128)(2,1)S(1)}, bf16[2,128,896]{2,1,0:T(8,128)(2,1)S(1)}, u32[]{:S(2)}, u32[]{:S(2)}) collective-permute-start(bf16[2,128,896]{2,1,0:T(8,128)(2,1)S(1)} %get-tuple-element.67), channel_id=1, source_target_pairs={{0,4},{4,0},{8,12},{12,8},{1,5},{5,1},{9,13},{13,9},{2,6},{6,2},{1... | collective-permute-start | bytes 1376264 | tf_op jit(solution)/shard_map/ppermute | solution.py:244
  134.0 24.8 %collective-permute-start.22 = (bf16[2,128,896]{2,1,0:T(8,128)(2,1)S(1)}, bf16[2,128,896]{2,1,0:T(8,128)(2,1)S(1)}, u32[]{:S(2)}, u32[]{:S(2)}) collective-permute-start(bf16[2,128,896]{2,1,0:T(8,128)(2,1)S(1)} %get-tuple-element.68), channel_id=1, source_target_pairs={{0,8},{4,12},{8,0},{12,4},{1,9},{5,13},{9,1},{13,5},{2,10},{6,14},... | collective-permute-start | bytes 1376264 | tf_op jit(solution)/shard_map/ppermute | solution.py:244
  139.2 31.7 %collective-permute-start.23 = (bf16[2,128,896]{2,1,0:T(8,128)(2,1)S(1)}, bf16[2,128,896]{2,1,0:T(8,128)(2,1)S(1)}, u32[]{:S(2)}, u32[]{:S(2)}) collective-permute-start(bf16[2,128,896]{2,1,0:T(8,128)(2,1)S(1)} %get-tuple-element.69), channel_id=1, source_target_pairs={{0,12},{4,8},{8,4},{12,0},{1,13},{5,9},{9,5},{13,1},{2,14},{6,10},... | collective-permute-start | bytes 1376264 | tf_op jit(solution)/shard_map/ppermute | solution.py:244
  145.4 1.8 %copy-start.5 = (f32[2,128,896]{2,1,0:T(8,128)S(1)}, f32[2,128,896]{2,1,0:T(8,128)}, u32[]{:S(2)}) copy-start(f32[2,128,896]{2,1,0:T(8,128)} %copy-done.4) | copy-start | bytes 2752516
  147.2 1.8 %copy-start.7 = (f32[2,128,896]{2,1,0:T(8,128)S(1)}, f32[2,128,896]{2,1,0:T(8,128)}, u32[]{:S(2)}) copy-start(f32[2,128,896]{2,1,0:T(8,128)} %copy-done.6) | copy-start | bytes 2752516
  147.2 2.1 %copy-start.9 = (f32[2,128,896]{2,1,0:T(8,128)S(1)}, f32[2,128,896]{2,1,0:T(8,128)}, u32[]{:S(2)}) copy-start(f32[2,128,896]{2,1,0:T(8,128)} %copy-done.8) | copy-start | bytes 2752516
  (9 other events, 8.4 us)

commit v2 on v1

v2 whole, which is shorter than its diff:
```python
import functools

import jax
import jax.numpy as jnp
from jax import lax
from jax.experimental import pallas as pl
from jax.experimental.pallas import tpu as pltpu
from jax.sharding import PartitionSpec as P

BLOCK = 128
decay_rate = 0.95
step_size = 0.3

ANY = pl.BlockSpec(memory_space=pl.ANY)
SMEM = pl.BlockSpec(memory_space=pltpu.SMEM)
VMEM = pl.BlockSpec(memory_space=pltpu.VMEM)
HBM = pl.BlockSpec(memory_space=pltpu.HBM)
LIMIT = pltpu.CompilerParams(vmem_limit_bytes=8 << 20)


def held(value):
    return pltpu.with_memory_space_constraint(value, pltpu.VMEM)


def outside(value):
    return pltpu.with_memory_space_constraint(value, pltpu.HBM)


def kept(shape, dtype):
    return pltpu.VMEM(shape, dtype)


def cost(bytes_accessed, flops=0):
    return pl.CostEstimate(flops=flops, bytes_accessed=bytes_accessed, transcendentals=0)


def squares_kernel(gradient_ref, out_ref):
    experts, rows, cols = gradient_ref.shape
    step = 32
    total = jnp.zeros((8, cols), jnp.float32)
    for expert in range(experts):

        def add(i, total):
            values = gradient_ref[expert, pl.ds(pl.multiple_of(i * step, step), step), :].astype(jnp.float32)
            return total + jnp.sum((values * values).reshape(step // 8, 8, cols), axis=0)

        total = lax.fori_loop(0, rows // step, add, total)
    tile = sum(total[:, c : c + 128] for c in range(0, cols, 128))
    out_ref[...] = jnp.broadcast_to(jnp.sum(tile, axis=0, keepdims=True), out_ref.shape)


def local_squares(gradient, devices):
    return pl.pallas_call(
        squares_kernel,
        in_specs=[VMEM],
        out_specs=VMEM,
        out_shape=jax.ShapeDtypeStruct((devices, 128), jnp.float32),
        cost_estimate=cost(gradient.size * 2, gradient.size * 2),
        compiler_params=LIMIT,
        name="local_squares",
    )(held(gradient))


def load_kernel(chunk, n, *refs):
    sources, outs, sems = refs[:n], refs[-n - 1 : -1], refs[-1]
    copies = [
        pltpu.make_async_copy(
            source.at[expert, pl.ds(chunk * BLOCK, BLOCK), :], out.at[expert], sems.at[number, expert]
        )
        for number, (source, out) in enumerate(zip(sources, outs))
        for expert in range(out.shape[0])
    ]
    for copy in copies:
        copy.start()
    for copy in copies:
        copy.wait()


def load_rows(values, chunk, after):
    n = len(values)
    shapes = [(value.shape[0], BLOCK, value.shape[2]) for value in values]
    return pl.pallas_call(
        functools.partial(load_kernel, chunk, n),
        in_specs=[HBM] * n + [ANY] * len(after),
        out_specs=[VMEM] * n,
        out_shape=[kept(shape, value.dtype) for shape, value in zip(shapes, values)],
        scratch_shapes=[pltpu.SemaphoreType.DMA((n, shapes[0][0]))],
        cost_estimate=cost(sum(2 * a * b * c * 4 for a, b, c in shapes)),
        compiler_params=LIMIT,
        name="load_rows",
    )(*(outside(value) for value in values), *after)


def new_rows(scale, master, gradient, second):
    clipped = gradient.astype(jnp.float32) * scale
    second_new = decay_rate * second + (1.0 - decay_rate) * clipped * clipped
    return master - step_size * clipped / (jnp.sqrt(second_new) + 1e-08), second_new


def scale_of(count, total_ref):
    square_sum = jnp.sum(jnp.sum(total_ref[...], axis=0, keepdims=True), axis=1, keepdims=True)
    return 1.0 / jnp.sqrt(square_sum / count + 1e-06)


def weights_kernel(count, total_ref, master_ref, gradient_ref, second_ref, weights_out):
    scale = scale_of(count, total_ref)
    step = 32
    for expert in range(master_ref.shape[0]):

        @pl.loop(0, BLOCK // step)
        def _(i):
            here = pl.ds(pl.multiple_of(i * step, step), step)
            master_new, _ = new_rows(
                scale, master_ref[expert, here, :], gradient_ref[expert, here, :], second_ref[expert, here, :]
            )
            weights_out[expert, here, :] = master_new.astype(jnp.bfloat16)


def first_weights(count, total, master, gradient, second):
    return pl.pallas_call(
        functools.partial(weights_kernel, count),
        in_specs=[VMEM] * 4,
        out_specs=VMEM,
        out_shape=kept(master.shape, jnp.bfloat16),
        cost_estimate=cost(master.size * 12, master.size * 20),
        compiler_params=LIMIT,
        name="first_weights",
    )(held(total), held(master), held(gradient), held(second))


def update_kernel(count, chunk, total_ref, *refs):
    sources, (master_out, second_out, weights_out, *scratch) = refs[:3], refs[-10:]
    master_in, gradient_in, second_in, master_new, second_new, in_sems, out_sems = scratch
    scale = scale_of(count, total_ref)
    experts = weights_out.shape[0]
    step, half = 32, BLOCK // 2
    pieces = [(expert, part) for expert in range(experts) for part in range(2)]

    def rows_of(part):
        return pl.ds(part * half, half), pl.ds(chunk * BLOCK + part * half, half)

    arriving, leaving = {}, []
    for expert, part in pieces:
        here, there = rows_of(part)
        arriving[expert, part] = [
            pltpu.make_async_copy(source.at[expert, there, :], place.at[expert, here, :], in_sems.at[n, expert, part])
            for n, (source, place) in enumerate(zip(sources, (master_in, gradient_in, second_in)))
        ]
        for copy in arriving[expert, part]:
            copy.start()
    for expert, part in pieces:
        for copy in arriving[expert, part]:
            copy.wait()

        @pl.loop(0, half // step)
        def _(i):
            here = pl.ds(pl.multiple_of(part * half + i * step, step), step)
            master, second = new_rows(
                scale, master_in[expert, here, :], gradient_in[expert, here, :], second_in[expert, here, :]
            )
            master_new[expert, here, :] = master
            second_new[expert, here, :] = second
            weights_out[expert, here, :] = master.astype(jnp.bfloat16)

        here, there = rows_of(part)
        for n, (place, out) in enumerate(((master_new, master_out), (second_new, second_out))):
            copy = pltpu.make_async_copy(
                place.at[expert, here, :], out.at[expert, there, :], out_sems.at[n, expert, part]
            )
            copy.start()
            leaving.append(copy)
    for copy in leaving:
        copy.wait()


def update_rows(count, total, master, gradient, second, chunk, earlier, after):
    experts, rows, cols = master.shape
    shape = (experts, BLOCK, cols)
    size = experts * BLOCK * cols
    return pl.pallas_call(
        functools.partial(update_kernel, count, chunk),
        in_specs=[VMEM] + [HBM] * 3 + [ANY] * (len(earlier) + len(after)),
        out_specs=[HBM, HBM, VMEM],
        out_shape=[
            jax.ShapeDtypeStruct(master.shape, jnp.float32),
            jax.ShapeDtypeStruct(master.shape, jnp.float32),
            kept(shape, jnp.bfloat16),
        ],
        input_output_aliases={4: 0, 5: 1} if earlier else {},
        scratch_shapes=[
            pltpu.VMEM(shape, jnp.float32),
            pltpu.VMEM(shape, jnp.bfloat16),
            pltpu.VMEM(shape, jnp.float32),
            pltpu.VMEM(shape, jnp.float32),
            pltpu.VMEM(shape, jnp.float32),
            pltpu.SemaphoreType.DMA((3, experts, 2)),
            pltpu.SemaphoreType.DMA((2, experts, 2)),
        ],
        cost_estimate=cost(size * 20, size * 20),
        compiler_params=LIMIT,
        name="update_rows",
    )(held(total), outside(master), outside(gradient), outside(second), *earlier, *after)


def slot_table(placement, holders, per_device):
    matches = (placement[:, None, :] == jnp.arange(holders, dtype=jnp.int32)[None, :, None]).astype(jnp.int32)
    rank_within = jnp.cumsum(matches, axis=-1) - 1
    expert_ids = jnp.arange(placement.shape[-1], dtype=jnp.int32)
    slot_numbers = jnp.arange(per_device, dtype=jnp.int32)
    selected = matches[..., None, :] * (rank_within[..., None, :] == slot_numbers[:, None]).astype(jnp.int32)
    return jnp.sum(selected * expert_ids, axis=-1)


def step_kernel(moves, n, table_ref, *refs):
    arrays, outs = refs[:n], refs[len(refs) - 1 - max(m[0] for m in moves) :]
    for out, place, entry, sources in moves:
        if entry is None:
            array, index = sources
            outs[out][place] = arrays[array][index]
            continue
        code = table_ref[entry]
        for steps, (low, high) in enumerate(sources):
            if low[0] == high[0]:

                @pl.when(code // 2 == steps)
                def _():
                    outs[out][place] = arrays[low[0]][low[1] + code % 2]

            else:
                for number, (array, index) in enumerate((low, high)):

                    @pl.when(code == 2 * steps + number)
                    def _():
                        outs[out][place] = arrays[array][index]


def make_step(table, outs, after=(), work=0):
    arrays, moves = [], []

    def number_of(array):
        for number, known in enumerate(arrays):
            if known is array:
                return number
        arrays.append(array)
        return len(arrays) - 1

    for out, pieces in enumerate(outs):
        for place, (first, second) in enumerate(pieces):
            if isinstance(first, int):
                sources = [tuple((number_of(a), i) for a, i in pair) for pair in second]
                moves.append((out, place, first, sources))
            else:
                moves.append((out, place, None, (number_of(first), second)))
    rows, cols = arrays[0].shape[1:]
    return pl.pallas_call(
        functools.partial(step_kernel, moves, len(arrays)),
        in_specs=[SMEM] + [VMEM] * len(arrays) + [ANY] * len(after),
        out_specs=[VMEM] * len(outs),
        out_shape=[kept((len(pieces), rows, cols), jnp.bfloat16) for pieces in outs],
        cost_estimate=cost(max(int(work * 3.3e6), len(moves) * rows * cols * 4)),
        compiler_params=LIMIT,
        name="make_step",
    )(table, *(held(a) for a in arrays), *after)


def quantize_kernel(places, replica_ref, *refs):
    n = len({place[0] for place in places})
    parts, earlier, (out_ref, scales_ref, ready, sems) = refs[:n], refs[n:-4], refs[-4:]
    scales_ref[...] = earlier[1][...] if earlier else jnp.zeros_like(scales_ref)
    rows, cols = parts[0].shape[1:]
    blocks = cols // BLOCK
    copies = []
    for number, (part, index, flip, slot, chunk) in enumerate(places):
        block_row = jnp.bitwise_xor(replica_ref[0], flip) * 4 + chunk
        tops = []
        for block in range(blocks):
            values = jnp.abs(parts[part][index, :, block * BLOCK : (block + 1) * BLOCK].astype(jnp.float32))
            tops.append(jnp.max(values.reshape(rows // 8, 8, BLOCK), axis=0).max(axis=0, keepdims=True))
        tops = jnp.concatenate(tops + [jnp.zeros((8 - blocks, BLOCK), jnp.float32)], axis=0)
        largest = jnp.max(tops, axis=1, keepdims=True) + 1e-06
        inverse = 1.0 / largest
        for block in range(blocks):
            at = slice(block * BLOCK, (block + 1) * BLOCK)
            values = parts[part][index, :, at].astype(jnp.float32)
            ready[number, :, at] = (values * inverse[block : block + 1, :]).astype(jnp.bfloat16)
        lane = lax.broadcasted_iota(jnp.int32, (1, blocks), 1)
        line = jnp.zeros((1, blocks), jnp.float32)
        for block in range(blocks):
            line = jnp.where(lane == block, largest[block : block + 1, :], line)
        scales_ref[0, 0, slot, pl.ds(block_row, 1), :] = line
        target = out_ref.at[0, 0, slot, pl.ds(pl.multiple_of(block_row * BLOCK, BLOCK), BLOCK), :]
        copies.append(pltpu.make_async_copy(ready.at[number], target, sems.at[number]))
        copies[-1].start()
    for copy in copies:
        copy.wait()


def quantize(replica, parts, places, shape, earlier):
    rows, cols = parts[0].shape[1:]
    scales_shape = (1, 1, shape[2], shape[3] // BLOCK, cols // BLOCK)
    n = len(parts)
    return pl.pallas_call(
        functools.partial(quantize_kernel, tuple(places)),
        in_specs=[SMEM] + [VMEM] * n + ([ANY, VMEM] if earlier else []),
        out_specs=[HBM, VMEM],
        out_shape=[jax.ShapeDtypeStruct(shape, jnp.bfloat16), jax.ShapeDtypeStruct(scales_shape, jnp.float32)],
        input_output_aliases={1 + n: 0} if earlier else {},
        scratch_shapes=[
            pltpu.VMEM((len(places), rows, cols), jnp.bfloat16),
            pltpu.SemaphoreType.DMA((len(places),)),
        ],
        cost_estimate=cost(len(places) * rows * cols * 4, len(places) * rows * cols * 5),
        compiler_params=pltpu.CompilerParams(vmem_limit_bytes=12 << 20),
        name="quantize_rows",
    )(replica, *(held(p) for p in parts), *earlier)


def body(master, gradient, second, placement):
    n_train, n_replica, n_ep = (lax.axis_size(a) for a in ("train", "replica", "ep"))
    experts, rows, cols = master.shape
    count = float(master.size * n_train * n_replica * n_ep)
    replica, holder = lax.axis_index("replica"), lax.axis_index("ep")

    slots = slot_table(placement, n_ep, experts)[:, holder]
    order = jnp.bitwise_xor(replica, jnp.arange(n_replica, dtype=jnp.int32))
    named = slots[order].reshape(-1)
    table = 2 * ((named // 2 - holder) % n_ep) + named % 2
    replica_ref = replica[None]

    devices = ("train", "replica", "ep")
    part = local_squares(gradient, n_train * n_replica * n_ep)
    master1, gradient1, second1 = load_rows((master, gradient, second), 1, (part,))
    total = lax.all_to_all(part, devices, 0, 0, tiled=True)

    def send(value, axis, order, name):
        with jax.named_scope(name):
            return lax.ppermute(value, axis, order)

    def up(value, name):
        return send(value, "ep", [(i, (i + 1) % n_ep) for i in range(n_ep)], name + "_up")

    def down(value, name):
        return send(value, "ep", [(i, (i - 1) % n_ep) for i in range(n_ep)], name + "_down")

    def flip(value, by, name):
        return send(value, "replica", [(i, i ^ by) for i in range(n_replica)], name)

    def step(name, outs, after=()):
        with jax.named_scope(name):
            return make_step(table, outs, tuple(after))

    def both(array, first=0):
        return [(array, first), (array, first + 1)]

    def slots_of(flips, here, above, far, below):
        return [(2 * j + k, [here, above, far, below]) for j in flips for k in range(2)]

    def update(chunk, earlier, after=()):
        *new, weights = update_rows(count, total, master, gradient, second, chunk, tuple(earlier), after)
        return new, weights

    def place(chunk, *entries):
        return [(part, index + k, j, k, chunk) for part, index, j in entries for k in range(2)]

    shape = (1, 1, experts, n_replica * rows, cols)

    w1 = first_weights(count, total, master1, gradient1, second1)
    below1, above1 = up(w1, "one"), down(w1, "one")
    new, e = update(0, (), (w1,))
    new, w2 = update(2, new)

    a, b = step("turn_one", [[(below1, 0)] + both(w2), [(above1, 1)] + both(w2)], (e,))
    below2, above2 = up(a, "two"), down(b, "two")
    f = flip(e, 2, "cross")
    new, w3 = update(3, new, (a,))

    def pick(name, ring, flips, after):
        outs = [sum((slots_of((j,), *ring) for j in group), []) for group in flips]
        return step("pick_" + name, outs + [slots_of((0,), *ring)], after)

    a, b = step("turn_two", [[(below2, 1)] + both(w3), [(above2, 2)] + both(w3)], (f,))
    below3, above3 = up(a, "three"), down(b, "three")
    ring1 = (both(w1), both(above1), [(below2, 0), (above2, 0)], both(below1))
    x, o1, s1 = pick("one", ring1, ((2, 3), (1,)), (a,))
    y1 = flip(x, 2, "chip_one")
    new, again = update(1, new, (s1,))

    a, b = step("turn_three", [[(below3, 1)] + both(e), [(above3, 2)] + both(e)], (s1, again))
    below4, above4 = up(a, "four"), down(b, "four")
    z1 = flip(o1, 1, "core_one")
    ring2 = (both(w2), both(above2, 1), [(below3, 0), (above3, 0)], both(below2, 1))
    x, o2, s2 = pick("two", ring2, ((2, 3), (1,)), (a,))
    y2 = flip(x, 2, "chip_two")

    a, b = step("turn_four", [[(below4, 1)] + both(f), [(above4, 2)] + both(f)], (s2, y1, z1))
    below5, above5 = up(a, "five"), down(b, "five")
    ring3 = (both(w3), both(above3, 1), [(below4, 0), (above4, 0)], both(below3, 1))
    x3, v3, o3, s3 = pick("three", ring3, ((2,), (3,), (1,)), (a,))
    x3 = flip(x3, 2, "chip_three")
    z2 = flip(o2, 1, "core_two")
    (c,) = step("pass_one", [both(y1, 2)], (s3,))
    t1 = flip(c, 1, "core_pass")

    a, b = step("turn_five", [[(below5, 1)], [(above5, 2)]], (c, y2, x3, z2, t1))
    far_low_f, far_high_f = up(a, "last"), down(b, "last")
    v3 = flip(v3, 3, "both_three")
    places = place(1, (0, 0, 0), (1, 0, 1), (2, 0, 2), (3, 0, 3))
    result = quantize(replica_ref, [s1, z1, y1, t1], places, shape, ())

    ring_e = (both(e), both(above4, 1), [(below5, 0), (above5, 0)], both(below4, 1))
    ring_f = (both(f), both(above5, 1), [(far_low_f, 0), (far_high_f, 0)], both(below5, 1))
    c, sf, se = step(
        "join_last",
        [
            both(y2, 2) + both(o3) + slots_of((1,), *ring_e) + slots_of((1,), *ring_f),
            slots_of((0,), *ring_f),
            slots_of((0,), *ring_e),
        ],
        (result[1], v3),
    )
    z = flip(c, 1, "core_last")
    places = place(2, (0, 0, 0), (1, 0, 1), (2, 0, 2)) + place(3, (3, 0, 0), (4, 0, 2), (5, 0, 3))
    places += place(0, (6, 0, 0), (7, 0, 2))
    result = quantize(replica_ref, [s2, z2, y2, s3, x3, v3, se, sf], places, shape, tuple(result))
    places = place(2, (0, 0, 3)) + place(3, (0, 2, 1)) + place(0, (0, 4, 1), (0, 6, 3))
    result = quantize(replica_ref, [z], places, shape, tuple(result))
    return (*new, *result)


def solution(mesh):
    return jax.shard_map(
        body,
        mesh=mesh,
        in_specs=(
            P("ep", "replica", "train"),
            P("ep", "replica", "train"),
            P("ep", "replica", "train"),
            P(),
        ),
        out_specs=(
            P("ep", "replica", "train"),
            P("ep", "replica", "train"),
            P("replica", "ep", None, None, "train"),
            P("replica", "ep", None, None, "train"),
        ),
        check_vma=False,
    )
```

time: 176 us -> 130 us (0.74)
  waiting for transfers between devices: 78 us -> 55.8 us
  local copies, waits for them, and re-layouts: 19.4 us -> 3.08 us
  starting transfers between devices: 51.7 us -> 39 us
  Pallas kernels: 24.1 us -> 28.7 us
    ppermute x36 -> x21, waiting for transfers between devices: 78 us -> 49.5 us  [send(): return lax.ppermute(value, axis, order)]
    ppermute x36 -> x21, starting transfers between devices: 51.7 us -> 27.5 us  [send(): return lax.ppermute(value, axis, order)]
    unnamed x43 -> x3, local copies, waits for them, and re-layouts: 18.5 us -> 2.17 us
    all_to_all x0 -> x1, starting transfers between devices: none -> 11.5 us  [body(): total = lax.all_to_all(part, devices, 0, 0, tiled=True)]
    pallas_call x4, Pallas kernels: 4.67 us -> 11.1 us  [update_rows(): pl.pallas_call(functools.partial(update_kernel, count, chunk), in_specs=[...]
    all_to_all x0 -> x1, waiting for transfers between devices: none -> 6.3 us  [body(): total = lax.all_to_all(part, devices, 0, 0, tiled=True)]
    pallas_call x12 -> x15, Pallas kernels: 19.2 us -> 16.5 us  [the longest x10 7.56 us: make_step(): pl.pallas_call(functools.partial(step_kernel, moves, len(arrays)), in_spe...]
  transfers between devices with their start and end apart: 36 -> 22, of which waited for: 20 -> 11; matrix products, arithmetic and copies ran while one was open for 1% -> 2% of each run, Pallas kernels for 12% -> 18%
where the time goes in v2:
time: 130 us; the launch traced here: 129 us
  waiting for transfers between devices  55.8 us (43%)
  starting transfers between devices  39 us (30%)
  Pallas kernels  28.7 us (22%)
  local copies, waits for them, and re-layouts  3.08 us (2%)
  other arithmetic  1.67 us (1%)
    ppermute x21, waiting for transfers between devices, send(): return lax.ppermute(value, axis, order)  49.5 us
    ppermute x21, starting transfers between devices, send(): return lax.ppermute(value, axis, order)  27.5 us
    all_to_all x1, starting transfers between devices, body(): total = lax.all_to_all(part, devices, 0, 0, tiled=True)  11.5 us
    pallas_call x4, Pallas kernels, update_rows(): pl.pallas_call(functools.partial(update_kernel, count, chunk), in_specs=[...  11.1 us
    pallas_call x10, Pallas kernels, make_step(): pl.pallas_call(functools.partial(step_kernel, moves, len(arrays)), in_spe...  7.56 us
    pallas_call x3, Pallas kernels, quantize(): pl.pallas_call(functools.partial(quantize_kernel, tuple(places)), in_spec...  6.57 us
    all_to_all x1, waiting for transfers between devices, body(): total = lax.all_to_all(part, devices, 0, 0, tiled=True)  6.3 us
  transfers between devices with their start and end apart: 22, of which 11 were waited for; matrix products, arithmetic and copies ran while one was open for 2% of the time, Pallas kernels for 18%

profile of v2, /device:TPU:1, one launch (start us, length us, event | category | flops | bytes accessed | tf_op | source)
XLA Modules:
  0.0 129.2 jit_solution(17509271196321185162)
XLA Ops:
  0.6 1.5 %copy-done = bf16[2,512,896]{2,1,0:T(8,128)(2,1)S(1)} copy-done((bf16[2,512,896]{2,1,0:T(8,128)(2,1)S(1)}, bf16[2,512,896]{2,1,0:T(8,128)(2,1)}, u32[]{:S(2)}) %copy-start) | copy-done | bytes 1835032
  2.1 1.1 local_squares.1.refs_3_
  3.2 11.5 %all-to-all-start = ((f32[128,1,128]{2,1,0:T(1,128)}), f32[128,1,128]{2,1,0:T(1,128)S(1)}, u32[]{:S(2)}, u32[]{:S(2)}) async-start(f32[128,1,128]{2,1,0:T(1,128)} %bitcast.1), calls=%async_computation | async-start | bytes 131072 | tf_op jit(solution)/shard_map/all_to_all | solution.py:333
  14.7 0.7 fusion
  15.4 0.7 reduce_window_sum.11
  16.1 1.6 %load_rows.1 = (f32[2,128,896]{2,1,0:T(8,128)S(1)}, bf16[2,128,896]{2,1,0:T(8,128)(2,1)S(1)}, f32[2,128,896]{2,1,0:T(8,128)S(1)}) custom-call(f32[2,512,896]{2,1,0:T(8,128)} %refs_0_.9, bf16[2,512,896]{2,1,0:T(8,128)(2,1)} %refs_1_.9, f32[2,512,896]{2,1,0:T(8,128)} %refs_2_.9, f32[128,128]{1,0:T(8,128)} %local_squares.1.refs_3_), custom_call_target="tpu_custom_call" | custom-call | bytes 5505024 | tf_op jit(solution)/shard_map/load_rows/pallas_call | solution.py:82
  18.0 6.3 %all-to-all-done = f32[128,1,128]{2,1,0:T(1,128)S(1)} async-done(((f32[128,1,128]{2,1,0:T(1,128)}), f32[128,1,128]{2,1,0:T(1,128)S(1)}, u32[]{:S(2)}, u32[]{:S(2)}) %all-to-all-start) | async-done | bytes 65568 | tf_op jit(solution)/shard_map/all_to_all | solution.py:333
  24.3 0.8 first_weights.1.refs_3_.refs_0_
  25.1 0.6 collective-permute-start
  25.7 2.1 %collective-permute-start.1 = (bf16[2,128,896]{2,1,0:T(8,128)(2,1)S(1)}, bf16[2,128,896]{2,1,0:T(8,128)(2,1)S(1)}, u32[]{:S(2)}, u32[]{:S(2)}) collective-permute-start(bf16[2,128,896]{2,1,0:T(8,128)(2,1)S(1)} %first_weights.1.refs_3_.refs_0_), channel_id=1, source_target_pairs={{0,3},{1,0},{2,1},{3,2},{4,7},{5,4},{6,5},{7,6},{8,11},{9,8},{10,9... | collective-permute-start | bytes 1376264 | tf_op jit(solution)/shard_map/one_down/ppermute | solution.py:337
  28.1 0.6 gather_fusion
  28.8 2.8 %update_rows.4 = (f32[2,512,896]{2,1,0:T(8,128)}, f32[2,512,896]{2,1,0:T(8,128)}, bf16[2,128,896]{2,1,0:T(8,128)(2,1)S(1)}) custom-call(f32[128,128]{1,0:T(8,128)S(1)} %bitcast.9, f32[2,512,896]{2,1,0:T(8,128)} %refs_0_.9, bf16[2,512,896]{2,1,0:T(8,128)(2,1)} %refs_1_.9, f32[2,512,896]{2,1,0:T(8,128)} %refs_2_.9, ...), custom_call_target="tpu_custom_call" | custom-call | flops 4587520 | bytes 4587520 | tf_op jit(solution)/shard_map/update_rows/pallas_call | solution.py:180
  31.6 2.8 %update_rows.5 = (f32[2,512,896]{2,1,0:T(8,128)}, f32[2,512,896]{2,1,0:T(8,128)}, bf16[2,128,896]{2,1,0:T(8,128)(2,1)S(1)}) custom-call(f32[128,128]{1,0:T(8,128)S(1)} %bitcast.10, f32[2,512,896]{2,1,0:T(8,128)} %refs_0_.9, bf16[2,512,896]{2,1,0:T(8,128)(2,1)} %refs_1_.9, f32[2,512,896]{2,1,0:T(8,128)} %refs_2_.9, ...), custom_call_target="tpu_custom_call", output_to_operand_aliasing={{0}: (4, {}), {1}: (5, {})} | custom-call | flops 4587520 | bytes 4587520 | tf_op jit(solution)/shard_map/update_rows/pallas_call | solution.py:180
  34.3 3.5 %collective-permute-done.refs_0_.refs_4_ = bf16[2,128,896]{2,1,0:T(8,128)(2,1)S(1)} collective-permute-done((bf16[2,128,896]{2,1,0:T(8,128)(2,1)S(1)}, bf16[2,128,896]{2,1,0:T(8,128)(2,1)S(1)}, u32[]{:S(2)}, u32[]{:S(2)}) %collective-permute-start) | collective-permute-done | bytes 458784 | tf_op jit(solution)/shard_map/one_up/ppermute | solution.py:337
  37.9 0.6 make_step.10
  38.6 2.7 %collective-permute-start.3 = (bf16[3,128,896]{2,1,0:T(8,128)(2,1)S(1)}, bf16[3,128,896]{2,1,0:T(8,128)(2,1)S(1)}, u32[]{:S(2)}, u32[]{:S(2)}) collective-permute-start(bf16[3,128,896]{2,1,0:T(8,128)(2,1)S(1)} %get-tuple-element.60), channel_id=1, source_target_pairs={{0,3},{1,0},{2,1},{3,2},{4,7},{5,4},{6,5},{7,6},{8,11},{9,8},{10,9... | collective-permute-start | bytes 2064392 | tf_op jit(solution)/shard_map/two_down/ppermute | solution.py:337
  41.4 2.8 %update_rows.6 = (f32[2,512,896]{2,1,0:T(8,128)}, f32[2,512,896]{2,1,0:T(8,128)}, bf16[2,128,896]{2,1,0:T(8,128)(2,1)S(1)}) custom-call(f32[128,128]{1,0:T(8,128)S(1)} %bitcast.11, f32[2,512,896]{2,1,0:T(8,128)} %refs_0_.9, bf16[2,512,896]{2,1,0:T(8,128)(2,1)} %refs_1_.9, f32[2,512,896]{2,1,0:T(8,128)} %refs_2_.9, ...), custom_call_target="tpu_custom_call", output_to_operand_aliasing={{0}: (4, {}), {1}: (5, {})} | custom-call | flops 4587520 | bytes 4587520 | tf_op jit(solution)/shard_map/update_rows/pallas_call | solution.py:180
  44.2 7.2 %collective-permute-done.4.refs_3_.refs_1_.refs_7_ = bf16[2,128,896]{2,1,0:T(8,128)(2,1)S(1)} collective-permute-done((bf16[2,128,896]{2,1,0:T(8,128)(2,1)S(1)}, bf16[2,128,896]{2,1,0:T(8,128)(2,1)S(1)}, u32[]{:S(2)}, u32[]{:S(2)}) %collective-permute-start.4) | collective-permute-done | bytes 458784 | tf_op jit(solution)/shard_map/cross/ppermute | solution.py:337
  51.3 4.0 %collective-permute-done.2.refs_0_.refs_2_.refs_4_ = bf16[3,128,896]{2,1,0:T(8,128)(2,1)S(1)} collective-permute-done((bf16[3,128,896]{2,1,0:T(8,128)(2,1)S(1)}, bf16[3,128,896]{2,1,0:T(8,128)(2,1)S(1)}, u32[]{:S(2)}, u32[]{:S(2)}) %collective-permute-start.2) | collective-permute-done | bytes 688160 | tf_op jit(solution)/shard_map/two_up/ppermute | solution.py:337
  55.4 0.6 make_step.11
  56.3 2.5 %collective-permute-start.6 = (bf16[3,128,896]{2,1,0:T(8,128)(2,1)S(1)}, bf16[3,128,896]{2,1,0:T(8,128)(2,1)S(1)}, u32[]{:S(2)}, u32[]{:S(2)}) collective-permute-start(bf16[3,128,896]{2,1,0:T(8,128)(2,1)S(1)} %get-tuple-element.66), channel_id=1, source_target_pairs={{0,3},{1,0},{2,1},{3,2},{4,7},{5,4},{6,5},{7,6},{8,11},{9,8},{10,9... | collective-permute-start | bytes 2064392 | tf_op jit(solution)/shard_map/three_down/ppermute | solution.py:337
  58.8 0.9 make_step.12
  59.8 2.8 %update_rows.7 = (f32[2,512,896]{2,1,0:T(8,128)}, f32[2,512,896]{2,1,0:T(8,128)}, bf16[2,128,896]{2,1,0:T(8,128)(2,1)S(1)}) custom-call(f32[128,128]{1,0:T(8,128)S(1)} %bitcast.12, f32[2,512,896]{2,1,0:T(8,128)} %refs_0_.9, bf16[2,512,896]{2,1,0:T(8,128)(2,1)} %refs_1_.9, f32[2,512,896]{2,1,0:T(8,128)} %refs_2_.9, ...), custom_call_target="tpu_custom_call", output_to_operand_aliasing={{0}: (4, {}), {1}: (5, {})} | custom-call | flops 4587520 | bytes 4587520 | tf_op jit(solution)/shard_map/update_rows/pallas_call | solution.py:180
  62.6 9.3 %collective-permute-done.5.refs_0_.refs_2_.refs_4_ = bf16[3,128,896]{2,1,0:T(8,128)(2,1)S(1)} collective-permute-done((bf16[3,128,896]{2,1,0:T(8,128)(2,1)S(1)}, bf16[3,128,896]{2,1,0:T(8,128)(2,1)S(1)}, u32[]{:S(2)}, u32[]{:S(2)}) %collective-permute-start.5) | collective-permute-done | bytes 688160 | tf_op jit(solution)/shard_map/three_up/ppermute | solution.py:337
  71.9 0.6 make_step.13
  72.7 2.6 %collective-permute-start.9 = (bf16[3,128,896]{2,1,0:T(8,128)(2,1)S(1)}, bf16[3,128,896]{2,1,0:T(8,128)(2,1)S(1)}, u32[]{:S(2)}, u32[]{:S(2)}) collective-permute-start(bf16[3,128,896]{2,1,0:T(8,128)(2,1)S(1)} %get-tuple-element.70), channel_id=1, source_target_pairs={{0,3},{1,0},{2,1},{3,2},{4,7},{5,4},{6,5},{7,6},{8,11},{9,8},{10,9... | collective-permute-start | bytes 2064392 | tf_op jit(solution)/shard_map/four_down/ppermute | solution.py:337
  75.3 3.8 %collective-permute-start.11 = (bf16[2,128,896]{2,1,0:T(8,128)(2,1)S(1)}, bf16[2,128,896]{2,1,0:T(8,128)(2,1)S(1)}, u32[]{:S(2)}, u32[]{:S(2)}) collective-permute-start(bf16[2,128,896]{2,1,0:T(8,128)(2,1)S(1)} %get-tuple-element.73), channel_id=1, source_target_pairs={{0,4},{4,0},{8,12},{12,8},{1,5},{5,1},{9,13},{13,9},{2,6},{6,2},{1... | collective-permute-start | bytes 1376264 | tf_op jit(solution)/shard_map/core_one/ppermute | solution.py:337
  79.1 0.9 make_step.14
  80.1 0.4 collective-permute-done.11.refs_5_.refs_1_
  80.9 6.6 %collective-permute-done.8.refs_0_.refs_2_.refs_6_ = bf16[3,128,896]{2,1,0:T(8,128)(2,1)S(1)} collective-permute-done((bf16[3,128,896]{2,1,0:T(8,128)(2,1)S(1)}, bf16[3,128,896]{2,1,0:T(8,128)(2,1)S(1)}, u32[]{:S(2)}, u32[]{:S(2)}) %collective-permute-start.8) | collective-permute-done | bytes 688160 | tf_op jit(solution)/shard_map/four_up/ppermute | solution.py:337
  87.5 0.6 make_step.15
  88.3 2.6 %collective-permute-start.13 = (bf16[3,128,896]{2,1,0:T(8,128)(2,1)S(1)}, bf16[3,128,896]{2,1,0:T(8,128)(2,1)S(1)}, u32[]{:S(2)}, u32[]{:S(2)}) collective-permute-start(bf16[3,128,896]{2,1,0:T(8,128)(2,1)S(1)} %get-tuple-element.76), channel_id=1, source_target_pairs={{0,3},{1,0},{2,1},{3,2},{4,7},{5,4},{6,5},{7,6},{8,11},{9,8},{10,9... | collective-permute-start | bytes 2064392 | tf_op jit(solution)/shard_map/five_down/ppermute | solution.py:337
  90.9 0.9 make_step.16
  92.0 0.6 make_step.17.refs_2_
  92.6 5.1 %collective-permute-start.16 = (bf16[2,128,896]{2,1,0:T(8,128)(2,1)S(1)}, bf16[2,128,896]{2,1,0:T(8,128)(2,1)S(1)}, u32[]{:S(2)}, u32[]{:S(2)}) collective-permute-start(bf16[2,128,896]{2,1,0:T(8,128)(2,1)S(1)} %make_step.17.refs_2_), channel_id=1, source_target_pairs={{0,4},{4,0},{8,12},{12,8},{1,5},{5,1},{9,13},{13,9},{2,6},{6,2},{1... | collective-permute-start | bytes 1376264 | tf_op jit(solution)/shard_map/core_pass/ppermute | solution.py:337
  97.7 4.4 %collective-permute-done.7.refs_3_.refs_0_.refs_2_ = bf16[4,128,896]{2,1,0:T(8,128)(2,1)S(1)} collective-permute-done((bf16[4,128,896]{2,1,0:T(8,128)(2,1)S(1)}, bf16[4,128,896]{2,1,0:T(8,128)(2,1)S(1)}, u32[]{:S(2)}, u32[]{:S(2)}) %collective-permute-start.7) | collective-permute-done | bytes 917536 | tf_op jit(solution)/shard_map/chip_two/ppermute | solution.py:337
  102.1 1.0 collective-permute-start.19
  103.2 8.8 %collective-permute-done.14.refs_4_ = bf16[2,128,896]{2,1,0:T(8,128)(2,1)S(1)} collective-permute-done((bf16[2,128,896]{2,1,0:T(8,128)(2,1)S(1)}, bf16[2,128,896]{2,1,0:T(8,128)(2,1)S(1)}, u32[]{:S(2)}, u32[]{:S(2)}) %collective-permute-start.14) | collective-permute-done | bytes 458784 | tf_op jit(solution)/shard_map/chip_three/ppermute | solution.py:337
  112.0 0.6 make_step.18
  112.6 2.7 %collective-permute-start.18 = (bf16[1,128,896]{2,1,0:T(8,128)(2,1)S(1)}, bf16[1,128,896]{2,1,0:T(8,128)(2,1)S(1)}, u32[]{:S(2)}, u32[]{:S(2)}) collective-permute-start(bf16[1,128,896]{2,1,0:T(8,128)(2,1)S(1)} %get-tuple-element.81), channel_id=1, source_target_pairs={{0,3},{1,0},{2,1},{3,2},{4,7},{5,4},{6,5},{7,6},{8,11},{9,8},{10,9... | collective-permute-start | bytes 688136 | tf_op jit(solution)/shard_map/last_down/ppermute | solution.py:337
  115.3 1.8 %quantize_rows.3 = (bf16[1,1,2,2048,896]{4,3,2,1,0:T(8,128)(2,1)}, f32[1,1,2,16,7]{4,3,2,1,0:T(8,128)S(1)}) custom-call(s32[1]{0:T(128)} %bitcast.5.replica_ref, bf16[2,128,896]{2,1,0:T(8,128)(2,1)S(1)} %get-tuple-element.63.refs_5_.refs_3_.refs_0_, bf16[2,128,896]{2,1,0:T(8,128)(2,1)S(1)} %collective-permute-done.11.refs_5_.refs_1_, ...), custom_call_target="tpu_custom_call" | custom-call | flops 4587520 | bytes 3670016 | tf_op jit(solution)/shard_map/quantize_rows/pallas_call | solution.py:302
  117.1 4.8 %collective-permute-done.19.refs_11_.refs_5_ = bf16[2,128,896]{2,1,0:T(8,128)(2,1)S(1)} collective-permute-done((bf16[2,128,896]{2,1,0:T(8,128)(2,1)S(1)}, bf16[2,128,896]{2,1,0:T(8,128)(2,1)S(1)}, u32[]{:S(2)}, u32[]{:S(2)}) %collective-permute-start.19) | collective-permute-done | bytes 458784 | tf_op jit(solution)/shard_map/both_three/ppermute | solution.py:337
  121.9 1.0 make_step.19
  122.9 0.4 collective-permute-start.20
  123.3 3.0 %quantize_rows.4 = (bf16[1,1,2,2048,896]{4,3,2,1,0:T(8,128)(2,1)}, f32[1,1,2,16,7]{4,3,2,1,0:T(8,128)S(1)}) custom-call(s32[1]{0:T(128)} %bitcast.5.replica_ref, bf16[2,128,896]{2,1,0:T(8,128)(2,1)S(1)} %get-tuple-element.71.refs_3_.refs_0_, bf16[2,128,896]{2,1,0:T(8,128)(2,1)S(1)} %collective-permute-done.15.refs_5_.refs_1_, ...), custom_call_target="tpu_custom_call", output_to_operand_aliasing={{0}: (9, {})} | custom-call | flops 9175040 | bytes 7340032 | tf_op jit(solution)/shard_map/quantize_rows/pallas_call | solution.py:302
  126.3 0.5 collective-permute-done.20.refs_0_
  126.8 1.8 %quantize_rows.5 = (bf16[1,1,2,2048,896]{4,3,2,1,0:T(8,128)(2,1)}, f32[1,1,2,16,7]{4,3,2,1,0:T(8,128)S(1)}) custom-call(s32[1]{0:T(128)} %bitcast.5.replica_ref, bf16[8,128,896]{2,1,0:T(8,128)(2,1)S(1)} %collective-permute-done.20.refs_0_, bf16[1,1,2,2048,896]{4,3,2,1,0:T(8,128)(2,1)} %get-tuple-element.88.refs_1_, ...), custom_call_target="tpu_custom_call", output_to_operand_aliasing={{0}: (2, {})} | custom-call | flops 4587520 | bytes 3670016 | tf_op jit(solution)/shard_map/quantize_rows/pallas_call | solution.py:302
  128.6 0.7 copy.26
  (31 shorter events, 2.1 us)
Async XLA Ops:
  0.6 1.5 %copy-start = (bf16[2,512,896]{2,1,0:T(8,128)(2,1)S(1)}, bf16[2,512,896]{2,1,0:T(8,128)(2,1)}, u32[]{:S(2)}) copy-start(bf16[2,512,896]{2,1,0:T(8,128)(2,1)} %refs_1_.9) | copy-start | bytes 5505028
  3.2 21.1 %all-to-all-start = ((f32[128,1,128]{2,1,0:T(1,128)}), f32[128,1,128]{2,1,0:T(1,128)S(1)}, u32[]{:S(2)}, u32[]{:S(2)}) async-start(f32[128,1,128]{2,1,0:T(1,128)} %bitcast.1), calls=%async_computation | async-start | bytes 131072 | tf_op jit(solution)/shard_map/all_to_all | solution.py:333
  25.1 12.8 %collective-permute-start = (bf16[2,128,896]{2,1,0:T(8,128)(2,1)S(1)}, bf16[2,128,896]{2,1,0:T(8,128)(2,1)S(1)}, u32[]{:S(2)}, u32[]{:S(2)}) collective-permute-start(bf16[2,128,896]{2,1,0:T(8,128)(2,1)S(1)} %first_weights.1.refs_3_.refs_0_), channel_id=1, source_target_pairs={{0,1},{1,2},{2,3},{3,0},{4,5},{5,6},{6,7},{7,4},{8,9},{9,10},{10,1... | collective-permute-start | bytes 1376264 | tf_op jit(solution)/shard_map/one_up/ppermute | solution.py:337
  25.7 12.2 %collective-permute-start.1 = (bf16[2,128,896]{2,1,0:T(8,128)(2,1)S(1)}, bf16[2,128,896]{2,1,0:T(8,128)(2,1)S(1)}, u32[]{:S(2)}, u32[]{:S(2)}) collective-permute-start(bf16[2,128,896]{2,1,0:T(8,128)(2,1)S(1)} %first_weights.1.refs_3_.refs_0_), channel_id=1, source_target_pairs={{0,3},{1,0},{2,1},{3,2},{4,7},{5,4},{6,5},{7,6},{8,11},{9,8},{10,9... | collective-permute-start | bytes 1376264 | tf_op jit(solution)/shard_map/one_down/ppermute | solution.py:337
  38.5 16.8 %collective-permute-start.2 = (bf16[3,128,896]{2,1,0:T(8,128)(2,1)S(1)}, bf16[3,128,896]{2,1,0:T(8,128)(2,1)S(1)}, u32[]{:S(2)}, u32[]{:S(2)}) collective-permute-start(bf16[3,128,896]{2,1,0:T(8,128)(2,1)S(1)} %get-tuple-element.57.refs_5_), channel_id=1, source_target_pairs={{0,1},{1,2},{2,3},{3,0},{4,5},{5,6},{6,7},{7,4},{8,9},{9,10},{10,1... | collective-permute-start | bytes 2064392 | tf_op jit(solution)/shard_map/two_up/ppermute | solution.py:337
  38.6 16.7 %collective-permute-start.3 = (bf16[3,128,896]{2,1,0:T(8,128)(2,1)S(1)}, bf16[3,128,896]{2,1,0:T(8,128)(2,1)S(1)}, u32[]{:S(2)}, u32[]{:S(2)}) collective-permute-start(bf16[3,128,896]{2,1,0:T(8,128)(2,1)S(1)} %get-tuple-element.60), channel_id=1, source_target_pairs={{0,3},{1,0},{2,1},{3,2},{4,7},{5,4},{6,5},{7,6},{8,11},{9,8},{10,9... | collective-permute-start | bytes 2064392 | tf_op jit(solution)/shard_map/two_down/ppermute | solution.py:337
  41.3 10.1 %collective-permute-start.4 = (bf16[2,128,896]{2,1,0:T(8,128)(2,1)S(1)}, bf16[2,128,896]{2,1,0:T(8,128)(2,1)S(1)}, u32[]{:S(2)}, u32[]{:S(2)}) collective-permute-start(bf16[2,128,896]{2,1,0:T(8,128)(2,1)S(1)} %get-tuple-element.56.refs_3_.refs_1_.refs_2_), channel_id=1, source_target_pairs={{0,8},{4,12},{8,0},{12,4},{1,9},{5,13},{9,1},{13,5},{2,10},{6,14},... | collective-permute-start | bytes 1376264 | tf_op jit(solution)/shard_map/cross/ppermute | solution.py:337
  56.0 15.9 %collective-permute-start.5 = (bf16[3,128,896]{2,1,0:T(8,128)(2,1)S(1)}, bf16[3,128,896]{2,1,0:T(8,128)(2,1)S(1)}, u32[]{:S(2)}, u32[]{:S(2)}) collective-permute-start(bf16[3,128,896]{2,1,0:T(8,128)(2,1)S(1)} %get-tuple-element.62.refs_5_), channel_id=1, source_target_pairs={{0,1},{1,2},{2,3},{3,0},{4,5},{5,6},{6,7},{7,4},{8,9},{9,10},{10,1... | collective-permute-start | bytes 2064392 | tf_op jit(solution)/shard_map/three_up/ppermute | solution.py:337
  56.3 15.6 %collective-permute-start.6 = (bf16[3,128,896]{2,1,0:T(8,128)(2,1)S(1)}, bf16[3,128,896]{2,1,0:T(8,128)(2,1)S(1)}, u32[]{:S(2)}, u32[]{:S(2)}) collective-permute-start(bf16[3,128,896]{2,1,0:T(8,128)(2,1)S(1)} %get-tuple-element.66), channel_id=1, source_target_pairs={{0,3},{1,0},{2,1},{3,2},{4,7},{5,4},{6,5},{7,6},{8,11},{9,8},{10,9... | collective-permute-start | bytes 2064392 | tf_op jit(solution)/shard_map/three_down/ppermute | solution.py:337
  59.7 21.2 %collective-permute-start.10 = (bf16[4,128,896]{2,1,0:T(8,128)(2,1)S(1)}, bf16[4,128,896]{2,1,0:T(8,128)(2,1)S(1)}, u32[]{:S(2)}, u32[]{:S(2)}) collective-permute-start(bf16[4,128,896]{2,1,0:T(8,128)(2,1)S(1)} %get-tuple-element.72), channel_id=1, source_target_pairs={{0,8},{4,12},{8,0},{12,4},{1,9},{5,13},{9,1},{13,5},{2,10},{6,14},... | collective-permute-start | bytes 2752520 | tf_op jit(solution)/shard_map/chip_one/ppermute | solution.py:337
  72.6 15.0 %collective-permute-start.8 = (bf16[3,128,896]{2,1,0:T(8,128)(2,1)S(1)}, bf16[3,128,896]{2,1,0:T(8,128)(2,1)S(1)}, u32[]{:S(2)}, u32[]{:S(2)}) collective-permute-start(bf16[3,128,896]{2,1,0:T(8,128)(2,1)S(1)} %get-tuple-element.68.refs_5_), channel_id=1, source_target_pairs={{0,1},{1,2},{2,3},{3,0},{4,5},{5,6},{6,7},{7,4},{8,9},{9,10},{10,1... | collective-permute-start | bytes 2064392 | tf_op jit(solution)/shard_map/four_up/ppermute | solution.py:337
  72.7 14.8 %collective-permute-start.9 = (bf16[3,128,896]{2,1,0:T(8,128)(2,1)S(1)}, bf16[3,128,896]{2,1,0:T(8,128)(2,1)S(1)}, u32[]{:S(2)}, u32[]{:S(2)}) collective-permute-start(bf16[3,128,896]{2,1,0:T(8,128)(2,1)S(1)} %get-tuple-element.70), channel_id=1, source_target_pairs={{0,3},{1,0},{2,1},{3,2},{4,7},{5,4},{6,5},{7,6},{8,11},{9,8},{10,9... | collective-permute-start | bytes 2064392 | tf_op jit(solution)/shard_map/four_down/ppermute | solution.py:337
  75.3 5.2 %collective-permute-start.11 = (bf16[2,128,896]{2,1,0:T(8,128)(2,1)S(1)}, bf16[2,128,896]{2,1,0:T(8,128)(2,1)S(1)}, u32[]{:S(2)}, u32[]{:S(2)}) collective-permute-start(bf16[2,128,896]{2,1,0:T(8,128)(2,1)S(1)} %get-tuple-element.73), channel_id=1, source_target_pairs={{0,4},{4,0},{8,12},{12,8},{1,5},{5,1},{9,13},{13,9},{2,6},{6,2},{1... | collective-permute-start | bytes 1376264 | tf_op jit(solution)/shard_map/core_one/ppermute | solution.py:337
  80.1 22.1 %collective-permute-start.7 = (bf16[4,128,896]{2,1,0:T(8,128)(2,1)S(1)}, bf16[4,128,896]{2,1,0:T(8,128)(2,1)S(1)}, u32[]{:S(2)}, u32[]{:S(2)}) collective-permute-start(bf16[4,128,896]{2,1,0:T(8,128)(2,1)S(1)} %get-tuple-element.69), channel_id=1, source_target_pairs={{0,8},{4,12},{8,0},{12,4},{1,9},{5,13},{9,1},{13,5},{2,10},{6,14},... | collective-permute-start | bytes 2752520 | tf_op jit(solution)/shard_map/chip_two/ppermute | solution.py:337
  80.5 12.0 %collective-permute-start.15 = (bf16[2,128,896]{2,1,0:T(8,128)(2,1)S(1)}, bf16[2,128,896]{2,1,0:T(8,128)(2,1)S(1)}, u32[]{:S(2)}, u32[]{:S(2)}) collective-permute-start(bf16[2,128,896]{2,1,0:T(8,128)(2,1)S(1)} %get-tuple-element.79), channel_id=1, source_target_pairs={{0,4},{4,0},{8,12},{12,8},{1,5},{5,1},{9,13},{13,9},{2,6},{6,2},{1... | collective-permute-start | bytes 1376264 | tf_op jit(solution)/shard_map/core_two/ppermute | solution.py:337
  88.2 23.8 %collective-permute-start.12 = (bf16[3,128,896]{2,1,0:T(8,128)(2,1)S(1)}, bf16[3,128,896]{2,1,0:T(8,128)(2,1)S(1)}, u32[]{:S(2)}, u32[]{:S(2)}) collective-permute-start(bf16[3,128,896]{2,1,0:T(8,128)(2,1)S(1)} %get-tuple-element.74.refs_5_), channel_id=1, source_target_pairs={{0,1},{1,2},{2,3},{3,0},{4,5},{5,6},{6,7},{7,4},{8,9},{9,10},{10,1... | collective-permute-start | bytes 2064392 | tf_op jit(solution)/shard_map/five_up/ppermute | solution.py:337
  88.3 23.7 %collective-permute-start.13 = (bf16[3,128,896]{2,1,0:T(8,128)(2,1)S(1)}, bf16[3,128,896]{2,1,0:T(8,128)(2,1)S(1)}, u32[]{:S(2)}, u32[]{:S(2)}) collective-permute-start(bf16[3,128,896]{2,1,0:T(8,128)(2,1)S(1)} %get-tuple-element.76), channel_id=1, source_target_pairs={{0,3},{1,0},{2,1},{3,2},{4,7},{5,4},{6,5},{7,6},{8,11},{9,8},{10,9... | collective-permute-start | bytes 2064392 | tf_op jit(solution)/shard_map/five_down/ppermute | solution.py:337
  91.9 20.1 %collective-permute-start.14 = (bf16[2,128,896]{2,1,0:T(8,128)(2,1)S(1)}, bf16[2,128,896]{2,1,0:T(8,128)(2,1)S(1)}, u32[]{:S(2)}, u32[]{:S(2)}) collective-permute-start(bf16[2,128,896]{2,1,0:T(8,128)(2,1)S(1)} %get-tuple-element.78), channel_id=1, source_target_pairs={{0,8},{4,12},{8,0},{12,4},{1,9},{5,13},{9,1},{13,5},{2,10},{6,14},... | collective-permute-start | bytes 1376264 | tf_op jit(solution)/shard_map/chip_three/ppermute | solution.py:337
  92.6 19.4 %collective-permute-start.16 = (bf16[2,128,896]{2,1,0:T(8,128)(2,1)S(1)}, bf16[2,128,896]{2,1,0:T(8,128)(2,1)S(1)}, u32[]{:S(2)}, u32[]{:S(2)}) collective-permute-start(bf16[2,128,896]{2,1,0:T(8,128)(2,1)S(1)} %make_step.17.refs_2_), channel_id=1, source_target_pairs={{0,4},{4,0},{8,12},{12,8},{1,5},{5,1},{9,13},{13,9},{2,6},{6,2},{1... | collective-permute-start | bytes 1376264 | tf_op jit(solution)/shard_map/core_pass/ppermute | solution.py:337
  102.1 19.8 %collective-permute-start.19 = (bf16[2,128,896]{2,1,0:T(8,128)(2,1)S(1)}, bf16[2,128,896]{2,1,0:T(8,128)(2,1)S(1)}, u32[]{:S(2)}, u32[]{:S(2)}) collective-permute-start(bf16[2,128,896]{2,1,0:T(8,128)(2,1)S(1)} %get-tuple-element.83), channel_id=1, source_target_pairs={{0,12},{4,8},{8,4},{12,0},{1,13},{5,9},{9,5},{13,1},{2,14},{6,10},... | collective-permute-start | bytes 1376264 | tf_op jit(solution)/shard_map/both_three/ppermute | solution.py:337
  112.5 9.3 %collective-permute-start.17 = (bf16[1,128,896]{2,1,0:T(8,128)(2,1)S(1)}, bf16[1,128,896]{2,1,0:T(8,128)(2,1)S(1)}, u32[]{:S(2)}, u32[]{:S(2)}) collective-permute-start(bf16[1,128,896]{2,1,0:T(8,128)(2,1)S(1)} %get-tuple-element.80), channel_id=1, source_target_pairs={{0,1},{1,2},{2,3},{3,0},{4,5},{5,6},{6,7},{7,4},{8,9},{9,10},{10,1... | collective-permute-start | bytes 688136 | tf_op jit(solution)/shard_map/last_up/ppermute | solution.py:337
  112.6 9.3 %collective-permute-start.18 = (bf16[1,128,896]{2,1,0:T(8,128)(2,1)S(1)}, bf16[1,128,896]{2,1,0:T(8,128)(2,1)S(1)}, u32[]{:S(2)}, u32[]{:S(2)}) collective-permute-start(bf16[1,128,896]{2,1,0:T(8,128)(2,1)S(1)} %get-tuple-element.81), channel_id=1, source_target_pairs={{0,3},{1,0},{2,1},{3,2},{4,7},{5,4},{6,5},{7,6},{8,11},{9,8},{10,9... | collective-permute-start | bytes 688136 | tf_op jit(solution)/shard_map/last_down/ppermute | solution.py:337
  122.9 3.9 %collective-permute-start.20 = (bf16[8,128,896]{2,1,0:T(8,128)(2,1)S(1)}, bf16[8,128,896]{2,1,0:T(8,128)(2,1)S(1)}, u32[]{:S(2)}, u32[]{:S(2)}) collective-permute-start(bf16[8,128,896]{2,1,0:T(8,128)(2,1)S(1)} %get-tuple-element.84), channel_id=1, source_target_pairs={{0,4},{4,0},{8,12},{12,8},{1,5},{5,1},{9,13},{13,9},{2,6},{6,2},{1... | collective-permute-start | bytes 5505032 | tf_op jit(solution)/shard_map/core_last/ppermute | solution.py:337

commit v3 on v2

--- a/solution.py
+++ b/solution.py
@@ -36,7 +36,7 @@
 
 def squares_kernel(gradient_ref, out_ref):
     experts, rows, cols = gradient_ref.shape
-    step = 32
+    step = 64
     total = jnp.zeros((8, cols), jnp.float32)
     for expert in range(experts):
 
@@ -211,7 +211,8 @@
     return jnp.sum(selected * expert_ids, axis=-1)
 
 
-def step_kernel(moves, n, table_ref, *refs):
+def step_kernel(moves, n, *refs):
+    table_ref = refs[n]
     arrays, outs = refs[:n], refs[len(refs) - 1 - max(m[0] for m in moves) :]
     for out, place, entry, sources in moves:
         if entry is None:
@@ -252,26 +253,28 @@
             else:
                 moves.append((out, place, None, (number_of(first), second)))
     rows, cols = arrays[0].shape[1:]
+    tables = [table] if any(move[2] is not None for move in moves) else []
     return pl.pallas_call(
         functools.partial(step_kernel, moves, len(arrays)),
-        in_specs=[SMEM] + [VMEM] * len(arrays) + [ANY] * len(after),
+        in_specs=[VMEM] * len(arrays) + [SMEM] * len(tables) + [ANY] * len(after),
         out_specs=[VMEM] * len(outs),
         out_shape=[kept((len(pieces), rows, cols), jnp.bfloat16) for pieces in outs],
         cost_estimate=cost(max(int(work * 3.3e6), len(moves) * rows * cols * 4)),
         compiler_params=LIMIT,
         name="make_step",
-    )(table, *(held(a) for a in arrays), *after)
-
-
-def quantize_kernel(places, replica_ref, *refs):
+    )(*(held(a) for a in arrays), *tables, *after)
+
+
+def quantize_kernel(places, *refs):
     n = len({place[0] for place in places})
+    replica = lax.axis_index("replica")
     parts, earlier, (out_ref, scales_ref, ready, sems) = refs[:n], refs[n:-4], refs[-4:]
     scales_ref[...] = earlier[1][...] if earlier else jnp.zeros_like(scales_ref)
     rows, cols = parts[0].shape[1:]
     blocks = cols // BLOCK
     copies = []
     for number, (part, index, flip, slot, chunk) in enumerate(places):
-        block_row = jnp.bitwise_xor(replica_ref[0], flip) * 4 + chunk
+        block_row = jnp.bitwise_xor(replica, flip) * 4 + chunk
         tops = []
         for block in range(blocks):
             values = jnp.abs(parts[part][index, :, block * BLOCK : (block + 1) * BLOCK].astype(jnp.float32))
@@ -295,16 +298,16 @@
         copy.wait()
 
 
-def quantize(replica, parts, places, shape, earlier):
+def quantize(parts, places, shape, earlier):
     rows, cols = parts[0].shape[1:]
     scales_shape = (1, 1, shape[2], shape[3] // BLOCK, cols // BLOCK)
     n = len(parts)
     return pl.pallas_call(
         functools.partial(quantize_kernel, tuple(places)),
-        in_specs=[SMEM] + [VMEM] * n + ([ANY, VMEM] if earlier else []),
+        in_specs=[VMEM] * n + ([ANY, VMEM] if earlier else []),
         out_specs=[HBM, VMEM],
         out_shape=[jax.ShapeDtypeStruct(shape, jnp.bfloat16), jax.ShapeDtypeStruct(scales_shape, jnp.float32)],
-        input_output_aliases={1 + n: 0} if earlier else {},
+        input_output_aliases={n: 0} if earlier else {},
         scratch_shapes=[
             pltpu.VMEM((len(places), rows, cols), jnp.bfloat16),
             pltpu.SemaphoreType.DMA((len(places),)),
@@ -312,7 +315,7 @@
         cost_estimate=cost(len(places) * rows * cols * 4, len(places) * rows * cols * 5),
         compiler_params=pltpu.CompilerParams(vmem_limit_bytes=12 << 20),
         name="quantize_rows",
-    )(replica, *(held(p) for p in parts), *earlier)
+    )(*(held(p) for p in parts), *earlier)
 
 
 def body(master, gradient, second, placement):
@@ -325,11 +328,10 @@
     order = jnp.bitwise_xor(replica, jnp.arange(n_replica, dtype=jnp.int32))
     named = slots[order].reshape(-1)
     table = 2 * ((named // 2 - holder) % n_ep) + named % 2
-    replica_ref = replica[None]
 
     devices = ("train", "replica", "ep")
     part = local_squares(gradient, n_train * n_replica * n_ep)
-    master1, gradient1, second1 = load_rows((master, gradient, second), 1, (part,))
+    master1, gradient1, second1 = load_rows((master, gradient, second), 1, (part, table))
     total = lax.all_to_all(part, devices, 0, 0, tiled=True)
 
     def send(value, axis, order, name):
@@ -369,7 +371,8 @@
     new, e = update(0, (), (w1,))
     new, w2 = update(2, new)
 
-    a, b = step("turn_one", [[(below1, 0)] + both(w2), [(above1, 1)] + both(w2)], (e,))
+    (a,) = step("turn_one_up", [[(below1, 0)] + both(w2)], (e,))
+    (b,) = step("turn_one_down", [[(above1, 1)] + both(w2)], (a,))
     below2, above2 = up(a, "two"), down(b, "two")
     f = flip(e, 2, "cross")
     new, w3 = update(3, new, (a,))
@@ -378,52 +381,60 @@
         outs = [sum((slots_of((j,), *ring) for j in group), []) for group in flips]
         return step("pick_" + name, outs + [slots_of((0,), *ring)], after)
 
-    a, b = step("turn_two", [[(below2, 1)] + both(w3), [(above2, 2)] + both(w3)], (f,))
+    (a,) = step("turn_two_up", [[(below2, 1)] + both(w3)], (f,))
+    (b,) = step("turn_two_down", [[(above2, 2)] + both(w3)], (a,))
     below3, above3 = up(a, "three"), down(b, "three")
     ring1 = (both(w1), both(above1), [(below2, 0), (above2, 0)], both(below1))
     x, o1, s1 = pick("one", ring1, ((2, 3), (1,)), (a,))
     y1 = flip(x, 2, "chip_one")
     new, again = update(1, new, (s1,))
 
-    a, b = step("turn_three", [[(below3, 1)] + both(e), [(above3, 2)] + both(e)], (s1, again))
+    (a,) = step("turn_three_up", [[(below3, 1)] + both(e)], (again,))
+    (b,) = step("turn_three_down", [[(above3, 2)] + both(e)], (a,))
     below4, above4 = up(a, "four"), down(b, "four")
-    z1 = flip(o1, 1, "core_one")
     ring2 = (both(w2), both(above2, 1), [(below3, 0), (above3, 0)], both(below2, 1))
-    x, o2, s2 = pick("two", ring2, ((2, 3), (1,)), (a,))
+    x, o1, o2, s2 = step(
+        "pick_two",
+        [slots_of((2, 3), *ring2), both(o1), slots_of((1,), *ring2), slots_of((0,), *ring2)],
+        (a,),
+    )
     y2 = flip(x, 2, "chip_two")
-
-    a, b = step("turn_four", [[(below4, 1)] + both(f), [(above4, 2)] + both(f)], (s2, y1, z1))
+    z1, z2 = flip(o1, 1, "core_one"), flip(o2, 1, "core_two")
+
+    (a,) = step("turn_four_up", [[(below4, 1)] + both(f)], (s2, y1, z1, z2))
+    (b,) = step("turn_four_down", [[(above4, 2)] + both(f)], (a,))
     below5, above5 = up(a, "five"), down(b, "five")
     ring3 = (both(w3), both(above3, 1), [(below4, 0), (above4, 0)], both(below3, 1))
-    x3, v3, o3, s3 = pick("three", ring3, ((2,), (3,), (1,)), (a,))
-    x3 = flip(x3, 2, "chip_three")
-    z2 = flip(o2, 1, "core_two")
+    x = slots_of((2,), *ring3)
+    xa, xb, xc, o3, s3 = step(
+        "pick_three",
+        [x[:1], x[1:], slots_of((3,), *ring3), slots_of((1,), *ring3), slots_of((0,), *ring3)],
+        (a,),
+    )
+    xa = flip(xa, 2, "chip_three")
     (c,) = step("pass_one", [both(y1, 2)], (s3,))
-    t1 = flip(c, 1, "core_pass")
-
-    a, b = step("turn_five", [[(below5, 1)], [(above5, 2)]], (c, y2, x3, z2, t1))
+    t1 = flip(c, 1, "core_pass_one")
+
+    (a,) = step("turn_five_up", [[(below5, 1)]], (t1, y2, xa))
+    b, c = step("turn_five_down", [[(above5, 2)], both(y2, 2) + both(o3)], (a,))
     far_low_f, far_high_f = up(a, "last"), down(b, "last")
-    v3 = flip(v3, 3, "both_three")
-    places = place(1, (0, 0, 0), (1, 0, 1), (2, 0, 2), (3, 0, 3))
-    result = quantize(replica_ref, [s1, z1, y1, t1], places, shape, ())
+    z = flip(c, 1, "core_join")
+    xb, xc = flip(xb, 2, "chip_three_more"), flip(xc, 3, "both_three")
+    places = place(1, (0, 0, 0), (1, 0, 1), (2, 0, 2), (3, 0, 3)) + place(2, (4, 0, 0), (5, 0, 1), (6, 0, 2))
+    result = quantize([s1, z1, y1, t1, s2, z2, y2], places, shape, ())
 
     ring_e = (both(e), both(above4, 1), [(below5, 0), (above5, 0)], both(below4, 1))
     ring_f = (both(f), both(above5, 1), [(far_low_f, 0), (far_high_f, 0)], both(below5, 1))
-    c, sf, se = step(
-        "join_last",
-        [
-            both(y2, 2) + both(o3) + slots_of((1,), *ring_e) + slots_of((1,), *ring_f),
-            slots_of((0,), *ring_f),
-            slots_of((0,), *ring_e),
-        ],
-        (result[1], v3),
-    )
-    z = flip(c, 1, "core_last")
-    places = place(2, (0, 0, 0), (1, 0, 1), (2, 0, 2)) + place(3, (3, 0, 0), (4, 0, 2), (5, 0, 3))
-    places += place(0, (6, 0, 0), (7, 0, 2))
-    result = quantize(replica_ref, [s2, z2, y2, s3, x3, v3, se, sf], places, shape, tuple(result))
-    places = place(2, (0, 0, 3)) + place(3, (0, 2, 1)) + place(0, (0, 4, 1), (0, 6, 3))
-    result = quantize(replica_ref, [z], places, shape, tuple(result))
+    pieces = slots_of((1,), *ring_e) + slots_of((1,), *ring_f)
+    outs = [[piece] for piece in pieces] + [slots_of((0,), *ring_e), slots_of((0,), *ring_f)]
+    *pieces, se, sf = step("pick_last", outs, (result[1], xb))
+    pieces = [flip(piece, 1, "core_last") for piece in pieces]
+    places = place(3, (0, 0, 0), (1, 2, 1)) + [(2, 0, 2, 0, 3), (3, 0, 2, 1, 3)]
+    places += place(0, (4, 0, 0), (5, 0, 2)) + place(2, (1, 0, 3))
+    result = quantize([s3, z, xa, xb, se, sf], places, shape, tuple(result))
+    places = [(0, 0, 1, 0, 0), (1, 0, 1, 1, 0), (2, 0, 3, 0, 0), (3, 0, 3, 1, 0)]
+    result = quantize(pieces, places, shape, tuple(result))
+    result = quantize([xc], place(3, (0, 0, 3)), shape, tuple(result))
     return (*new, *result)
 
 

time: 130 us -> 125 us (0.962)
  waiting for transfers between devices: 55.8 us -> 48.3 us
  starting transfers between devices: 39 us -> 45.1 us
  Pallas kernels: 28.7 us -> 26 us
    ppermute x21 -> x26, waiting for transfers between devices: 49.5 us -> 42.9 us  [send(): return lax.ppermute(value, axis, order)]
    ppermute x21 -> x26, starting transfers between devices: 27.5 us -> 33.6 us  [send(): return lax.ppermute(value, axis, order)]
    pallas_call x10 -> x15, Pallas kernels: 7.56 us -> 4.31 us  [make_step(): pl.pallas_call(functools.partial(step_kernel, moves, len(arrays)), in_spe...]
    pallas_call x3 -> x4, Pallas kernels: 6.57 us -> 7.27 us  [quantize(): pl.pallas_call(functools.partial(quantize_kernel, tuple(places)), in_spec...]
  transfers between devices with their start and end apart: 22 -> 27, of which waited for: 11 -> 12; matrix products, arithmetic and copies ran while one was open for 2% -> 2% of each run, Pallas kernels for 18% -> 19%
where the time goes in v3:
time: 125 us
  waiting for transfers between devices  48.3 us (39%)
  starting transfers between devices  45.1 us (36%)
  Pallas kernels  26 us (21%)
  local copies, waits for them, and re-layouts  3.09 us (2%)
  other arithmetic  1.67 us (1%)
    ppermute x26, waiting for transfers between devices, send(): return lax.ppermute(value, axis, order)  42.9 us
    ppermute x26, starting transfers between devices, send(): return lax.ppermute(value, axis, order)  33.6 us
    all_to_all x1, starting transfers between devices, body(): total = lax.all_to_all(part, devices, 0, 0, tiled=True)  11.5 us
    pallas_call x4, Pallas kernels, update_rows(): pl.pallas_call(functools.partial(update_kernel, count, chunk), in_specs=[...  11.1 us
    pallas_call x4, Pallas kernels, quantize(): pl.pallas_call(functools.partial(quantize_kernel, tuple(places)), in_spec...  7.27 us
    all_to_all x1, waiting for transfers between devices, body(): total = lax.all_to_all(part, devices, 0, 0, tiled=True)  5.33 us
    pallas_call x15, Pallas kernels, make_step(): pl.pallas_call(functools.partial(step_kernel, moves, len(arrays)), in_spe...  4.31 us
  transfers between devices with their start and end apart: 27, of which 12 were waited for; matrix products, arithmetic and copies ran while one was open for 2% of the time, Pallas kernels for 19%

profile of v3, /device:TPU:1, one launch (start us, length us, event | category | flops | bytes accessed | tf_op | source)
XLA Modules:
  0.0 125.1 jit_solution(10821300988897401670)
XLA Ops:
  0.6 1.5 %copy-done = bf16[2,512,896]{2,1,0:T(8,128)(2,1)S(1)} copy-done((bf16[2,512,896]{2,1,0:T(8,128)(2,1)S(1)}, bf16[2,512,896]{2,1,0:T(8,128)(2,1)}, u32[]{:S(2)}) %copy-start) | copy-done | bytes 1835032
  2.1 0.9 local_squares.1.refs_3_
  3.0 11.5 %all-to-all-start = ((f32[128,1,128]{2,1,0:T(1,128)}), f32[128,1,128]{2,1,0:T(1,128)S(1)}, u32[]{:S(2)}, u32[]{:S(2)}) async-start(f32[128,1,128]{2,1,0:T(1,128)} %bitcast.1), calls=%async_computation | async-start | bytes 131072 | tf_op jit(solution)/shard_map/all_to_all | solution.py:335
  14.5 0.7 fusion
  15.2 0.7 reduce_window_sum.11
  15.9 0.2 multiply_reduce_fusion
  16.5 0.6 gather_fusion
  17.1 1.6 %load_rows.1 = (f32[2,128,896]{2,1,0:T(8,128)S(1)}, bf16[2,128,896]{2,1,0:T(8,128)(2,1)S(1)}, f32[2,128,896]{2,1,0:T(8,128)S(1)}) custom-call(f32[2,512,896]{2,1,0:T(8,128)} %refs_0_.9, bf16[2,512,896]{2,1,0:T(8,128)(2,1)} %refs_1_.9, f32[2,512,896]{2,1,0:T(8,128)} %refs_2_.9, f32[128,128]{1,0:T(8,128)} %local_squares.1.refs_3_, ...), custom_call_target="tpu_custom_call" | custom-call | bytes 5505024 | tf_op jit(solution)/shard_map/load_rows/pallas_call | solution.py:82
  18.8 5.3 %all-to-all-done = f32[128,1,128]{2,1,0:T(1,128)S(1)} async-done(((f32[128,1,128]{2,1,0:T(1,128)}), f32[128,1,128]{2,1,0:T(1,128)S(1)}, u32[]{:S(2)}, u32[]{:S(2)}) %all-to-all-start) | async-done | bytes 65568 | tf_op jit(solution)/shard_map/all_to_all | solution.py:335
  24.1 0.8 first_weights.1.refs_3_.refs_0_
  24.9 0.6 collective-permute-start
  25.5 2.1 %collective-permute-start.1 = (bf16[2,128,896]{2,1,0:T(8,128)(2,1)S(1)}, bf16[2,128,896]{2,1,0:T(8,128)(2,1)S(1)}, u32[]{:S(2)}, u32[]{:S(2)}) collective-permute-start(bf16[2,128,896]{2,1,0:T(8,128)(2,1)S(1)} %first_weights.1.refs_3_.refs_0_), channel_id=1, source_target_pairs={{0,3},{1,0},{2,1},{3,2},{4,7},{5,4},{6,5},{7,6},{8,11},{9,8},{10,9... | collective-permute-start | bytes 1376264 | tf_op jit(solution)/shard_map/one_down/ppermute | solution.py:339
  27.6 2.8 %update_rows.4 = (f32[2,512,896]{2,1,0:T(8,128)}, f32[2,512,896]{2,1,0:T(8,128)}, bf16[2,128,896]{2,1,0:T(8,128)(2,1)S(1)}) custom-call(f32[128,128]{1,0:T(8,128)S(1)} %bitcast.8, f32[2,512,896]{2,1,0:T(8,128)} %refs_0_.9, bf16[2,512,896]{2,1,0:T(8,128)(2,1)} %refs_1_.9, f32[2,512,896]{2,1,0:T(8,128)} %refs_2_.9, ...), custom_call_target="tpu_custom_call" | custom-call | flops 4587520 | bytes 4587520 | tf_op jit(solution)/shard_map/update_rows/pallas_call | solution.py:180
  30.4 2.8 %update_rows.5 = (f32[2,512,896]{2,1,0:T(8,128)}, f32[2,512,896]{2,1,0:T(8,128)}, bf16[2,128,896]{2,1,0:T(8,128)(2,1)S(1)}) custom-call(f32[128,128]{1,0:T(8,128)S(1)} %bitcast.9, f32[2,512,896]{2,1,0:T(8,128)} %refs_0_.9, bf16[2,512,896]{2,1,0:T(8,128)(2,1)} %refs_1_.9, f32[2,512,896]{2,1,0:T(8,128)} %refs_2_.9, ...), custom_call_target="tpu_custom_call", output_to_operand_aliasing={{0}: (4, {}), {1}: (5, {})} | custom-call | flops 4587520 | bytes 4587520 | tf_op jit(solution)/shard_map/update_rows/pallas_call | solution.py:180
  33.2 4.5 %collective-permute-done.refs_0_.refs_4_ = bf16[2,128,896]{2,1,0:T(8,128)(2,1)S(1)} collective-permute-done((bf16[2,128,896]{2,1,0:T(8,128)(2,1)S(1)}, bf16[2,128,896]{2,1,0:T(8,128)(2,1)S(1)}, u32[]{:S(2)}, u32[]{:S(2)}) %collective-permute-start) | collective-permute-done | bytes 458784 | tf_op jit(solution)/shard_map/one_up/ppermute | solution.py:339
  37.9 2.7 %collective-permute-start.3 = (bf16[3,128,896]{2,1,0:T(8,128)(2,1)S(1)}, bf16[3,128,896]{2,1,0:T(8,128)(2,1)S(1)}, u32[]{:S(2)}, u32[]{:S(2)}) collective-permute-start(bf16[3,128,896]{2,1,0:T(8,128)(2,1)S(1)} %make_step.16), channel_id=1, source_target_pairs={{0,3},{1,0},{2,1},{3,2},{4,7},{5,4},{6,5},{7,6},{8,11},{9,8},{10,9... | collective-permute-start | bytes 2064392 | tf_op jit(solution)/shard_map/two_down/ppermute | solution.py:339
  40.6 0.1 collective-permute-start.4
  40.7 2.8 %update_rows.6 = (f32[2,512,896]{2,1,0:T(8,128)}, f32[2,512,896]{2,1,0:T(8,128)}, bf16[2,128,896]{2,1,0:T(8,128)(2,1)S(1)}) custom-call(f32[128,128]{1,0:T(8,128)S(1)} %bitcast.10, f32[2,512,896]{2,1,0:T(8,128)} %refs_0_.9, bf16[2,512,896]{2,1,0:T(8,128)(2,1)} %refs_1_.9, f32[2,512,896]{2,1,0:T(8,128)} %refs_2_.9, ...), custom_call_target="tpu_custom_call", output_to_operand_aliasing={{0}: (4, {}), {1}: (5, {})} | custom-call | flops 4587520 | bytes 4587520 | tf_op jit(solution)/shard_map/update_rows/pallas_call | solution.py:180
  43.5 7.2 %collective-permute-done.4.refs_2_.refs_1_.refs_5_ = bf16[2,128,896]{2,1,0:T(8,128)(2,1)S(1)} collective-permute-done((bf16[2,128,896]{2,1,0:T(8,128)(2,1)S(1)}, bf16[2,128,896]{2,1,0:T(8,128)(2,1)S(1)}, u32[]{:S(2)}, u32[]{:S(2)}) %collective-permute-start.4) | collective-permute-done | bytes 458784 | tf_op jit(solution)/shard_map/cross/ppermute | solution.py:339
  50.7 3.9 %collective-permute-done.2.refs_0_.refs_2_.refs_4_ = bf16[3,128,896]{2,1,0:T(8,128)(2,1)S(1)} collective-permute-done((bf16[3,128,896]{2,1,0:T(8,128)(2,1)S(1)}, bf16[3,128,896]{2,1,0:T(8,128)(2,1)S(1)}, u32[]{:S(2)}, u32[]{:S(2)}) %collective-permute-start.2) | collective-permute-done | bytes 688160 | tf_op jit(solution)/shard_map/two_up/ppermute | solution.py:339
  54.8 2.7 %collective-permute-start.5 = (bf16[3,128,896]{2,1,0:T(8,128)(2,1)S(1)}, bf16[3,128,896]{2,1,0:T(8,128)(2,1)S(1)}, u32[]{:S(2)}, u32[]{:S(2)}) collective-permute-start(bf16[3,128,896]{2,1,0:T(8,128)(2,1)S(1)} %make_step.19), channel_id=1, source_target_pairs={{0,3},{1,0},{2,1},{3,2},{4,7},{5,4},{6,5},{7,6},{8,11},{9,8},{10,9... | collective-permute-start | bytes 2064392 | tf_op jit(solution)/shard_map/three_down/ppermute | solution.py:339
  57.5 0.9 make_step.18
  58.6 2.8 %update_rows.7 = (f32[2,512,896]{2,1,0:T(8,128)}, f32[2,512,896]{2,1,0:T(8,128)}, bf16[2,128,896]{2,1,0:T(8,128)(2,1)S(1)}) custom-call(f32[128,128]{1,0:T(8,128)S(1)} %bitcast.11, f32[2,512,896]{2,1,0:T(8,128)} %refs_0_.9, bf16[2,512,896]{2,1,0:T(8,128)(2,1)} %refs_1_.9, f32[2,512,896]{2,1,0:T(8,128)} %refs_2_.9, ...), custom_call_target="tpu_custom_call", output_to_operand_aliasing={{0}: (4, {}), {1}: (5, {})} | custom-call | flops 4587520 | bytes 4587520 | tf_op jit(solution)/shard_map/update_rows/pallas_call | solution.py:180
  61.3 9.2 %collective-permute-done.6.refs_0_.refs_2_.refs_4_ = bf16[3,128,896]{2,1,0:T(8,128)(2,1)S(1)} collective-permute-done((bf16[3,128,896]{2,1,0:T(8,128)(2,1)S(1)}, bf16[3,128,896]{2,1,0:T(8,128)(2,1)S(1)}, u32[]{:S(2)}, u32[]{:S(2)}) %collective-permute-start.6) | collective-permute-done | bytes 688160 | tf_op jit(solution)/shard_map/three_up/ppermute | solution.py:339
  70.7 2.7 %collective-permute-start.8 = (bf16[3,128,896]{2,1,0:T(8,128)(2,1)S(1)}, bf16[3,128,896]{2,1,0:T(8,128)(2,1)S(1)}, u32[]{:S(2)}, u32[]{:S(2)}) collective-permute-start(bf16[3,128,896]{2,1,0:T(8,128)(2,1)S(1)} %make_step.21), channel_id=1, source_target_pairs={{0,3},{1,0},{2,1},{3,2},{4,7},{5,4},{6,5},{7,6},{8,11},{9,8},{10,9... | collective-permute-start | bytes 2064392 | tf_op jit(solution)/shard_map/four_down/ppermute | solution.py:339
  73.5 1.0 make_step.22
  74.4 3.9 %collective-permute-start.10 = (bf16[2,128,896]{2,1,0:T(8,128)(2,1)S(1)}, bf16[2,128,896]{2,1,0:T(8,128)(2,1)S(1)}, u32[]{:S(2)}, u32[]{:S(2)}) collective-permute-start(bf16[2,128,896]{2,1,0:T(8,128)(2,1)S(1)} %get-tuple-element.66), channel_id=1, source_target_pairs={{0,4},{4,0},{8,12},{12,8},{1,5},{5,1},{9,13},{13,9},{2,6},{6,2},{1... | collective-permute-start | bytes 1376264 | tf_op jit(solution)/shard_map/core_one/ppermute | solution.py:339
  78.4 1.3 %collective-permute-done.10.refs_4_.refs_1_ = bf16[2,128,896]{2,1,0:T(8,128)(2,1)S(1)} collective-permute-done((bf16[2,128,896]{2,1,0:T(8,128)(2,1)S(1)}, bf16[2,128,896]{2,1,0:T(8,128)(2,1)S(1)}, u32[]{:S(2)}, u32[]{:S(2)}) %collective-permute-start.10) | collective-permute-done | bytes 458784 | tf_op jit(solution)/shard_map/core_one/ppermute | solution.py:339
  79.7 0.7 collective-permute-done.11.refs_5_
  80.4 5.2 %collective-permute-done.7.refs_0_.refs_2_.refs_4_ = bf16[3,128,896]{2,1,0:T(8,128)(2,1)S(1)} collective-permute-done((bf16[3,128,896]{2,1,0:T(8,128)(2,1)S(1)}, bf16[3,128,896]{2,1,0:T(8,128)(2,1)S(1)}, u32[]{:S(2)}, u32[]{:S(2)}) %collective-permute-start.7) | collective-permute-done | bytes 688160 | tf_op jit(solution)/shard_map/four_up/ppermute | solution.py:339
  85.8 2.7 %collective-permute-start.14 = (bf16[3,128,896]{2,1,0:T(8,128)(2,1)S(1)}, bf16[3,128,896]{2,1,0:T(8,128)(2,1)S(1)}, u32[]{:S(2)}, u32[]{:S(2)}) collective-permute-start(bf16[3,128,896]{2,1,0:T(8,128)(2,1)S(1)} %make_step.25), channel_id=1, source_target_pairs={{0,3},{1,0},{2,1},{3,2},{4,7},{5,4},{6,5},{7,6},{8,11},{9,8},{10,9... | collective-permute-start | bytes 2064392 | tf_op jit(solution)/shard_map/five_down/ppermute | solution.py:339
  88.5 0.9 make_step.24
  89.5 4.8 %collective-permute-start.15 = (bf16[2,128,896]{2,1,0:T(8,128)(2,1)S(1)}, bf16[2,128,896]{2,1,0:T(8,128)(2,1)S(1)}, u32[]{:S(2)}, u32[]{:S(2)}) collective-permute-start(bf16[2,128,896]{2,1,0:T(8,128)(2,1)S(1)} %make_step.26), channel_id=1, source_target_pairs={{0,4},{4,0},{8,12},{12,8},{1,5},{5,1},{9,13},{13,9},{2,6},{6,2},{1... | collective-permute-start | bytes 1376264 | tf_op jit(solution)/shard_map/core_pass_one/ppermute | solution.py:339
  94.3 3.1 %collective-permute-done.16.refs_2_.refs_1_.refs_6_ = bf16[4,128,896]{2,1,0:T(8,128)(2,1)S(1)} collective-permute-done((bf16[4,128,896]{2,1,0:T(8,128)(2,1)S(1)}, bf16[4,128,896]{2,1,0:T(8,128)(2,1)S(1)}, u32[]{:S(2)}, u32[]{:S(2)}) %collective-permute-start.16) | collective-permute-done | bytes 917536 | tf_op jit(solution)/shard_map/chip_two/ppermute | solution.py:339
  97.3 4.9 %collective-permute-done.17.refs_3_.refs_2_ = bf16[1,128,896]{2,1,0:T(8,128)(2,1)S(1)} collective-permute-done((bf16[1,128,896]{2,1,0:T(8,128)(2,1)S(1)}, bf16[1,128,896]{2,1,0:T(8,128)(2,1)S(1)}, u32[]{:S(2)}, u32[]{:S(2)}) %collective-permute-start.17) | collective-permute-done | bytes 229408 | tf_op jit(solution)/shard_map/chip_three/ppermute | solution.py:339
  102.4 3.9 %collective-permute-start.25 = (bf16[4,128,896]{2,1,0:T(8,128)(2,1)S(1)}, bf16[4,128,896]{2,1,0:T(8,128)(2,1)S(1)}, u32[]{:S(2)}, u32[]{:S(2)}) collective-permute-start(bf16[4,128,896]{2,1,0:T(8,128)(2,1)S(1)} %get-tuple-element.80), channel_id=1, source_target_pairs={{0,4},{4,0},{8,12},{12,8},{1,5},{5,1},{9,13},{13,9},{2,6},{6,2},{1... | collective-permute-start | bytes 2752520 | tf_op jit(solution)/shard_map/core_join/ppermute | solution.py:339
  106.3 2.7 %collective-permute-start.19 = (bf16[1,128,896]{2,1,0:T(8,128)(2,1)S(1)}, bf16[1,128,896]{2,1,0:T(8,128)(2,1)S(1)}, u32[]{:S(2)}, u32[]{:S(2)}) collective-permute-start(bf16[1,128,896]{2,1,0:T(8,128)(2,1)S(1)} %get-tuple-element.73), channel_id=1, source_target_pairs={{0,3},{1,0},{2,1},{3,2},{4,7},{5,4},{6,5},{7,6},{8,11},{9,8},{10,9... | collective-permute-start | bytes 688136 | tf_op jit(solution)/shard_map/last_down/ppermute | solution.py:339
  109.0 2.3 %collective-permute-start.12 = (bf16[2,128,896]{2,1,0:T(8,128)(2,1)S(1)}, bf16[2,128,896]{2,1,0:T(8,128)(2,1)S(1)}, u32[]{:S(2)}, u32[]{:S(2)}) collective-permute-start(bf16[2,128,896]{2,1,0:T(8,128)(2,1)S(1)} %get-tuple-element.68), channel_id=1, source_target_pairs={{0,12},{4,8},{8,4},{12,0},{1,13},{5,9},{9,5},{13,1},{2,14},{6,10},... | collective-permute-start | bytes 1376264 | tf_op jit(solution)/shard_map/both_three/ppermute | solution.py:339
  111.3 2.7 %quantize_rows.4 = (bf16[1,1,2,2048,896]{4,3,2,1,0:T(8,128)(2,1)}, f32[1,1,2,16,7]{4,3,2,1,0:T(8,128)S(1)}) custom-call(bf16[2,128,896]{2,1,0:T(8,128)(2,1)S(1)} %get-tuple-element.59.refs_5_.refs_0_, bf16[2,128,896]{2,1,0:T(8,128)(2,1)S(1)} %collective-permute-done.10.refs_4_.refs_1_, ...), custom_call_target="tpu_custom_call" | custom-call | flops 8028160 | bytes 6422528 | tf_op jit(solution)/shard_map/quantize_rows/pallas_call | solution.py:305
  114.0 0.4 collective-permute-done.18.refs_6_
  114.4 0.9 make_step.29
  115.3 1.3 %collective-permute-start.21 = (bf16[1,128,896]{2,1,0:T(8,128)(2,1)S(1)}, bf16[1,128,896]{2,1,0:T(8,128)(2,1)S(1)}, u32[]{:S(2)}, u32[]{:S(2)}) collective-permute-start(bf16[1,128,896]{2,1,0:T(8,128)(2,1)S(1)} %get-tuple-element.76), channel_id=1, source_target_pairs={{0,4},{4,0},{8,12},{12,8},{1,5},{5,1},{9,13},{13,9},{2,6},{6,2},{1... | collective-permute-start | bytes 688136 | tf_op jit(solution)/shard_map/core_last/ppermute | solution.py:339
  116.7 0.4 collective-permute-start.23
  117.2 2.4 %quantize_rows.5 = (bf16[1,1,2,2048,896]{4,3,2,1,0:T(8,128)(2,1)}, f32[1,1,2,16,7]{4,3,2,1,0:T(8,128)S(1)}) custom-call(bf16[2,128,896]{2,1,0:T(8,128)(2,1)S(1)} %get-tuple-element.69.refs_1_.refs_0_, bf16[4,128,896]{2,1,0:T(8,128)(2,1)S(1)} %collective-permute-done.25.refs_1_, ...), custom_call_target="tpu_custom_call", output_to_operand_aliasing={{0}: (6, {})} | custom-call | flops 6881280 | bytes 5505024 | tf_op jit(solution)/shard_map/quantize_rows/pallas_call | solution.py:305
  119.6 1.2 quantize_rows.6
  120.8 2.6 %collective-permute-done.12.refs_0_ = bf16[2,128,896]{2,1,0:T(8,128)(2,1)S(1)} collective-permute-done((bf16[2,128,896]{2,1,0:T(8,128)(2,1)S(1)}, bf16[2,128,896]{2,1,0:T(8,128)(2,1)S(1)}, u32[]{:S(2)}, u32[]{:S(2)}) %collective-permute-start.12) | collective-permute-done | bytes 458784 | tf_op jit(solution)/shard_map/both_three/ppermute | solution.py:339
  123.5 1.0 quantize_rows.7
  124.5 0.7 copy.27
  (47 shorter events, 1.7 us)
Async XLA Ops:
  0.6 1.5 %copy-start = (bf16[2,512,896]{2,1,0:T(8,128)(2,1)S(1)}, bf16[2,512,896]{2,1,0:T(8,128)(2,1)}, u32[]{:S(2)}) copy-start(bf16[2,512,896]{2,1,0:T(8,128)(2,1)} %refs_1_.9) | copy-start | bytes 5505028
  3.0 21.1 %all-to-all-start = ((f32[128,1,128]{2,1,0:T(1,128)}), f32[128,1,128]{2,1,0:T(1,128)S(1)}, u32[]{:S(2)}, u32[]{:S(2)}) async-start(f32[128,1,128]{2,1,0:T(1,128)} %bitcast.1), calls=%async_computation | async-start | bytes 131072 | tf_op jit(solution)/shard_map/all_to_all | solution.py:335
  24.9 12.8 %collective-permute-start = (bf16[2,128,896]{2,1,0:T(8,128)(2,1)S(1)}, bf16[2,128,896]{2,1,0:T(8,128)(2,1)S(1)}, u32[]{:S(2)}, u32[]{:S(2)}) collective-permute-start(bf16[2,128,896]{2,1,0:T(8,128)(2,1)S(1)} %first_weights.1.refs_3_.refs_0_), channel_id=1, source_target_pairs={{0,1},{1,2},{2,3},{3,0},{4,5},{5,6},{6,7},{7,4},{8,9},{9,10},{10,1... | collective-permute-start | bytes 1376264 | tf_op jit(solution)/shard_map/one_up/ppermute | solution.py:339
  25.5 12.3 %collective-permute-start.1 = (bf16[2,128,896]{2,1,0:T(8,128)(2,1)S(1)}, bf16[2,128,896]{2,1,0:T(8,128)(2,1)S(1)}, u32[]{:S(2)}, u32[]{:S(2)}) collective-permute-start(bf16[2,128,896]{2,1,0:T(8,128)(2,1)S(1)} %first_weights.1.refs_3_.refs_0_), channel_id=1, source_target_pairs={{0,3},{1,0},{2,1},{3,2},{4,7},{5,4},{6,5},{7,6},{8,11},{9,8},{10,9... | collective-permute-start | bytes 1376264 | tf_op jit(solution)/shard_map/one_down/ppermute | solution.py:339
  37.8 16.8 %collective-permute-start.2 = (bf16[3,128,896]{2,1,0:T(8,128)(2,1)S(1)}, bf16[3,128,896]{2,1,0:T(8,128)(2,1)S(1)}, u32[]{:S(2)}, u32[]{:S(2)}) collective-permute-start(bf16[3,128,896]{2,1,0:T(8,128)(2,1)S(1)} %make_step.15.refs_5_.refs_2_), channel_id=1, source_target_pairs={{0,1},{1,2},{2,3},{3,0},{4,5},{5,6},{6,7},{7,4},{8,9},{9,10},{10,1... | collective-permute-start | bytes 2064392 | tf_op jit(solution)/shard_map/two_up/ppermute | solution.py:339
  37.9 16.8 %collective-permute-start.3 = (bf16[3,128,896]{2,1,0:T(8,128)(2,1)S(1)}, bf16[3,128,896]{2,1,0:T(8,128)(2,1)S(1)}, u32[]{:S(2)}, u32[]{:S(2)}) collective-permute-start(bf16[3,128,896]{2,1,0:T(8,128)(2,1)S(1)} %make_step.16), channel_id=1, source_target_pairs={{0,3},{1,0},{2,1},{3,2},{4,7},{5,4},{6,5},{7,6},{8,11},{9,8},{10,9... | collective-permute-start | bytes 2064392 | tf_op jit(solution)/shard_map/two_down/ppermute | solution.py:339
  40.6 10.1 %collective-permute-start.4 = (bf16[2,128,896]{2,1,0:T(8,128)(2,1)S(1)}, bf16[2,128,896]{2,1,0:T(8,128)(2,1)S(1)}, u32[]{:S(2)}, u32[]{:S(2)}) collective-permute-start(bf16[2,128,896]{2,1,0:T(8,128)(2,1)S(1)} %get-tuple-element.55.refs_2_.refs_1_.refs_0_), channel_id=1, source_target_pairs={{0,8},{4,12},{8,0},{12,4},{1,9},{5,13},{9,1},{13,5},{2,10},{6,14},... | collective-permute-start | bytes 1376264 | tf_op jit(solution)/shard_map/cross/ppermute | solution.py:339
  54.6 15.9 %collective-permute-start.6 = (bf16[3,128,896]{2,1,0:T(8,128)(2,1)S(1)}, bf16[3,128,896]{2,1,0:T(8,128)(2,1)S(1)}, u32[]{:S(2)}, u32[]{:S(2)}) collective-permute-start(bf16[3,128,896]{2,1,0:T(8,128)(2,1)S(1)} %make_step.17.refs_6_.refs_2_), channel_id=1, source_target_pairs={{0,1},{1,2},{2,3},{3,0},{4,5},{5,6},{6,7},{7,4},{8,9},{9,10},{10,1... | collective-permute-start | bytes 2064392 | tf_op jit(solution)/shard_map/three_up/ppermute | solution.py:339
  54.8 15.9 %collective-permute-start.5 = (bf16[3,128,896]{2,1,0:T(8,128)(2,1)S(1)}, bf16[3,128,896]{2,1,0:T(8,128)(2,1)S(1)}, u32[]{:S(2)}, u32[]{:S(2)}) collective-permute-start(bf16[3,128,896]{2,1,0:T(8,128)(2,1)S(1)} %make_step.19), channel_id=1, source_target_pairs={{0,3},{1,0},{2,1},{3,2},{4,7},{5,4},{6,5},{7,6},{8,11},{9,8},{10,9... | collective-permute-start | bytes 2064392 | tf_op jit(solution)/shard_map/three_down/ppermute | solution.py:339
  58.5 19.9 %collective-permute-start.9 = (bf16[4,128,896]{2,1,0:T(8,128)(2,1)S(1)}, bf16[4,128,896]{2,1,0:T(8,128)(2,1)S(1)}, u32[]{:S(2)}, u32[]{:S(2)}) collective-permute-start(bf16[4,128,896]{2,1,0:T(8,128)(2,1)S(1)} %get-tuple-element.65), channel_id=1, source_target_pairs={{0,8},{4,12},{8,0},{12,4},{1,9},{5,13},{9,1},{13,5},{2,10},{6,14},... | collective-permute-start | bytes 2752520 | tf_op jit(solution)/shard_map/chip_one/ppermute | solution.py:339
  70.6 15.0 %collective-permute-start.7 = (bf16[3,128,896]{2,1,0:T(8,128)(2,1)S(1)}, bf16[3,128,896]{2,1,0:T(8,128)(2,1)S(1)}, u32[]{:S(2)}, u32[]{:S(2)}) collective-permute-start(bf16[3,128,896]{2,1,0:T(8,128)(2,1)S(1)} %make_step.20.refs_2_.refs_7_), channel_id=1, source_target_pairs={{0,1},{1,2},{2,3},{3,0},{4,5},{5,6},{6,7},{7,4},{8,9},{9,10},{10,1... | collective-permute-start | bytes 2064392 | tf_op jit(solution)/shard_map/four_up/ppermute | solution.py:339
  70.7 15.0 %collective-permute-start.8 = (bf16[3,128,896]{2,1,0:T(8,128)(2,1)S(1)}, bf16[3,128,896]{2,1,0:T(8,128)(2,1)S(1)}, u32[]{:S(2)}, u32[]{:S(2)}) collective-permute-start(bf16[3,128,896]{2,1,0:T(8,128)(2,1)S(1)} %make_step.21), channel_id=1, source_target_pairs={{0,3},{1,0},{2,1},{3,2},{4,7},{5,4},{6,5},{7,6},{8,11},{9,8},{10,9... | collective-permute-start | bytes 2064392 | tf_op jit(solution)/shard_map/four_down/ppermute | solution.py:339
  74.4 5.3 %collective-permute-start.10 = (bf16[2,128,896]{2,1,0:T(8,128)(2,1)S(1)}, bf16[2,128,896]{2,1,0:T(8,128)(2,1)S(1)}, u32[]{:S(2)}, u32[]{:S(2)}) collective-permute-start(bf16[2,128,896]{2,1,0:T(8,128)(2,1)S(1)} %get-tuple-element.66), channel_id=1, source_target_pairs={{0,4},{4,0},{8,12},{12,8},{1,5},{5,1},{9,13},{13,9},{2,6},{6,2},{1... | collective-permute-start | bytes 1376264 | tf_op jit(solution)/shard_map/core_one/ppermute | solution.py:339
  78.3 2.1 %collective-permute-start.11 = (bf16[2,128,896]{2,1,0:T(8,128)(2,1)S(1)}, bf16[2,128,896]{2,1,0:T(8,128)(2,1)S(1)}, u32[]{:S(2)}, u32[]{:S(2)}) collective-permute-start(bf16[2,128,896]{2,1,0:T(8,128)(2,1)S(1)} %get-tuple-element.67), channel_id=1, source_target_pairs={{0,4},{4,0},{8,12},{12,8},{1,5},{5,1},{9,13},{13,9},{2,6},{6,2},{1... | collective-permute-start | bytes 1376264 | tf_op jit(solution)/shard_map/core_two/ppermute | solution.py:339
  78.4 18.9 %collective-permute-start.16 = (bf16[4,128,896]{2,1,0:T(8,128)(2,1)S(1)}, bf16[4,128,896]{2,1,0:T(8,128)(2,1)S(1)}, u32[]{:S(2)}, u32[]{:S(2)}) collective-permute-start(bf16[4,128,896]{2,1,0:T(8,128)(2,1)S(1)} %get-tuple-element.70), channel_id=1, source_target_pairs={{0,8},{4,12},{8,0},{12,4},{1,9},{5,13},{9,1},{13,5},{2,10},{6,14},... | collective-permute-start | bytes 2752520 | tf_op jit(solution)/shard_map/chip_two/ppermute | solution.py:339
  85.6 16.6 %collective-permute-start.13 = (bf16[3,128,896]{2,1,0:T(8,128)(2,1)S(1)}, bf16[3,128,896]{2,1,0:T(8,128)(2,1)S(1)}, u32[]{:S(2)}, u32[]{:S(2)}) collective-permute-start(bf16[3,128,896]{2,1,0:T(8,128)(2,1)S(1)} %make_step.23.refs_6_.refs_2_), channel_id=1, source_target_pairs={{0,1},{1,2},{2,3},{3,0},{4,5},{5,6},{6,7},{7,4},{8,9},{9,10},{10,1... | collective-permute-start | bytes 2064392 | tf_op jit(solution)/shard_map/five_up/ppermute | solution.py:339
  85.8 16.5 %collective-permute-start.14 = (bf16[3,128,896]{2,1,0:T(8,128)(2,1)S(1)}, bf16[3,128,896]{2,1,0:T(8,128)(2,1)S(1)}, u32[]{:S(2)}, u32[]{:S(2)}) collective-permute-start(bf16[3,128,896]{2,1,0:T(8,128)(2,1)S(1)} %make_step.25), channel_id=1, source_target_pairs={{0,3},{1,0},{2,1},{3,2},{4,7},{5,4},{6,5},{7,6},{8,11},{9,8},{10,9... | collective-permute-start | bytes 2064392 | tf_op jit(solution)/shard_map/five_down/ppermute | solution.py:339
  89.5 12.8 %collective-permute-start.15 = (bf16[2,128,896]{2,1,0:T(8,128)(2,1)S(1)}, bf16[2,128,896]{2,1,0:T(8,128)(2,1)S(1)}, u32[]{:S(2)}, u32[]{:S(2)}) collective-permute-start(bf16[2,128,896]{2,1,0:T(8,128)(2,1)S(1)} %make_step.26), channel_id=1, source_target_pairs={{0,4},{4,0},{8,12},{12,8},{1,5},{5,1},{9,13},{13,9},{2,6},{6,2},{1... | collective-permute-start | bytes 1376264 | tf_op jit(solution)/shard_map/core_pass_one/ppermute | solution.py:339
  94.3 8.0 %collective-permute-start.17 = (bf16[1,128,896]{2,1,0:T(8,128)(2,1)S(1)}, bf16[1,128,896]{2,1,0:T(8,128)(2,1)S(1)}, u32[]{:S(2)}, u32[]{:S(2)}) collective-permute-start(bf16[1,128,896]{2,1,0:T(8,128)(2,1)S(1)} %get-tuple-element.71), channel_id=1, source_target_pairs={{0,8},{4,12},{8,0},{12,4},{1,9},{5,13},{9,1},{13,5},{2,10},{6,14},... | collective-permute-start | bytes 688136 | tf_op jit(solution)/shard_map/chip_three/ppermute | solution.py:339
  102.4 14.7 %collective-permute-start.25 = (bf16[4,128,896]{2,1,0:T(8,128)(2,1)S(1)}, bf16[4,128,896]{2,1,0:T(8,128)(2,1)S(1)}, u32[]{:S(2)}, u32[]{:S(2)}) collective-permute-start(bf16[4,128,896]{2,1,0:T(8,128)(2,1)S(1)} %get-tuple-element.80), channel_id=1, source_target_pairs={{0,4},{4,0},{8,12},{12,8},{1,5},{5,1},{9,13},{13,9},{2,6},{6,2},{1... | collective-permute-start | bytes 2752520 | tf_op jit(solution)/shard_map/core_join/ppermute | solution.py:339
  106.3 7.7 %collective-permute-start.20 = (bf16[1,128,896]{2,1,0:T(8,128)(2,1)S(1)}, bf16[1,128,896]{2,1,0:T(8,128)(2,1)S(1)}, u32[]{:S(2)}, u32[]{:S(2)}) collective-permute-start(bf16[1,128,896]{2,1,0:T(8,128)(2,1)S(1)} %get-tuple-element.75), channel_id=1, source_target_pairs={{0,8},{4,12},{8,0},{12,4},{1,9},{5,13},{9,1},{13,5},{2,10},{6,14},... | collective-permute-start | bytes 688136 | tf_op jit(solution)/shard_map/chip_three_more/ppermute | solution.py:339
  106.3 8.0 %collective-permute-start.18 = (bf16[1,128,896]{2,1,0:T(8,128)(2,1)S(1)}, bf16[1,128,896]{2,1,0:T(8,128)(2,1)S(1)}, u32[]{:S(2)}, u32[]{:S(2)}) collective-permute-start(bf16[1,128,896]{2,1,0:T(8,128)(2,1)S(1)} %make_step.27.refs_3_), channel_id=1, source_target_pairs={{0,1},{1,2},{2,3},{3,0},{4,5},{5,6},{6,7},{7,4},{8,9},{9,10},{10,1... | collective-permute-start | bytes 688136 | tf_op jit(solution)/shard_map/last_up/ppermute | solution.py:339
  106.3 8.0 %collective-permute-start.19 = (bf16[1,128,896]{2,1,0:T(8,128)(2,1)S(1)}, bf16[1,128,896]{2,1,0:T(8,128)(2,1)S(1)}, u32[]{:S(2)}, u32[]{:S(2)}) collective-permute-start(bf16[1,128,896]{2,1,0:T(8,128)(2,1)S(1)} %get-tuple-element.73), channel_id=1, source_target_pairs={{0,3},{1,0},{2,1},{3,2},{4,7},{5,4},{6,5},{7,6},{8,11},{9,8},{10,9... | collective-permute-start | bytes 688136 | tf_op jit(solution)/shard_map/last_down/ppermute | solution.py:339
  109.0 14.5 %collective-permute-start.12 = (bf16[2,128,896]{2,1,0:T(8,128)(2,1)S(1)}, bf16[2,128,896]{2,1,0:T(8,128)(2,1)S(1)}, u32[]{:S(2)}, u32[]{:S(2)}) collective-permute-start(bf16[2,128,896]{2,1,0:T(8,128)(2,1)S(1)} %get-tuple-element.68), channel_id=1, source_target_pairs={{0,12},{4,8},{8,4},{12,0},{1,13},{5,9},{9,5},{13,1},{2,14},{6,10},... | collective-permute-start | bytes 1376264 | tf_op jit(solution)/shard_map/both_three/ppermute | solution.py:339
  115.3 4.3 %collective-permute-start.21 = (bf16[1,128,896]{2,1,0:T(8,128)(2,1)S(1)}, bf16[1,128,896]{2,1,0:T(8,128)(2,1)S(1)}, u32[]{:S(2)}, u32[]{:S(2)}) collective-permute-start(bf16[1,128,896]{2,1,0:T(8,128)(2,1)S(1)} %get-tuple-element.76), channel_id=1, source_target_pairs={{0,4},{4,0},{8,12},{12,8},{1,5},{5,1},{9,13},{13,9},{2,6},{6,2},{1... | collective-permute-start | bytes 688136 | tf_op jit(solution)/shard_map/core_last/ppermute | solution.py:339
  116.6 3.0 %collective-permute-start.22 = (bf16[1,128,896]{2,1,0:T(8,128)(2,1)S(1)}, bf16[1,128,896]{2,1,0:T(8,128)(2,1)S(1)}, u32[]{:S(2)}, u32[]{:S(2)}) collective-permute-start(bf16[1,128,896]{2,1,0:T(8,128)(2,1)S(1)} %get-tuple-element.77), channel_id=1, source_target_pairs={{0,4},{4,0},{8,12},{12,8},{1,5},{5,1},{9,13},{13,9},{2,6},{6,2},{1... | collective-permute-start | bytes 688136 | tf_op jit(solution)/shard_map/core_last/ppermute | solution.py:339
  116.7 2.9 %collective-permute-start.23 = (bf16[1,128,896]{2,1,0:T(8,128)(2,1)S(1)}, bf16[1,128,896]{2,1,0:T(8,128)(2,1)S(1)}, u32[]{:S(2)}, u32[]{:S(2)}) collective-permute-start(bf16[1,128,896]{2,1,0:T(8,128)(2,1)S(1)} %get-tuple-element.78), channel_id=1, source_target_pairs={{0,4},{4,0},{8,12},{12,8},{1,5},{5,1},{9,13},{13,9},{2,6},{6,2},{1... | collective-permute-start | bytes 688136 | tf_op jit(solution)/shard_map/core_last/ppermute | solution.py:339
  117.1 2.5 %collective-permute-start.24 = (bf16[1,128,896]{2,1,0:T(8,128)(2,1)S(1)}, bf16[1,128,896]{2,1,0:T(8,128)(2,1)S(1)}, u32[]{:S(2)}, u32[]{:S(2)}) collective-permute-start(bf16[1,128,896]{2,1,0:T(8,128)(2,1)S(1)} %get-tuple-element.79), channel_id=1, source_target_pairs={{0,4},{4,0},{8,12},{12,8},{1,5},{5,1},{9,13},{13,9},{2,6},{6,2},{1... | collective-permute-start | bytes 688136 | tf_op jit(solution)/shard_map/core_last/ppermute | solution.py:339

commit v4 on v3

--- a/solution.py
+++ b/solution.py
@@ -371,9 +371,13 @@
     new, e = update(0, (), (w1,))
     new, w2 = update(2, new)
 
-    (a,) = step("turn_one_up", [[(below1, 0)] + both(w2)], (e,))
-    (b,) = step("turn_one_down", [[(above1, 1)] + both(w2)], (a,))
-    below2, above2 = up(a, "two"), down(b, "two")
+    (a,) = step("turn_one_up", [[(below1, 0)]], (e,))
+    (b,) = step("turn_one_down", [[(above1, 1)]], (a,))
+    far_low1, far_high1 = up(a, "on"), down(b, "on")
+    p, q = step("next_two", [[(w2, 0)], [(w2, 1)]], (b,))
+    below20, above20 = up(p, "two_low"), down(p, "two_low")
+    below21, above21 = up(q, "two_high"), down(q, "two_high")
+    above2, below2 = [(above20, 0), (above21, 0)], [(below20, 0), (below21, 0)]
     f = flip(e, 2, "cross")
     new, w3 = update(3, new, (a,))
 
@@ -381,27 +385,27 @@
         outs = [sum((slots_of((j,), *ring) for j in group), []) for group in flips]
         return step("pick_" + name, outs + [slots_of((0,), *ring)], after)
 
-    (a,) = step("turn_two_up", [[(below2, 1)] + both(w3)], (f,))
-    (b,) = step("turn_two_down", [[(above2, 2)] + both(w3)], (a,))
+    ring1 = (both(w1), both(above1), [(far_low1, 0), (far_high1, 0)], both(below1))
+    x, o1, s1 = pick("one", ring1, ((2, 3), (1,)), (q,))
+    y1 = flip(x, 2, "chip_one")
+    (a,) = step("turn_two_up", [[below2[0]] + both(w3)], (f, s1))
+    (b,) = step("turn_two_down", [[above2[1]] + both(w3)], (a,))
     below3, above3 = up(a, "three"), down(b, "three")
-    ring1 = (both(w1), both(above1), [(below2, 0), (above2, 0)], both(below1))
-    x, o1, s1 = pick("one", ring1, ((2, 3), (1,)), (a,))
-    y1 = flip(x, 2, "chip_one")
     new, again = update(1, new, (s1,))
 
     (a,) = step("turn_three_up", [[(below3, 1)] + both(e)], (again,))
     (b,) = step("turn_three_down", [[(above3, 2)] + both(e)], (a,))
     below4, above4 = up(a, "four"), down(b, "four")
-    ring2 = (both(w2), both(above2, 1), [(below3, 0), (above3, 0)], both(below2, 1))
+    ring2 = (both(w2), above2, [(below3, 0), (above3, 0)], below2)
     x, o1, o2, s2 = step(
         "pick_two",
         [slots_of((2, 3), *ring2), both(o1), slots_of((1,), *ring2), slots_of((0,), *ring2)],
         (a,),
     )
     y2 = flip(x, 2, "chip_two")
-    z1, z2 = flip(o1, 1, "core_one"), flip(o2, 1, "core_two")
-
-    (a,) = step("turn_four_up", [[(below4, 1)] + both(f)], (s2, y1, z1, z2))
+    z1 = flip(o1, 1, "core_one")
+
+    (a,) = step("turn_four_up", [[(below4, 1)] + both(f)], (s2, y1, z1))
     (b,) = step("turn_four_down", [[(above4, 2)] + both(f)], (a,))
     below5, above5 = up(a, "five"), down(b, "five")
     ring3 = (both(w3), both(above3, 1), [(below4, 0), (above4, 0)], both(below3, 1))
@@ -416,12 +420,12 @@
     t1 = flip(c, 1, "core_pass_one")
 
     (a,) = step("turn_five_up", [[(below5, 1)]], (t1, y2, xa))
-    b, c = step("turn_five_down", [[(above5, 2)], both(y2, 2) + both(o3)], (a,))
+    b, c = step("turn_five_down", [[(above5, 2)], both(y2, 2) + both(o3) + both(o2)], (a,))
     far_low_f, far_high_f = up(a, "last"), down(b, "last")
     z = flip(c, 1, "core_join")
     xb, xc = flip(xb, 2, "chip_three_more"), flip(xc, 3, "both_three")
-    places = place(1, (0, 0, 0), (1, 0, 1), (2, 0, 2), (3, 0, 3)) + place(2, (4, 0, 0), (5, 0, 1), (6, 0, 2))
-    result = quantize([s1, z1, y1, t1, s2, z2, y2], places, shape, ())
+    places = place(1, (0, 0, 0), (1, 0, 1), (2, 0, 2), (3, 0, 3)) + place(2, (4, 0, 0), (5, 0, 2))
+    result = quantize([s1, z1, y1, t1, s2, y2], places, shape, ())
 
     ring_e = (both(e), both(above4, 1), [(below5, 0), (above5, 0)], both(below4, 1))
     ring_f = (both(f), both(above5, 1), [(far_low_f, 0), (far_high_f, 0)], both(below5, 1))
@@ -430,7 +434,7 @@
     *pieces, se, sf = step("pick_last", outs, (result[1], xb))
     pieces = [flip(piece, 1, "core_last") for piece in pieces]
     places = place(3, (0, 0, 0), (1, 2, 1)) + [(2, 0, 2, 0, 3), (3, 0, 2, 1, 3)]
-    places += place(0, (4, 0, 0), (5, 0, 2)) + place(2, (1, 0, 3))
+    places += place(0, (4, 0, 0), (5, 0, 2)) + place(2, (1, 4, 1), (1, 0, 3))
     result = quantize([s3, z, xa, xb, se, sf], places, shape, tuple(result))
     places = [(0, 0, 1, 0, 0), (1, 0, 1, 1, 0), (2, 0, 3, 0, 0), (3, 0, 3, 1, 0)]
     result = quantize(pieces, places, shape, tuple(result))

time: 125 us -> 125 us (level)
  waiting for transfers between devices: 48.3 us -> 44.8 us
  starting transfers between devices: 45.1 us -> 47.9 us
    ppermute x26 -> x29, waiting for transfers between devices: 42.9 us -> 39.5 us  [send(): return lax.ppermute(value, axis, order)]
    ppermute x26 -> x29, starting transfers between devices: 33.6 us -> 36.4 us  [send(): return lax.ppermute(value, axis, order)]
    pallas_call x15 -> x16, Pallas kernels: 4.31 us -> 4.41 us  [make_step(): pl.pallas_call(functools.partial(step_kernel, moves, len(arrays)), in_spe...]
  transfers between devices with their start and end apart: 27 -> 30, of which waited for: 12 -> 12; matrix products, arithmetic and copies ran while one was open for 2% -> 2% of each run, Pallas kernels for 19% -> 19%
where the time goes in v4:
time: 125 us; the launch traced here: 124 us
  starting transfers between devices  47.9 us (38%)
  waiting for transfers between devices  44.8 us (36%)
  Pallas kernels  26 us (21%)
  local copies, waits for them, and re-layouts  3.09 us (2%)
  other arithmetic  1.67 us (1%)
    ppermute x29, waiting for transfers between devices, send(): return lax.ppermute(value, axis, order)  39.5 us
    ppermute x29, starting transfers between devices, send(): return lax.ppermute(value, axis, order)  36.4 us
    all_to_all x1, starting transfers between devices, body(): total = lax.all_to_all(part, devices, 0, 0, tiled=True)  11.5 us
    pallas_call x4, Pallas kernels, update_rows(): pl.pallas_call(functools.partial(update_kernel, count, chunk), in_specs=[...  11.1 us
    pallas_call x4, Pallas kernels, quantize(): pl.pallas_call(functools.partial(quantize_kernel, tuple(places)), in_spec...  7.23 us
    all_to_all x1, waiting for transfers between devices, body(): total = lax.all_to_all(part, devices, 0, 0, tiled=True)  5.33 us
    pallas_call x16, Pallas kernels, make_step(): pl.pallas_call(functools.partial(step_kernel, moves, len(arrays)), in_spe...  4.41 us
  transfers between devices with their start and end apart: 30, of which 12 were waited for; matrix products, arithmetic and copies ran while one was open for 2% of the time, Pallas kernels for 19%

profile of v4, /device:TPU:1, one launch (start us, length us, event | category | flops | bytes accessed | tf_op | source)
XLA Modules:
  0.0 124.4 jit_solution(5226579663273248450)
XLA Ops:
  0.6 1.5 %copy-done = bf16[2,512,896]{2,1,0:T(8,128)(2,1)S(1)} copy-done((bf16[2,512,896]{2,1,0:T(8,128)(2,1)S(1)}, bf16[2,512,896]{2,1,0:T(8,128)(2,1)}, u32[]{:S(2)}) %copy-start) | copy-done | bytes 1835032
  2.1 0.9 local_squares.1.refs_3_
  3.0 11.5 %all-to-all-start = ((f32[128,1,128]{2,1,0:T(1,128)}), f32[128,1,128]{2,1,0:T(1,128)S(1)}, u32[]{:S(2)}, u32[]{:S(2)}) async-start(f32[128,1,128]{2,1,0:T(1,128)} %bitcast.1), calls=%async_computation | async-start | bytes 131072 | tf_op jit(solution)/shard_map/all_to_all | solution.py:335
  14.5 0.7 fusion
  15.2 0.7 reduce_window_sum.11
  16.5 0.6 gather_fusion
  17.1 1.6 %load_rows.1 = (f32[2,128,896]{2,1,0:T(8,128)S(1)}, bf16[2,128,896]{2,1,0:T(8,128)(2,1)S(1)}, f32[2,128,896]{2,1,0:T(8,128)S(1)}) custom-call(f32[2,512,896]{2,1,0:T(8,128)} %refs_0_.9, bf16[2,512,896]{2,1,0:T(8,128)(2,1)} %refs_1_.9, f32[2,512,896]{2,1,0:T(8,128)} %refs_2_.9, f32[128,128]{1,0:T(8,128)} %local_squares.1.refs_3_, ...), custom_call_target="tpu_custom_call" | custom-call | bytes 5505024 | tf_op jit(solution)/shard_map/load_rows/pallas_call | solution.py:82
  18.8 5.3 %all-to-all-done = f32[128,1,128]{2,1,0:T(1,128)S(1)} async-done(((f32[128,1,128]{2,1,0:T(1,128)}), f32[128,1,128]{2,1,0:T(1,128)S(1)}, u32[]{:S(2)}, u32[]{:S(2)}) %all-to-all-start) | async-done | bytes 65568 | tf_op jit(solution)/shard_map/all_to_all | solution.py:335
  24.1 0.8 first_weights.1.refs_3_.refs_0_
  24.9 0.6 collective-permute-start
  25.5 2.1 %collective-permute-start.1 = (bf16[2,128,896]{2,1,0:T(8,128)(2,1)S(1)}, bf16[2,128,896]{2,1,0:T(8,128)(2,1)S(1)}, u32[]{:S(2)}, u32[]{:S(2)}) collective-permute-start(bf16[2,128,896]{2,1,0:T(8,128)(2,1)S(1)} %first_weights.1.refs_3_.refs_0_), channel_id=1, source_target_pairs={{0,3},{1,0},{2,1},{3,2},{4,7},{5,4},{6,5},{7,6},{8,11},{9,8},{10,9... | collective-permute-start | bytes 1376264 | tf_op jit(solution)/shard_map/one_down/ppermute | solution.py:339
  27.6 2.8 %update_rows.4 = (f32[2,512,896]{2,1,0:T(8,128)}, f32[2,512,896]{2,1,0:T(8,128)}, bf16[2,128,896]{2,1,0:T(8,128)(2,1)S(1)}) custom-call(f32[128,128]{1,0:T(8,128)S(1)} %bitcast.8, f32[2,512,896]{2,1,0:T(8,128)} %refs_0_.9, bf16[2,512,896]{2,1,0:T(8,128)(2,1)} %refs_1_.9, f32[2,512,896]{2,1,0:T(8,128)} %refs_2_.9, ...), custom_call_target="tpu_custom_call" | custom-call | flops 4587520 | bytes 4587520 | tf_op jit(solution)/shard_map/update_rows/pallas_call | solution.py:180
  30.7 2.8 %update_rows.5 = (f32[2,512,896]{2,1,0:T(8,128)}, f32[2,512,896]{2,1,0:T(8,128)}, bf16[2,128,896]{2,1,0:T(8,128)(2,1)S(1)}) custom-call(f32[128,128]{1,0:T(8,128)S(1)} %bitcast.9, f32[2,512,896]{2,1,0:T(8,128)} %refs_0_.9, bf16[2,512,896]{2,1,0:T(8,128)(2,1)} %refs_1_.9, f32[2,512,896]{2,1,0:T(8,128)} %refs_2_.9, ...), custom_call_target="tpu_custom_call", output_to_operand_aliasing={{0}: (4, {}), {1}: (5, {})} | custom-call | flops 4587520 | bytes 4587520 | tf_op jit(solution)/shard_map/update_rows/pallas_call | solution.py:180
  33.5 4.2 %collective-permute-done.refs_0_.refs_4_ = bf16[2,128,896]{2,1,0:T(8,128)(2,1)S(1)} collective-permute-done((bf16[2,128,896]{2,1,0:T(8,128)(2,1)S(1)}, bf16[2,128,896]{2,1,0:T(8,128)(2,1)S(1)}, u32[]{:S(2)}, u32[]{:S(2)}) %collective-permute-start) | collective-permute-done | bytes 458784 | tf_op jit(solution)/shard_map/one_up/ppermute | solution.py:339
  37.9 2.7 %collective-permute-start.3 = (bf16[1,128,896]{2,1,0:T(8,128)(2,1)S(1)}, bf16[1,128,896]{2,1,0:T(8,128)(2,1)S(1)}, u32[]{:S(2)}, u32[]{:S(2)}) collective-permute-start(bf16[1,128,896]{2,1,0:T(8,128)(2,1)S(1)} %make_step.17.refs_1_), channel_id=1, source_target_pairs={{0,3},{1,0},{2,1},{3,2},{4,7},{5,4},{6,5},{7,6},{8,11},{9,8},{10,9... | collective-permute-start | bytes 688136 | tf_op jit(solution)/shard_map/on_down/ppermute | solution.py:339
  40.7 2.7 %collective-permute-start.4 = (bf16[1,128,896]{2,1,0:T(8,128)(2,1)S(1)}, bf16[1,128,896]{2,1,0:T(8,128)(2,1)S(1)}, u32[]{:S(2)}, u32[]{:S(2)}) collective-permute-start(bf16[1,128,896]{2,1,0:T(8,128)(2,1)S(1)} %get-tuple-element.60.refs_6_), channel_id=1, source_target_pairs={{0,3},{1,0},{2,1},{3,2},{4,7},{5,4},{6,5},{7,6},{8,11},{9,8},{10,9... | collective-permute-start | bytes 688136 | tf_op jit(solution)/shard_map/two_high_down/ppermute | solution.py:339
  43.4 2.8 %update_rows.6 = (f32[2,512,896]{2,1,0:T(8,128)}, f32[2,512,896]{2,1,0:T(8,128)}, bf16[2,128,896]{2,1,0:T(8,128)(2,1)S(1)}) custom-call(f32[128,128]{1,0:T(8,128)S(1)} %bitcast.10, f32[2,512,896]{2,1,0:T(8,128)} %refs_0_.9, bf16[2,512,896]{2,1,0:T(8,128)(2,1)} %refs_1_.9, f32[2,512,896]{2,1,0:T(8,128)} %refs_2_.9, ...), custom_call_target="tpu_custom_call", output_to_operand_aliasing={{0}: (4, {}), {1}: (5, {})} | custom-call | flops 4587520 | bytes 4587520 | tf_op jit(solution)/shard_map/update_rows/pallas_call | solution.py:180
  46.2 0.9 make_step.19
  47.1 2.5 %collective-permute-done.5.refs_0_.refs_5_ = bf16[1,128,896]{2,1,0:T(8,128)(2,1)S(1)} collective-permute-done((bf16[1,128,896]{2,1,0:T(8,128)(2,1)S(1)}, bf16[1,128,896]{2,1,0:T(8,128)(2,1)S(1)}, u32[]{:S(2)}, u32[]{:S(2)}) %collective-permute-start.5) | collective-permute-done | bytes 229408 | tf_op jit(solution)/shard_map/two_low_up/ppermute | solution.py:339
  49.8 2.7 %collective-permute-start.7 = (bf16[3,128,896]{2,1,0:T(8,128)(2,1)S(1)}, bf16[3,128,896]{2,1,0:T(8,128)(2,1)S(1)}, u32[]{:S(2)}, u32[]{:S(2)}) collective-permute-start(bf16[3,128,896]{2,1,0:T(8,128)(2,1)S(1)} %make_step.21), channel_id=1, source_target_pairs={{0,3},{1,0},{2,1},{3,2},{4,7},{5,4},{6,5},{7,6},{8,11},{9,8},{10,9... | collective-permute-start | bytes 2064392 | tf_op jit(solution)/shard_map/three_down/ppermute | solution.py:339
  52.7 1.3 %collective-permute-start.12 = (bf16[1,128,896]{2,1,0:T(8,128)(2,1)S(1)}, bf16[1,128,896]{2,1,0:T(8,128)(2,1)S(1)}, u32[]{:S(2)}, u32[]{:S(2)}) collective-permute-start(bf16[1,128,896]{2,1,0:T(8,128)(2,1)S(1)} %get-tuple-element.60.refs_6_), channel_id=1, source_target_pairs={{0,1},{1,2},{2,3},{3,0},{4,5},{5,6},{6,7},{7,4},{8,9},{9,10},{10,1... | collective-permute-start | bytes 688136 | tf_op jit(solution)/shard_map/two_high_up/ppermute | solution.py:339
  54.0 2.8 %update_rows.7 = (f32[2,512,896]{2,1,0:T(8,128)}, f32[2,512,896]{2,1,0:T(8,128)}, bf16[2,128,896]{2,1,0:T(8,128)(2,1)S(1)}) custom-call(f32[128,128]{1,0:T(8,128)S(1)} %bitcast.11, f32[2,512,896]{2,1,0:T(8,128)} %refs_0_.9, bf16[2,512,896]{2,1,0:T(8,128)(2,1)} %refs_1_.9, f32[2,512,896]{2,1,0:T(8,128)} %refs_2_.9, ...), custom_call_target="tpu_custom_call", output_to_operand_aliasing={{0}: (4, {}), {1}: (5, {})} | custom-call | flops 4587520 | bytes 4587520 | tf_op jit(solution)/shard_map/update_rows/pallas_call | solution.py:180
  56.8 8.8 %collective-permute-done.8.refs_0_.refs_3_.refs_4_ = bf16[3,128,896]{2,1,0:T(8,128)(2,1)S(1)} collective-permute-done((bf16[3,128,896]{2,1,0:T(8,128)(2,1)S(1)}, bf16[3,128,896]{2,1,0:T(8,128)(2,1)S(1)}, u32[]{:S(2)}, u32[]{:S(2)}) %collective-permute-start.8) | collective-permute-done | bytes 688160 | tf_op jit(solution)/shard_map/three_up/ppermute | solution.py:339
  65.8 2.7 %collective-permute-start.10 = (bf16[3,128,896]{2,1,0:T(8,128)(2,1)S(1)}, bf16[3,128,896]{2,1,0:T(8,128)(2,1)S(1)}, u32[]{:S(2)}, u32[]{:S(2)}) collective-permute-start(bf16[3,128,896]{2,1,0:T(8,128)(2,1)S(1)} %make_step.23), channel_id=1, source_target_pairs={{0,3},{1,0},{2,1},{3,2},{4,7},{5,4},{6,5},{7,6},{8,11},{9,8},{10,9... | collective-permute-start | bytes 2064392 | tf_op jit(solution)/shard_map/four_down/ppermute | solution.py:339
  68.5 1.1 collective-permute-done.11.refs_1_
  69.6 0.9 collective-permute-done.12.refs_6_
  70.5 1.0 make_step.24
  71.5 6.2 %collective-permute-start.14 = (bf16[2,128,896]{2,1,0:T(8,128)(2,1)S(1)}, bf16[2,128,896]{2,1,0:T(8,128)(2,1)S(1)}, u32[]{:S(2)}, u32[]{:S(2)}) collective-permute-start(bf16[2,128,896]{2,1,0:T(8,128)(2,1)S(1)} %get-tuple-element.70), channel_id=1, source_target_pairs={{0,4},{4,0},{8,12},{12,8},{1,5},{5,1},{9,13},{13,9},{2,6},{6,2},{1... | collective-permute-start | bytes 1376264 | tf_op jit(solution)/shard_map/core_one/ppermute | solution.py:339
  77.8 1.3 %collective-permute-done.14.refs_4_.refs_1_ = bf16[2,128,896]{2,1,0:T(8,128)(2,1)S(1)} collective-permute-done((bf16[2,128,896]{2,1,0:T(8,128)(2,1)S(1)}, bf16[2,128,896]{2,1,0:T(8,128)(2,1)S(1)}, u32[]{:S(2)}, u32[]{:S(2)}) %collective-permute-start.14) | collective-permute-done | bytes 458784 | tf_op jit(solution)/shard_map/core_one/ppermute | solution.py:339
  79.1 6.1 %collective-permute-done.9.refs_0_.refs_2_.refs_4_ = bf16[3,128,896]{2,1,0:T(8,128)(2,1)S(1)} collective-permute-done((bf16[3,128,896]{2,1,0:T(8,128)(2,1)S(1)}, bf16[3,128,896]{2,1,0:T(8,128)(2,1)S(1)}, u32[]{:S(2)}, u32[]{:S(2)}) %collective-permute-start.9) | collective-permute-done | bytes 688160 | tf_op jit(solution)/shard_map/four_up/ppermute | solution.py:339
  85.5 2.9 %collective-permute-start.17 = (bf16[3,128,896]{2,1,0:T(8,128)(2,1)S(1)}, bf16[3,128,896]{2,1,0:T(8,128)(2,1)S(1)}, u32[]{:S(2)}, u32[]{:S(2)}) collective-permute-start(bf16[3,128,896]{2,1,0:T(8,128)(2,1)S(1)} %make_step.27), channel_id=1, source_target_pairs={{0,3},{1,0},{2,1},{3,2},{4,7},{5,4},{6,5},{7,6},{8,11},{9,8},{10,9... | collective-permute-start | bytes 2064392 | tf_op jit(solution)/shard_map/five_down/ppermute | solution.py:339
  88.4 0.9 make_step.26
  89.4 3.9 %collective-permute-start.18 = (bf16[2,128,896]{2,1,0:T(8,128)(2,1)S(1)}, bf16[2,128,896]{2,1,0:T(8,128)(2,1)S(1)}, u32[]{:S(2)}, u32[]{:S(2)}) collective-permute-start(bf16[2,128,896]{2,1,0:T(8,128)(2,1)S(1)} %make_step.28), channel_id=1, source_target_pairs={{0,4},{4,0},{8,12},{12,8},{1,5},{5,1},{9,13},{13,9},{2,6},{6,2},{1... | collective-permute-start | bytes 1376264 | tf_op jit(solution)/shard_map/core_pass_one/ppermute | solution.py:339
  93.2 6.3 %collective-permute-done.19.refs_2_.refs_1_.refs_5_ = bf16[4,128,896]{2,1,0:T(8,128)(2,1)S(1)} collective-permute-done((bf16[4,128,896]{2,1,0:T(8,128)(2,1)S(1)}, bf16[4,128,896]{2,1,0:T(8,128)(2,1)S(1)}, u32[]{:S(2)}, u32[]{:S(2)}) %collective-permute-start.19) | collective-permute-done | bytes 917536 | tf_op jit(solution)/shard_map/chip_two/ppermute | solution.py:339
  99.6 4.9 %collective-permute-done.20.refs_3_.refs_2_ = bf16[1,128,896]{2,1,0:T(8,128)(2,1)S(1)} collective-permute-done((bf16[1,128,896]{2,1,0:T(8,128)(2,1)S(1)}, bf16[1,128,896]{2,1,0:T(8,128)(2,1)S(1)}, u32[]{:S(2)}, u32[]{:S(2)}) %collective-permute-start.20) | collective-permute-done | bytes 229408 | tf_op jit(solution)/shard_map/chip_three/ppermute | solution.py:339
  104.7 1.0 collective-permute-start.28
  105.7 3.1 %collective-permute-start.22 = (bf16[1,128,896]{2,1,0:T(8,128)(2,1)S(1)}, bf16[1,128,896]{2,1,0:T(8,128)(2,1)S(1)}, u32[]{:S(2)}, u32[]{:S(2)}) collective-permute-start(bf16[1,128,896]{2,1,0:T(8,128)(2,1)S(1)} %get-tuple-element.77), channel_id=1, source_target_pairs={{0,3},{1,0},{2,1},{3,2},{4,7},{5,4},{6,5},{7,6},{8,11},{9,8},{10,9... | collective-permute-start | bytes 688136 | tf_op jit(solution)/shard_map/last_down/ppermute | solution.py:339
  108.8 1.9 %collective-permute-start.15 = (bf16[2,128,896]{2,1,0:T(8,128)(2,1)S(1)}, bf16[2,128,896]{2,1,0:T(8,128)(2,1)S(1)}, u32[]{:S(2)}, u32[]{:S(2)}) collective-permute-start(bf16[2,128,896]{2,1,0:T(8,128)(2,1)S(1)} %get-tuple-element.71), channel_id=1, source_target_pairs={{0,12},{4,8},{8,4},{12,0},{1,13},{5,9},{9,5},{13,1},{2,14},{6,10},... | collective-permute-start | bytes 1376264 | tf_op jit(solution)/shard_map/both_three/ppermute | solution.py:339
  110.7 2.4 %quantize_rows.4 = (bf16[1,1,2,2048,896]{4,3,2,1,0:T(8,128)(2,1)}, f32[1,1,2,16,7]{4,3,2,1,0:T(8,128)S(1)}) custom-call(bf16[2,128,896]{2,1,0:T(8,128)(2,1)S(1)} %get-tuple-element.61.refs_5_.refs_3_.refs_0_, bf16[2,128,896]{2,1,0:T(8,128)(2,1)S(1)} %collective-permute-done.14.refs_4_.refs_1_, ...), custom_call_target="tpu_custom_call" | custom-call | flops 6881280 | bytes 5505024 | tf_op jit(solution)/shard_map/quantize_rows/pallas_call | solution.py:305
  113.1 1.4 %collective-permute-done.21.refs_6_ = bf16[1,128,896]{2,1,0:T(8,128)(2,1)S(1)} collective-permute-done((bf16[1,128,896]{2,1,0:T(8,128)(2,1)S(1)}, bf16[1,128,896]{2,1,0:T(8,128)(2,1)S(1)}, u32[]{:S(2)}, u32[]{:S(2)}) %collective-permute-start.21) | collective-permute-done | bytes 229408 | tf_op jit(solution)/shard_map/last_up/ppermute | solution.py:339
  114.5 0.9 make_step.31
  115.5 1.0 collective-permute-start.24
  116.5 0.4 collective-permute-start.26
  117.0 2.7 %quantize_rows.5 = (bf16[1,1,2,2048,896]{4,3,2,1,0:T(8,128)(2,1)}, f32[1,1,2,16,7]{4,3,2,1,0:T(8,128)S(1)}) custom-call(bf16[2,128,896]{2,1,0:T(8,128)(2,1)S(1)} %get-tuple-element.72.refs_1_.refs_0_, bf16[6,128,896]{2,1,0:T(8,128)(2,1)S(1)} %collective-permute-done.28.refs_1_, ...), custom_call_target="tpu_custom_call", output_to_operand_aliasing={{0}: (6, {})} | custom-call | flops 8028160 | bytes 6422528 | tf_op jit(solution)/shard_map/quantize_rows/pallas_call | solution.py:305
  119.7 1.2 quantize_rows.6
  121.0 1.8 %collective-permute-done.15.refs_0_ = bf16[2,128,896]{2,1,0:T(8,128)(2,1)S(1)} collective-permute-done((bf16[2,128,896]{2,1,0:T(8,128)(2,1)S(1)}, bf16[2,128,896]{2,1,0:T(8,128)(2,1)S(1)}, u32[]{:S(2)}, u32[]{:S(2)}) %collective-permute-start.15) | collective-permute-done | bytes 458784 | tf_op jit(solution)/shard_map/both_three/ppermute | solution.py:339
  122.8 1.0 quantize_rows.7
  123.8 0.7 copy.27
  (54 shorter events, 2.5 us)
Async XLA Ops:
  0.6 1.5 %copy-start = (bf16[2,512,896]{2,1,0:T(8,128)(2,1)S(1)}, bf16[2,512,896]{2,1,0:T(8,128)(2,1)}, u32[]{:S(2)}) copy-start(bf16[2,512,896]{2,1,0:T(8,128)(2,1)} %refs_1_.9) | copy-start | bytes 5505028
  3.0 21.1 %all-to-all-start = ((f32[128,1,128]{2,1,0:T(1,128)}), f32[128,1,128]{2,1,0:T(1,128)S(1)}, u32[]{:S(2)}, u32[]{:S(2)}) async-start(f32[128,1,128]{2,1,0:T(1,128)} %bitcast.1), calls=%async_computation | async-start | bytes 131072 | tf_op jit(solution)/shard_map/all_to_all | solution.py:335
  24.9 12.8 %collective-permute-start = (bf16[2,128,896]{2,1,0:T(8,128)(2,1)S(1)}, bf16[2,128,896]{2,1,0:T(8,128)(2,1)S(1)}, u32[]{:S(2)}, u32[]{:S(2)}) collective-permute-start(bf16[2,128,896]{2,1,0:T(8,128)(2,1)S(1)} %first_weights.1.refs_3_.refs_0_), channel_id=1, source_target_pairs={{0,1},{1,2},{2,3},{3,0},{4,5},{5,6},{6,7},{7,4},{8,9},{9,10},{10,1... | collective-permute-start | bytes 1376264 | tf_op jit(solution)/shard_map/one_up/ppermute | solution.py:339
  25.5 12.3 %collective-permute-start.1 = (bf16[2,128,896]{2,1,0:T(8,128)(2,1)S(1)}, bf16[2,128,896]{2,1,0:T(8,128)(2,1)S(1)}, u32[]{:S(2)}, u32[]{:S(2)}) collective-permute-start(bf16[2,128,896]{2,1,0:T(8,128)(2,1)S(1)} %first_weights.1.refs_3_.refs_0_), channel_id=1, source_target_pairs={{0,3},{1,0},{2,1},{3,2},{4,7},{5,4},{6,5},{7,6},{8,11},{9,8},{10,9... | collective-permute-start | bytes 1376264 | tf_op jit(solution)/shard_map/one_down/ppermute | solution.py:339
  30.4 16.7 %collective-permute-start.6 = (bf16[2,128,896]{2,1,0:T(8,128)(2,1)S(1)}, bf16[2,128,896]{2,1,0:T(8,128)(2,1)S(1)}, u32[]{:S(2)}, u32[]{:S(2)}) collective-permute-start(bf16[2,128,896]{2,1,0:T(8,128)(2,1)S(1)} %get-tuple-element.56.refs_1_.refs_0_), channel_id=1, source_target_pairs={{0,8},{4,12},{8,0},{12,4},{1,9},{5,13},{9,1},{13,5},{2,10},{6,14},... | collective-permute-start | bytes 1376264 | tf_op jit(solution)/shard_map/cross/ppermute | solution.py:339
  37.7 8.4 %collective-permute-start.2 = (bf16[1,128,896]{2,1,0:T(8,128)(2,1)S(1)}, bf16[1,128,896]{2,1,0:T(8,128)(2,1)S(1)}, u32[]{:S(2)}, u32[]{:S(2)}) collective-permute-start(bf16[1,128,896]{2,1,0:T(8,128)(2,1)S(1)} %make_step.16.refs_5_.refs_1_), channel_id=1, source_target_pairs={{0,1},{1,2},{2,3},{3,0},{4,5},{5,6},{6,7},{7,4},{8,9},{9,10},{10,1... | collective-permute-start | bytes 688136 | tf_op jit(solution)/shard_map/on_up/ppermute | solution.py:339
  37.9 8.3 %collective-permute-start.3 = (bf16[1,128,896]{2,1,0:T(8,128)(2,1)S(1)}, bf16[1,128,896]{2,1,0:T(8,128)(2,1)S(1)}, u32[]{:S(2)}, u32[]{:S(2)}) collective-permute-start(bf16[1,128,896]{2,1,0:T(8,128)(2,1)S(1)} %make_step.17.refs_1_), channel_id=1, source_target_pairs={{0,3},{1,0},{2,1},{3,2},{4,7},{5,4},{6,5},{7,6},{8,11},{9,8},{10,9... | collective-permute-start | bytes 688136 | tf_op jit(solution)/shard_map/on_down/ppermute | solution.py:339
  40.6 9.0 %collective-permute-start.5 = (bf16[1,128,896]{2,1,0:T(8,128)(2,1)S(1)}, bf16[1,128,896]{2,1,0:T(8,128)(2,1)S(1)}, u32[]{:S(2)}, u32[]{:S(2)}) collective-permute-start(bf16[1,128,896]{2,1,0:T(8,128)(2,1)S(1)} %get-tuple-element.65), channel_id=1, source_target_pairs={{0,1},{1,2},{2,3},{3,0},{4,5},{5,6},{6,7},{7,4},{8,9},{9,10},{10,1... | collective-permute-start | bytes 688136 | tf_op jit(solution)/shard_map/two_low_up/ppermute | solution.py:339
  40.7 9.1 %collective-permute-start.4 = (bf16[1,128,896]{2,1,0:T(8,128)(2,1)S(1)}, bf16[1,128,896]{2,1,0:T(8,128)(2,1)S(1)}, u32[]{:S(2)}, u32[]{:S(2)}) collective-permute-start(bf16[1,128,896]{2,1,0:T(8,128)(2,1)S(1)} %get-tuple-element.60.refs_6_), channel_id=1, source_target_pairs={{0,3},{1,0},{2,1},{3,2},{4,7},{5,4},{6,5},{7,6},{8,11},{9,8},{10,9... | collective-permute-start | bytes 688136 | tf_op jit(solution)/shard_map/two_high_down/ppermute | solution.py:339
  49.7 15.9 %collective-permute-start.8 = (bf16[3,128,896]{2,1,0:T(8,128)(2,1)S(1)}, bf16[3,128,896]{2,1,0:T(8,128)(2,1)S(1)}, u32[]{:S(2)}, u32[]{:S(2)}) collective-permute-start(bf16[3,128,896]{2,1,0:T(8,128)(2,1)S(1)} %make_step.20.refs_2_), channel_id=1, source_target_pairs={{0,1},{1,2},{2,3},{3,0},{4,5},{5,6},{6,7},{7,4},{8,9},{9,10},{10,1... | collective-permute-start | bytes 2064392 | tf_op jit(solution)/shard_map/three_up/ppermute | solution.py:339
  49.8 15.9 %collective-permute-start.7 = (bf16[3,128,896]{2,1,0:T(8,128)(2,1)S(1)}, bf16[3,128,896]{2,1,0:T(8,128)(2,1)S(1)}, u32[]{:S(2)}, u32[]{:S(2)}) collective-permute-start(bf16[3,128,896]{2,1,0:T(8,128)(2,1)S(1)} %make_step.21), channel_id=1, source_target_pairs={{0,3},{1,0},{2,1},{3,2},{4,7},{5,4},{6,5},{7,6},{8,11},{9,8},{10,9... | collective-permute-start | bytes 2064392 | tf_op jit(solution)/shard_map/three_down/ppermute | solution.py:339
  52.6 25.2 %collective-permute-start.13 = (bf16[4,128,896]{2,1,0:T(8,128)(2,1)S(1)}, bf16[4,128,896]{2,1,0:T(8,128)(2,1)S(1)}, u32[]{:S(2)}, u32[]{:S(2)}) collective-permute-start(bf16[4,128,896]{2,1,0:T(8,128)(2,1)S(1)} %get-tuple-element.69), channel_id=1, source_target_pairs={{0,8},{4,12},{8,0},{12,4},{1,9},{5,13},{9,1},{13,5},{2,10},{6,14},... | collective-permute-start | bytes 2752520 | tf_op jit(solution)/shard_map/chip_one/ppermute | solution.py:339
  52.6 17.0 %collective-permute-start.11 = (bf16[1,128,896]{2,1,0:T(8,128)(2,1)S(1)}, bf16[1,128,896]{2,1,0:T(8,128)(2,1)S(1)}, u32[]{:S(2)}, u32[]{:S(2)}) collective-permute-start(bf16[1,128,896]{2,1,0:T(8,128)(2,1)S(1)} %get-tuple-element.65), channel_id=1, source_target_pairs={{0,3},{1,0},{2,1},{3,2},{4,7},{5,4},{6,5},{7,6},{8,11},{9,8},{10,9... | collective-permute-start | bytes 688136 | tf_op jit(solution)/shard_map/two_low_down/ppermute | solution.py:339
  52.7 17.8 %collective-permute-start.12 = (bf16[1,128,896]{2,1,0:T(8,128)(2,1)S(1)}, bf16[1,128,896]{2,1,0:T(8,128)(2,1)S(1)}, u32[]{:S(2)}, u32[]{:S(2)}) collective-permute-start(bf16[1,128,896]{2,1,0:T(8,128)(2,1)S(1)} %get-tuple-element.60.refs_6_), channel_id=1, source_target_pairs={{0,1},{1,2},{2,3},{3,0},{4,5},{5,6},{6,7},{7,4},{8,9},{9,10},{10,1... | collective-permute-start | bytes 688136 | tf_op jit(solution)/shard_map/two_high_up/ppermute | solution.py:339
  65.6 19.6 %collective-permute-start.9 = (bf16[3,128,896]{2,1,0:T(8,128)(2,1)S(1)}, bf16[3,128,896]{2,1,0:T(8,128)(2,1)S(1)}, u32[]{:S(2)}, u32[]{:S(2)}) collective-permute-start(bf16[3,128,896]{2,1,0:T(8,128)(2,1)S(1)} %make_step.22.refs_2_.refs_9_), channel_id=1, source_target_pairs={{0,1},{1,2},{2,3},{3,0},{4,5},{5,6},{6,7},{7,4},{8,9},{9,10},{10,1... | collective-permute-start | bytes 2064392 | tf_op jit(solution)/shard_map/four_up/ppermute | solution.py:339
  65.8 19.6 %collective-permute-start.10 = (bf16[3,128,896]{2,1,0:T(8,128)(2,1)S(1)}, bf16[3,128,896]{2,1,0:T(8,128)(2,1)S(1)}, u32[]{:S(2)}, u32[]{:S(2)}) collective-permute-start(bf16[3,128,896]{2,1,0:T(8,128)(2,1)S(1)} %make_step.23), channel_id=1, source_target_pairs={{0,3},{1,0},{2,1},{3,2},{4,7},{5,4},{6,5},{7,6},{8,11},{9,8},{10,9... | collective-permute-start | bytes 2064392 | tf_op jit(solution)/shard_map/four_down/ppermute | solution.py:339
  71.5 7.6 %collective-permute-start.14 = (bf16[2,128,896]{2,1,0:T(8,128)(2,1)S(1)}, bf16[2,128,896]{2,1,0:T(8,128)(2,1)S(1)}, u32[]{:S(2)}, u32[]{:S(2)}) collective-permute-start(bf16[2,128,896]{2,1,0:T(8,128)(2,1)S(1)} %get-tuple-element.70), channel_id=1, source_target_pairs={{0,4},{4,0},{8,12},{12,8},{1,5},{5,1},{9,13},{13,9},{2,6},{6,2},{1... | collective-permute-start | bytes 1376264 | tf_op jit(solution)/shard_map/core_one/ppermute | solution.py:339
  77.7 21.9 %collective-permute-start.19 = (bf16[4,128,896]{2,1,0:T(8,128)(2,1)S(1)}, bf16[4,128,896]{2,1,0:T(8,128)(2,1)S(1)}, u32[]{:S(2)}, u32[]{:S(2)}) collective-permute-start(bf16[4,128,896]{2,1,0:T(8,128)(2,1)S(1)} %get-tuple-element.73), channel_id=1, source_target_pairs={{0,8},{4,12},{8,0},{12,4},{1,9},{5,13},{9,1},{13,5},{2,10},{6,14},... | collective-permute-start | bytes 2752520 | tf_op jit(solution)/shard_map/chip_two/ppermute | solution.py:339
  85.3 19.2 %collective-permute-start.16 = (bf16[3,128,896]{2,1,0:T(8,128)(2,1)S(1)}, bf16[3,128,896]{2,1,0:T(8,128)(2,1)S(1)}, u32[]{:S(2)}, u32[]{:S(2)}) collective-permute-start(bf16[3,128,896]{2,1,0:T(8,128)(2,1)S(1)} %make_step.25.refs_6_.refs_2_), channel_id=1, source_target_pairs={{0,1},{1,2},{2,3},{3,0},{4,5},{5,6},{6,7},{7,4},{8,9},{9,10},{10,1... | collective-permute-start | bytes 2064392 | tf_op jit(solution)/shard_map/five_up/ppermute | solution.py:339
  85.5 19.1 %collective-permute-start.17 = (bf16[3,128,896]{2,1,0:T(8,128)(2,1)S(1)}, bf16[3,128,896]{2,1,0:T(8,128)(2,1)S(1)}, u32[]{:S(2)}, u32[]{:S(2)}) collective-permute-start(bf16[3,128,896]{2,1,0:T(8,128)(2,1)S(1)} %make_step.27), channel_id=1, source_target_pairs={{0,3},{1,0},{2,1},{3,2},{4,7},{5,4},{6,5},{7,6},{8,11},{9,8},{10,9... | collective-permute-start | bytes 2064392 | tf_op jit(solution)/shard_map/five_down/ppermute | solution.py:339
  89.4 15.1 %collective-permute-start.18 = (bf16[2,128,896]{2,1,0:T(8,128)(2,1)S(1)}, bf16[2,128,896]{2,1,0:T(8,128)(2,1)S(1)}, u32[]{:S(2)}, u32[]{:S(2)}) collective-permute-start(bf16[2,128,896]{2,1,0:T(8,128)(2,1)S(1)} %make_step.28), channel_id=1, source_target_pairs={{0,4},{4,0},{8,12},{12,8},{1,5},{5,1},{9,13},{13,9},{2,6},{6,2},{1... | collective-permute-start | bytes 1376264 | tf_op jit(solution)/shard_map/core_pass_one/ppermute | solution.py:339
  93.2 11.3 %collective-permute-start.20 = (bf16[1,128,896]{2,1,0:T(8,128)(2,1)S(1)}, bf16[1,128,896]{2,1,0:T(8,128)(2,1)S(1)}, u32[]{:S(2)}, u32[]{:S(2)}) collective-permute-start(bf16[1,128,896]{2,1,0:T(8,128)(2,1)S(1)} %get-tuple-element.74), channel_id=1, source_target_pairs={{0,8},{4,12},{8,0},{12,4},{1,9},{5,13},{9,1},{13,5},{2,10},{6,14},... | collective-permute-start | bytes 688136 | tf_op jit(solution)/shard_map/chip_three/ppermute | solution.py:339
  104.7 12.3 %collective-permute-start.28 = (bf16[6,128,896]{2,1,0:T(8,128)(2,1)S(1)}, bf16[6,128,896]{2,1,0:T(8,128)(2,1)S(1)}, u32[]{:S(2)}, u32[]{:S(2)}) collective-permute-start(bf16[6,128,896]{2,1,0:T(8,128)(2,1)S(1)} %get-tuple-element.84), channel_id=1, source_target_pairs={{0,4},{4,0},{8,12},{12,8},{1,5},{5,1},{9,13},{13,9},{2,6},{6,2},{1... | collective-permute-start | bytes 4128776 | tf_op jit(solution)/shard_map/core_join/ppermute | solution.py:339
  105.6 7.5 %collective-permute-start.23 = (bf16[1,128,896]{2,1,0:T(8,128)(2,1)S(1)}, bf16[1,128,896]{2,1,0:T(8,128)(2,1)S(1)}, u32[]{:S(2)}, u32[]{:S(2)}) collective-permute-start(bf16[1,128,896]{2,1,0:T(8,128)(2,1)S(1)} %get-tuple-element.79), channel_id=1, source_target_pairs={{0,8},{4,12},{8,0},{12,4},{1,9},{5,13},{9,1},{13,5},{2,10},{6,14},... | collective-permute-start | bytes 688136 | tf_op jit(solution)/shard_map/chip_three_more/ppermute | solution.py:339
  105.7 8.8 %collective-permute-start.21 = (bf16[1,128,896]{2,1,0:T(8,128)(2,1)S(1)}, bf16[1,128,896]{2,1,0:T(8,128)(2,1)S(1)}, u32[]{:S(2)}, u32[]{:S(2)}) collective-permute-start(bf16[1,128,896]{2,1,0:T(8,128)(2,1)S(1)} %make_step.29.refs_4_), channel_id=1, source_target_pairs={{0,1},{1,2},{2,3},{3,0},{4,5},{5,6},{6,7},{7,4},{8,9},{9,10},{10,1... | collective-permute-start | bytes 688136 | tf_op jit(solution)/shard_map/last_up/ppermute | solution.py:339
  105.7 8.8 %collective-permute-start.22 = (bf16[1,128,896]{2,1,0:T(8,128)(2,1)S(1)}, bf16[1,128,896]{2,1,0:T(8,128)(2,1)S(1)}, u32[]{:S(2)}, u32[]{:S(2)}) collective-permute-start(bf16[1,128,896]{2,1,0:T(8,128)(2,1)S(1)} %get-tuple-element.77), channel_id=1, source_target_pairs={{0,3},{1,0},{2,1},{3,2},{4,7},{5,4},{6,5},{7,6},{8,11},{9,8},{10,9... | collective-permute-start | bytes 688136 | tf_op jit(solution)/shard_map/last_down/ppermute | solution.py:339
  108.8 14.0 %collective-permute-start.15 = (bf16[2,128,896]{2,1,0:T(8,128)(2,1)S(1)}, bf16[2,128,896]{2,1,0:T(8,128)(2,1)S(1)}, u32[]{:S(2)}, u32[]{:S(2)}) collective-permute-start(bf16[2,128,896]{2,1,0:T(8,128)(2,1)S(1)} %get-tuple-element.71), channel_id=1, source_target_pairs={{0,12},{4,8},{8,4},{12,0},{1,13},{5,9},{9,5},{13,1},{2,14},{6,10},... | collective-permute-start | bytes 1376264 | tf_op jit(solution)/shard_map/both_three/ppermute | solution.py:339
  115.5 4.2 %collective-permute-start.24 = (bf16[1,128,896]{2,1,0:T(8,128)(2,1)S(1)}, bf16[1,128,896]{2,1,0:T(8,128)(2,1)S(1)}, u32[]{:S(2)}, u32[]{:S(2)}) collective-permute-start(bf16[1,128,896]{2,1,0:T(8,128)(2,1)S(1)} %get-tuple-element.80), channel_id=1, source_target_pairs={{0,4},{4,0},{8,12},{12,8},{1,5},{5,1},{9,13},{13,9},{2,6},{6,2},{1... | collective-permute-start | bytes 688136 | tf_op jit(solution)/shard_map/core_last/ppermute | solution.py:339
  116.4 3.3 %collective-permute-start.25 = (bf16[1,128,896]{2,1,0:T(8,128)(2,1)S(1)}, bf16[1,128,896]{2,1,0:T(8,128)(2,1)S(1)}, u32[]{:S(2)}, u32[]{:S(2)}) collective-permute-start(bf16[1,128,896]{2,1,0:T(8,128)(2,1)S(1)} %get-tuple-element.81), channel_id=1, source_target_pairs={{0,4},{4,0},{8,12},{12,8},{1,5},{5,1},{9,13},{13,9},{2,6},{6,2},{1... | collective-permute-start | bytes 688136 | tf_op jit(solution)/shard_map/core_last/ppermute | solution.py:339
  116.5 3.2 %collective-permute-start.26 = (bf16[1,128,896]{2,1,0:T(8,128)(2,1)S(1)}, bf16[1,128,896]{2,1,0:T(8,128)(2,1)S(1)}, u32[]{:S(2)}, u32[]{:S(2)}) collective-permute-start(bf16[1,128,896]{2,1,0:T(8,128)(2,1)S(1)} %get-tuple-element.82), channel_id=1, source_target_pairs={{0,4},{4,0},{8,12},{12,8},{1,5},{5,1},{9,13},{13,9},{2,6},{6,2},{1... | collective-permute-start | bytes 688136 | tf_op jit(solution)/shard_map/core_last/ppermute | solution.py:339
  116.9 2.8 %collective-permute-start.27 = (bf16[1,128,896]{2,1,0:T(8,128)(2,1)S(1)}, bf16[1,128,896]{2,1,0:T(8,128)(2,1)S(1)}, u32[]{:S(2)}, u32[]{:S(2)}) collective-permute-start(bf16[1,128,896]{2,1,0:T(8,128)(2,1)S(1)} %get-tuple-element.83), channel_id=1, source_target_pairs={{0,4},{4,0},{8,12},{12,8},{1,5},{5,1},{9,13},{13,9},{2,6},{6,2},{1... | collective-permute-start | bytes 688136 | tf_op jit(solution)/shard_map/core_last/ppermute | solution.py:339
